TPU v7x, 256 devices: a whole 4x4x8 slice. The times are simulated.
256 devices in a mesh: dp: 64 (over z, x_lo, y), mp: 4 (over x_hi, core).
Axes of the slice: x: 4 (x_hi: 2, x_lo: 2; x = x_hi * 2 + x_lo), y: 4, z: 8, core: 2. Of those that a mesh axis runs over, the one named last changes fastest.
Arguments:
- image_features: bfloat16 [10240, 1152], P('dp'), may hold values from -36 to 36
- text_features: bfloat16 [10240, 1152], P('dp'), may hold values from -36 to 36
- image_proj: bfloat16 [1152, 1152], P(None, 'mp'), may hold values from -0.75 to 0.75
- text_proj: bfloat16 [1152, 1152], P(None, 'mp'), may hold values from -0.75 to 0.75
- log_scale: float32 [1], replicated, may hold values from 4.3 to 4.7
- bias: float32 [1], replicated, may hold values from -11 to -9
Outputs:
- grad_image_features: float32 [10240, 1152], P('dp', 'mp')
- grad_text_features: float32 [10240, 1152], P('dp', 'mp')
- grad_image_proj: float32 [1152, 1152], P('dp', 'mp')
- grad_text_proj: float32 [1152, 1152], P('dp', 'mp')
All inputs are finite; a program needn't handle non-finite values.
Results may differ from a plain program's by a relative error of at most 0.0075.
Values may be sent and summed in bfloat16 or wider, within the bound.
No kernel may reach another device: no remote copies, remote signals or barrier semaphores. Data moves between devices by JAX's collectives and lax.ppermute only.
A program may use at most 128 MiB of HBM per device.

v0:
```python
import jax
import jax.numpy as jnp
from jax import lax
from jax.experimental import pallas as pl
from jax.experimental.pallas import tpu as pltpu
from jax.sharding import Mesh, PartitionSpec as P

AXES = ("z", "xl", "y", "xh", "c")
SIZES = (8, 2, 4, 2, 2)
DP = ("z", "xl", "y")
MP = ("xh", "c")
PLANE = ("xl", "y", "xh")
BF = jnp.bfloat16
F32 = jnp.float32


def a2a(x, axes):
    return lax.all_to_all(x, axes, 0, 0, tiled=True)


def swap_core(x):
    return lax.ppermute(x, "c", [(0, 1), (1, 0)])


def shift(x, axis, size, step):
    return lax.ppermute(x, axis, [(i, (i + step) % size) for i in range(size)])


def ring_sum(to):
    rows = to[0].shape[0]
    far_up = shift(jnp.concatenate([to[4], to[3]]).astype(BF), "z", 8, 2).astype(F32)
    far_down = shift(jnp.concatenate([to[-3], to[-2]]).astype(BF), "z", 8, -2).astype(F32)
    near = [
        shift((to[2] + far_up[:rows]).astype(BF), "z", 8, 2),
        shift((to[1] + far_up[rows:]).astype(BF), "z", 8, 1),
        shift((to[-1] + far_down[:rows]).astype(BF), "z", 8, -1),
    ]
    return to[0] + far_down[rows:] + near[0].astype(F32) + near[1].astype(F32) + near[2].astype(F32)


def mp_shift(x, dx, dc):
    pairs = [(a * 2 + b, (a ^ dx) * 2 + (b ^ dc)) for a in range(2) for b in range(2)]
    return lax.ppermute(x, MP, pairs)


def rows_from_slices(pair, xh, c):
    quarters = pair.reshape(2, 2, 2, 40, 288)
    got = {}
    for dx in range(2):
        for dc in range(2):
            to = lax.dynamic_index_in_dim(quarters, xh ^ dx, 1, keepdims=False)
            to = lax.dynamic_index_in_dim(to, c ^ dc, 1, keepdims=False)
            got[dx, dc] = mp_shift(to, dx, dc) if dx or dc else to
    parts = []
    for a in range(2):
        for b in range(2):
            near = jnp.where(c == b, got[0, 0], got[0, 1])
            far = jnp.where(c == b, got[1, 0], got[1, 1])
            parts.append(jnp.where(xh == a, near, far))
    return jnp.concatenate(parts, axis=2)


def block_kernel(scalars, place, img_in, *refs):
    pieces = refs[:16]
    to_oth, to_own, to_img, img, parts, texts, coef, coef_t, t_oth, t_own, g_img, sems, out_sems = refs[16:]
    copies = [pltpu.make_async_copy(pieces[d], parts.at[d], sems.at[d]) for d in range(16)]
    copies.append(pltpu.make_async_copy(img_in, img, sems.at[16]))
    for copy in copies:
        copy.start()
    for d in range(8):
        copies[2 * d].wait()
        copies[2 * d + 1].wait()
        texts[80 * d : 80 * d + 80, :] = jnp.concatenate([parts[2 * d], parts[2 * d + 1]])
    copies[16].wait()
    scale, offset = scalars[0], scalars[1]
    dots = lax.dot_general(img[...], texts[...], (((1,), (1,)), ((), ())), preferred_element_type=F32)
    rows = lax.broadcasted_iota(jnp.int32, (640, 640), 0) - place[0] * 40
    cols = lax.broadcasted_iota(jnp.int32, (640, 640), 1) - 320
    sign = jnp.where((rows == cols) & (cols >= 0) & (cols < 40), F32(1.0), F32(-1.0))
    value = (-sign * scale * jax.nn.sigmoid(-sign * (scale * dots + offset))).astype(BF)
    coef[...] = value
    coef_t[...] = value.T
    sends = [
        pltpu.make_async_copy(t_oth, to_oth, out_sems.at[0]),
        pltpu.make_async_copy(t_own, to_own, out_sems.at[1]),
        pltpu.make_async_copy(g_img.at[pl.ds(0, 320)], to_img.at[pl.ds(0, 320)], out_sems.at[2]),
        pltpu.make_async_copy(g_img.at[pl.ds(320, 320)], to_img.at[pl.ds(320, 320)], out_sems.at[3]),
    ]
    t_oth[...] = jnp.dot(coef_t[:320, :], img[...], preferred_element_type=F32).astype(BF)
    sends[0].start()
    t_own[...] = jnp.dot(coef_t[320:, :], img[...], preferred_element_type=F32).astype(BF)
    sends[1].start()
    for half in range(2):
        at = 320 * half
        g_img[at : at + 320, :] = jnp.dot(
            coef[at : at + 320, :], texts[...], preferred_element_type=F32
        ).astype(BF)
        sends[2 + half].start()
    for send in sends:
        send.wait()


def block_grads(scalars, place, img, pieces):
    small = pl.BlockSpec(memory_space=pltpu.SMEM)
    large = pl.BlockSpec(memory_space=pltpu.HBM)
    return pl.pallas_call(
        block_kernel,
        out_shape=[
            jax.ShapeDtypeStruct((320, 1152), BF),
            jax.ShapeDtypeStruct((320, 1152), BF),
            jax.ShapeDtypeStruct((640, 1152), BF),
        ],
        in_specs=[small, small] + [large] * 17,
        out_specs=[large] * 3,
        scratch_shapes=[
            pltpu.VMEM((640, 1152), BF),
            pltpu.VMEM((16, 40, 1152), BF),
            pltpu.VMEM((640, 1152), BF),
            pltpu.VMEM((640, 640), BF),
            pltpu.VMEM((640, 640), BF),
            pltpu.VMEM((320, 1152), BF),
            pltpu.VMEM((320, 1152), BF),
            pltpu.VMEM((640, 1152), BF),
            pltpu.SemaphoreType.DMA((17,)),
            pltpu.SemaphoreType.DMA((4,)),
        ],
        compiler_params=pltpu.CompilerParams(vmem_limit_bytes=60 * 2**20),
        cost_estimate=pl.CostEstimate(flops=2900000000, bytes_accessed=8000000, transcendentals=400000),
    )(scalars, place, img, *pieces)


def shards(image_features, text_features, image_proj, text_proj, log_scale, bias):
    xl, y, xh, c = (lax.axis_index(a) for a in AXES[1:])
    p_img = jnp.dot(image_features, image_proj, preferred_element_type=F32)
    p_txt = jnp.dot(text_features, text_proj, preferred_element_type=F32)
    stacked = jnp.concatenate(lax.optimization_barrier((image_features, text_features, p_img, p_txt))[:2])
    col = jnp.arange(576, dtype=jnp.int32)
    source = (col % 144) // 18 * 144 + col // 144 * 18 + col % 18

    def pick(half, rows):
        chosen = jnp.arange(1152, dtype=jnp.int32)[:, None] == (source + 72 * half)[None, :]
        return jnp.dot(rows, chosen.astype(BF), preferred_element_type=F32).astype(BF)

    keep = pick(xl, stacked)
    give = pick(1 - xl, lax.dynamic_slice_in_dim(stacked, c * 160, 160, 0))
    own = rows_from_slices(jnp.stack([p_img, p_txt]), xh, c)
    r = lax.rsqrt(jnp.sum(own * own, axis=2, keepdims=True) + 1e-06)
    z = (own * r).astype(BF)
    z, keep, give = lax.optimization_barrier((z, keep, give))
    z_img, z_txt = z[0], z[1]
    r_img, r_txt = r[0], r[1]

    img = jnp.broadcast_to(z_img[None], (16, 40, 1152))
    img, z_near = lax.optimization_barrier((img, z_txt))
    img = a2a(img, PLANE).reshape(640, 1152)
    four = shift(z_near, "z", 8, 4)
    up, down = [z_near], [z_near]
    for d in range(3):
        up.append(shift(up[-1], "z", 8, 1))
        down.append(shift(down[-1], "z", 8, -1))
    txt_own = up + [four] + down[:0:-1]
    last_up, last_down, img = lax.optimization_barrier((up[3], down[3], img))
    txt_oth = [swap_core(piece) for piece in up[:3] + [last_up, four, last_down] + down[2:0:-1]]
    give, img = lax.optimization_barrier((give, img))
    come = lax.ppermute(give, "xl", [(0, 1), (1, 0)])
    place = (xl * 4 + y) * 2 + xh
    scalars = jnp.concatenate([jnp.exp(log_scale), bias])
    t_oth, t_own, g_img = block_grads(scalars, place.astype(jnp.int32).reshape(1), img, txt_oth + txt_own)
    t_oth, come = lax.optimization_barrier((t_oth, come))
    t_got = swap_core(t_oth)
    come_oth = swap_core(come)
    come = jnp.concatenate([jnp.where(c == 0, come, come_oth), jnp.where(c == 0, come_oth, come)])
    first, second = jnp.where(xl == 0, keep, come), jnp.where(xl == 0, come, keep)
    fi = jnp.concatenate([first[:160], second[:160]])
    ft = jnp.concatenate([first[160:], second[160:]])

    t_sum = t_own.astype(F32) + t_got.astype(F32)
    to = {k: t_sum[40 * (-k % 8) : 40 * (-k % 8) + 40] for k in range(-3, 5)}
    gz_txt = ring_sum(to)
    g_img = g_img.reshape(16, 40, 1152)
    gz_img = jnp.sum(a2a(g_img, PLANE).astype(F32), axis=0)

    gz = jnp.stack([gz_img, gz_txt])
    values = z.astype(F32)
    inner = jnp.sum(values * gz, axis=2, keepdims=True)
    gp_rows = (r * (gz - values * inner)).astype(BF)
    cut = gp_rows.reshape(2, 40, 4, 288).transpose(2, 0, 1, 3)
    rest = jnp.concatenate([cut[:, 0, :, 256:], cut[:, 1, :, 256:]], axis=2)
    rest = jnp.concatenate([rest, rest], axis=2)
    piece = jnp.concatenate(
        [cut[:, :, :, :128].reshape(4, 80, 128), cut[:, :, :, 128:256].reshape(4, 80, 128), rest], axis=1
    )
    got = a2a(jnp.broadcast_to(piece[None], (2, 4, 200, 128)).reshape(8, 200, 128), ("xl", "xh", "c"))
    a_img, a_txt, b_img, b_txt, rest = (got[:, 40 * i : 40 * i + 40].reshape(320, 128) for i in range(5))

    def rows_dot(x, g):
        return jnp.einsum("rd,re->de", x, g, preferred_element_type=F32)

    lane, rest = lax.optimization_barrier((lax.broadcasted_iota(jnp.int32, (576, 128), 1), rest))
    w = jnp.concatenate(
        [
            rows_dot(fi, jnp.concatenate([a_img, b_img], axis=1)),
            rows_dot(ft, jnp.concatenate([a_txt, b_txt], axis=1)),
            jnp.where(lane < 32, rows_dot(fi, rest), rows_dot(ft, rest)),
        ],
        axis=1,
    ).reshape(4, 144, 640)
    def block(k):
        return lax.dynamic_index_in_dim(w, (y + k) % 4, 0, keepdims=False)

    up, down = shift(block(2).astype(BF), "y", 4, 1), shift(block(3).astype(BF), "y", 4, -1)
    up = shift((up.astype(F32) + block(1)).astype(BF), "y", 4, 1)
    w = block(0) + down.astype(F32) + up.astype(F32)
    w = jnp.sum(a2a(w.astype(BF).reshape(8, 18, 640), ("z",)).astype(F32), axis=0)
    w_img = jnp.concatenate([w[:, :256], w[:, 512:544]], axis=1)
    w_txt = jnp.concatenate([w[:, 256:512], w[:, 544:576]], axis=1)

    mine = lax.dynamic_slice_in_dim(got, xl * 4, 4, 0)
    mine = [mine[:, 40 * i : 40 * i + 40].reshape(160, 128) for i in range(5)]
    gp_img = jnp.concatenate([mine[0], mine[2], mine[4][:, :32]], axis=1)
    gp_txt = jnp.concatenate([mine[1], mine[3], mine[4][:, 32:64]], axis=1)

    def feature_part(to):
        out = [
            jnp.einsum("re,de->rd", g, lax.dynamic_slice_in_dim(p, to * 288, 288, 0), preferred_element_type=F32)
            for g, p in ((gp_img, image_proj), (gp_txt, text_proj))
        ]
        return jnp.stack(out)

    f = feature_part(xh * 2 + c)
    for dx, dc in ((0, 1), (1, 0), (1, 1)):
        other = feature_part((xh ^ dx) * 2 + (c ^ dc)).astype(BF)
        f = f + mp_shift(other, dx, dc).astype(F32)
    return f[0], f[1], w_img, w_txt


def solution(mesh):
    fine = Mesh(mesh.devices.reshape(SIZES), AXES)
    in_specs = (P(DP, None), P(DP, None), P(None, MP), P(None, MP), P(), P())
    out_specs = (P(DP, MP), P(DP, MP), P(DP, MP), P(DP, MP))
    return jax.shard_map(shards, mesh=fine, in_specs=in_specs, out_specs=out_specs, check_vma=False)
```

profile of v0, /device:TPU:2, one launch (start us, length us, event | category | flops | bytes accessed | tf_op | source)
XLA Modules:
  0.0 137.6 jit_solution(8656626010722912920)
XLA Ops:
  1.7 1.5 %fusion.104 = f32[160,288]{1,0:T(8,128)S(1)} fusion(bf16[160,1152]{1,0:T(8,128)(2,1)} %param.6, bf16[1152,288]{0,1:T(8,128)(2,1)S(1)} %copy-done), kind=kOutput, calls=%fused_computation.186 | convolution fusion | flops 106168320 | bytes 1216512 | tf_op jit(solution)/shard_map/dot_general | solution.py:134
  4.4 2.1 %collective-permute-start.1 = (f32[2,40,288]{2,1,0:T(8,128)}, f32[2,40,288]{2,1,0:T(8,128)S(1)}, u32[]{:S(2)}, u32[]{:S(2)}) collective-permute-start(f32[2,40,288]{2,1,0:T(8,128)} %get-tuple-element.62), channel_id=1, source_target_pairs={{0,2},{1,3},{2,0},{3,1},{4,6},{5,7},{6,4},{7,5},{8,10},{9,11},{10,... | collective-permute-start | bytes 276488 | tf_op jit(solution)/shard_map/ppermute | solution.py:43
  8.7 1.4 %fusion.10 = bf16[160,576]{1,0:T(8,128)(2,1)} fusion(s32[576]{0:T(1024)S(1)} %get-tuple-element.91, bf16[320,1152]{1,0:T(8,128)(2,1)S(1)} %constant_dynamic-update-slice_fusion, s32[]{:T(128)S(6)} %select_n.236), kind=kOutput, calls=%fused_computation.15 | convolution fusion | flops 213092352 | bytes 557060 | tf_op jit(solution)/shard_map/dot_general | solution.py:142
  10.1 2.1 %collective-permute-done.1 = f32[2,40,288]{2,1,0:T(8,128)S(1)} collective-permute-done((f32[2,40,288]{2,1,0:T(8,128)}, f32[2,40,288]{2,1,0:T(8,128)S(1)}, u32[]{:S(2)}, u32[]{:S(2)}) %collective-permute-start.1) | collective-permute-done | bytes 92192 | tf_op jit(solution)/shard_map/ppermute | solution.py:43
  12.2 1.9 %collective-permute-done.2 = f32[2,40,288]{2,1,0:T(8,128)S(1)} collective-permute-done((f32[2,40,288]{2,1,0:T(8,128)S(1)}, f32[2,40,288]{2,1,0:T(8,128)S(1)}, u32[]{:S(2)}, u32[]{:S(2)}) %collective-permute-start.2) | collective-permute-done | bytes 92192 | tf_op jit(solution)/shard_map/ppermute | solution.py:43
  15.9 7.6 %all-to-all-start = ((bf16[16,40,1152]{2,1,0:T(8,128)(2,1)}), bf16[16,40,1152]{2,1,0:T(8,128)(2,1)S(1)}, u32[]{:S(2)}, u32[]{:S(2)}) async-start(bf16[16,40,1152]{2,1,0:T(8,128)(2,1)} %broadcast_in_dim.7), calls=%async_computation | async-start | bytes 2949120 | tf_op jit(solution)/shard_map/all_to_all | solution.py:18
  23.5 1.9 %collective-permute-start.3 = (bf16[40,1152]{1,0:T(8,128)(2,1)S(1)}, bf16[40,1152]{1,0:T(8,128)(2,1)S(1)}, u32[]{:S(2)}, u32[]{:S(2)}) collective-permute-start(bf16[40,1152]{1,0:T(8,128)(2,1)S(1)} %get-tuple-element.27.refs_8_), channel_id=1, source_target_pairs={{0,32},{32,64},{64,96},{96,128},{128,160},{160,192},{192,224},{224... | collective-permute-start | bytes 276488 | tf_op jit(solution)/shard_map/ppermute | solution.py:26
  25.4 4.0 %collective-permute-start.6 = (bf16[40,1152]{1,0:T(8,128)(2,1)S(1)}, bf16[40,1152]{1,0:T(8,128)(2,1)S(1)}, u32[]{:S(2)}, u32[]{:S(2)}) collective-permute-start(bf16[40,1152]{1,0:T(8,128)(2,1)S(1)} %get-tuple-element.27.refs_8_), channel_id=1, source_target_pairs={{0,224},{32,0},{64,32},{96,64},{128,96},{160,128},{192,160},{224,1... | collective-permute-start | bytes 276488 | tf_op jit(solution)/shard_map/ppermute | solution.py:26
  29.5 2.4 %collective-permute-done.3.refs_9_ = bf16[40,1152]{1,0:T(8,128)(2,1)S(1)} collective-permute-done((bf16[40,1152]{1,0:T(8,128)(2,1)S(1)}, bf16[40,1152]{1,0:T(8,128)(2,1)S(1)}, u32[]{:S(2)}, u32[]{:S(2)}) %collective-permute-start.3) | collective-permute-done | bytes 92192 | tf_op jit(solution)/shard_map/ppermute | solution.py:26
  31.9 3.3 %collective-permute-start.7 = (bf16[40,1152]{1,0:T(8,128)(2,1)S(1)}, bf16[40,1152]{1,0:T(8,128)(2,1)S(1)}, u32[]{:S(2)}, u32[]{:S(2)}) collective-permute-start(bf16[40,1152]{1,0:T(8,128)(2,1)S(1)} %collective-permute-done.6.refs_15_), channel_id=1, source_target_pairs={{0,224},{32,0},{64,32},{96,64},{128,96},{160,128},{192,160},{224,1... | collective-permute-start | bytes 276488 | tf_op jit(solution)/shard_map/ppermute | solution.py:26
  35.2 4.5 %collective-permute-start.13 = (bf16[40,1152]{1,0:T(8,128)(2,1)S(1)}, bf16[40,1152]{1,0:T(8,128)(2,1)S(1)}, u32[]{:S(2)}, u32[]{:S(2)}) collective-permute-start(bf16[40,1152]{1,0:T(8,128)(2,1)S(1)} %get-tuple-element.27.refs_8_), channel_id=1, source_target_pairs={{0,128},{32,160},{64,192},{96,224},{128,0},{160,32},{192,64},{224,... | collective-permute-start | bytes 276488 | tf_op jit(solution)/shard_map/ppermute | solution.py:26
  39.7 3.2 %collective-permute-start.8 = (bf16[40,1152]{1,0:T(8,128)(2,1)S(1)}, bf16[40,1152]{1,0:T(8,128)(2,1)}, u32[]{:S(2)}, u32[]{:S(2)}) collective-permute-start(bf16[40,1152]{1,0:T(8,128)(2,1)S(1)} %collective-permute-done.7.refs_14_), channel_id=1, source_target_pairs={{0,224},{32,0},{64,32},{96,64},{128,96},{160,128},{192,160},{224,1... | collective-permute-start | bytes 276488 | tf_op jit(solution)/shard_map/ppermute | solution.py:26
  43.5 1.6 %collective-permute-done.13.refs_12_ = bf16[40,1152]{1,0:T(8,128)(2,1)S(1)} collective-permute-done((bf16[40,1152]{1,0:T(8,128)(2,1)S(1)}, bf16[40,1152]{1,0:T(8,128)(2,1)S(1)}, u32[]{:S(2)}, u32[]{:S(2)}) %collective-permute-start.13) | collective-permute-done | bytes 92192 | tf_op jit(solution)/shard_map/ppermute | solution.py:26
  50.2 7.7 %shard_map.93 = (bf16[320,1152]{1,0:T(8,128)(2,1)}, bf16[320,1152]{1,0:T(8,128)(2,1)}, bf16[640,1152]{1,0:T(8,128)(2,1)}) custom-call(f32[2]{0:T(128)} %pad_maximum_fusion.18.scalars, s32[1]{0:T(128)} %bitcast.8.place, bf16[640,1152]{1,0:T(8,128)(2,1)} %bitcast.94, bf16[40,1152]{1,0:T(8,128)(2,1)} %collective-permute-done.9.refs_0_, ...), custom_call_target="tpu_custom_call" | custom-call | flops 2900000000 | bytes 8000000 | tf_op jit(solution)/shard_map/pallas_call | solution.py:106
  58.1 7.8 %all-to-all-start.1 = ((bf16[16,40,1152]{2,1,0:T(8,128)(2,1)}), bf16[16,40,1152]{2,1,0:T(8,128)(2,1)S(1)}, u32[]{:S(2)}, u32[]{:S(2)}) async-start(bf16[16,40,1152]{2,1,0:T(8,128)(2,1)} %bitcast.93), calls=%async_computation.1 | async-start | bytes 2949120 | tf_op jit(solution)/shard_map/all_to_all | solution.py:18
  66.0 1.3 convert_add_fusion
  67.3 2.5 %collective-permute-start.20 = (bf16[80,1152]{1,0:T(8,128)(2,1)S(1)}, bf16[80,1152]{1,0:T(8,128)(2,1)S(1)}, u32[]{:S(2)}, u32[]{:S(2)}) collective-permute-start(bf16[80,1152]{1,0:T(8,128)(2,1)S(1)} %pad_maximum_fusion.13), channel_id=1, source_target_pairs={{0,192},{32,224},{64,0},{96,32},{128,64},{160,96},{192,128},{224,1... | collective-permute-start | bytes 552968 | tf_op jit(solution)/shard_map/ppermute | solution.py:26
  71.3 6.1 %collective-permute-done.20 = bf16[80,1152]{1,0:T(8,128)(2,1)S(1)} collective-permute-done((bf16[80,1152]{1,0:T(8,128)(2,1)S(1)}, bf16[80,1152]{1,0:T(8,128)(2,1)S(1)}, u32[]{:S(2)}, u32[]{:S(2)}) %collective-permute-start.20) | collective-permute-done | bytes 184352 | tf_op jit(solution)/shard_map/ppermute | solution.py:26
  77.4 5.1 %collective-permute-done.21 = bf16[80,1152]{1,0:T(8,128)(2,1)S(1)} collective-permute-done((bf16[80,1152]{1,0:T(8,128)(2,1)S(1)}, bf16[80,1152]{1,0:T(8,128)(2,1)S(1)}, u32[]{:S(2)}, u32[]{:S(2)}) %collective-permute-start.21) | collective-permute-done | bytes 184352 | tf_op jit(solution)/shard_map/ppermute | solution.py:26
  82.8 1.3 collective-permute-start.23
  84.0 2.4 %collective-permute-start.24 = (bf16[40,1152]{1,0:T(8,128)(2,1)S(1)}, bf16[40,1152]{1,0:T(8,128)(2,1)S(1)}, u32[]{:S(2)}, u32[]{:S(2)}) collective-permute-start(bf16[40,1152]{1,0:T(8,128)(2,1)S(1)} %get-tuple-element.48), channel_id=1, source_target_pairs={{0,224},{32,0},{64,32},{96,64},{128,96},{160,128},{192,160},{224,1... | collective-permute-start | bytes 276488 | tf_op jit(solution)/shard_map/ppermute | solution.py:26
  86.7 3.9 %collective-permute-done.22 = bf16[40,1152]{1,0:T(8,128)(2,1)S(1)} collective-permute-done((bf16[40,1152]{1,0:T(8,128)(2,1)S(1)}, bf16[40,1152]{1,0:T(8,128)(2,1)S(1)}, u32[]{:S(2)}, u32[]{:S(2)}) %collective-permute-start.22) | collective-permute-done | bytes 92192 | tf_op jit(solution)/shard_map/ppermute | solution.py:26
  93.4 4.8 %all-to-all-start.2 = ((bf16[8,200,128]{2,1,0:T(8,128)(2,1)}), bf16[8,200,128]{2,1,0:T(8,128)(2,1)S(1)}, u32[]{:S(2)}, u32[]{:S(2)}) async-start(bf16[8,200,128]{2,1,0:T(8,128)(2,1)} %bitcast.20), calls=%async_computation.2 | async-start | bytes 819200 | tf_op jit(solution)/shard_map/all_to_all | solution.py:18
  98.3 7.0 %all-to-all-done.2 = bf16[8,200,128]{2,1,0:T(8,128)(2,1)S(1)} async-done(((bf16[8,200,128]{2,1,0:T(8,128)(2,1)}), bf16[8,200,128]{2,1,0:T(8,128)(2,1)S(1)}, u32[]{:S(2)}, u32[]{:S(2)}) %all-to-all-start.2) | async-done | bytes 409632 | tf_op jit(solution)/shard_map/all_to_all | solution.py:18
  106.9 1.5 %collective-permute-start.30 = (bf16[144,640]{1,0:T(8,128)(2,1)S(1)}, bf16[144,640]{1,0:T(8,128)(2,1)S(1)}, u32[]{:S(2)}, u32[]{:S(2)}) collective-permute-start(bf16[144,640]{1,0:T(8,128)(2,1)S(1)} %get-tuple-element.47), channel_id=1, source_target_pairs={{0,4},{4,8},{8,12},{12,0},{1,5},{5,9},{9,13},{13,1},{2,6},{6,10},{... | collective-permute-start | bytes 552968 | tf_op jit(solution)/shard_map/ppermute | solution.py:26
  108.4 1.8 %collective-permute-start.29 = (bf16[144,640]{1,0:T(8,128)(2,1)S(1)}, bf16[144,640]{1,0:T(8,128)(2,1)S(1)}, u32[]{:S(2)}, u32[]{:S(2)}) collective-permute-start(bf16[144,640]{1,0:T(8,128)(2,1)S(1)} %get-tuple-element.46), channel_id=1, source_target_pairs={{0,12},{4,0},{8,4},{12,8},{1,13},{5,1},{9,5},{13,9},{2,14},{6,2},{... | collective-permute-start | bytes 552968 | tf_op jit(solution)/shard_map/ppermute | solution.py:26
  111.8 2.4 %collective-permute-done.30 = bf16[144,640]{1,0:T(8,128)(2,1)S(1)} collective-permute-done((bf16[144,640]{1,0:T(8,128)(2,1)S(1)}, bf16[144,640]{1,0:T(8,128)(2,1)S(1)}, u32[]{:S(2)}, u32[]{:S(2)}) %collective-permute-start.30) | collective-permute-done | bytes 184352 | tf_op jit(solution)/shard_map/ppermute | solution.py:26
  114.6 1.7 %collective-permute-start.26 = (bf16[2,160,288]{2,1,0:T(8,128)(2,1)S(1)}, bf16[2,160,288]{2,1,0:T(8,128)(2,1)S(1)}, u32[]{:S(2)}, u32[]{:S(2)}) collective-permute-start(bf16[2,160,288]{2,1,0:T(8,128)(2,1)S(1)} %pad_maximum_fusion.11), channel_id=1, source_target_pairs={{0,2},{1,3},{2,0},{3,1},{4,6},{5,7},{6,4},{7,5},{8,10},{9,11},{10,... | collective-permute-start | bytes 552968 | tf_op jit(solution)/shard_map/ppermute | solution.py:43
  117.9 3.2 %collective-permute-done.31 = bf16[144,640]{1,0:T(8,128)(2,1)S(1)} collective-permute-done((bf16[144,640]{1,0:T(8,128)(2,1)S(1)}, bf16[144,640]{1,0:T(8,128)(2,1)S(1)}, u32[]{:S(2)}, u32[]{:S(2)}) %collective-permute-start.31) | collective-permute-done | bytes 184352 | tf_op jit(solution)/shard_map/ppermute | solution.py:26
  121.9 3.8 %all-to-all-start.3 = ((bf16[8,18,640]{2,1,0:T(8,128)(2,1)}), bf16[8,18,640]{2,1,0:T(8,128)(2,1)S(1)}, u32[]{:S(2)}, u32[]{:S(2)}) async-start(bf16[8,18,640]{2,1,0:T(8,128)(2,1)} %reshape.146), calls=%async_computation.3 | async-start | bytes 491520 | tf_op jit(solution)/shard_map/all_to_all | solution.py:18
  125.7 1.3 collective-permute-done.27
  127.9 8.3 %all-to-all-done.3 = bf16[8,18,640]{2,1,0:T(8,128)(2,1)S(1)} async-done(((bf16[8,18,640]{2,1,0:T(8,128)(2,1)}), bf16[8,18,640]{2,1,0:T(8,128)(2,1)S(1)}, u32[]{:S(2)}, u32[]{:S(2)}) %all-to-all-start.3) | async-done | bytes 184352 | tf_op jit(solution)/shard_map/all_to_all | solution.py:18
  (143 shorter events, 23.4 us)
Async XLA Ops:
  4.4 5.7 %collective-permute-start = (f32[2,40,288]{2,1,0:T(8,128)}, f32[2,40,288]{2,1,0:T(8,128)S(1)}, u32[]{:S(2)}, u32[]{:S(2)}) collective-permute-start(f32[2,40,288]{2,1,0:T(8,128)} %get-tuple-element.61), channel_id=1, source_target_pairs={{0,1},{1,0},{2,3},{3,2},{4,5},{5,4},{6,7},{7,6},{8,9},{9,8},{10,11... | collective-permute-start | bytes 276488 | tf_op jit(solution)/shard_map/ppermute | solution.py:43
  4.4 7.8 %collective-permute-start.1 = (f32[2,40,288]{2,1,0:T(8,128)}, f32[2,40,288]{2,1,0:T(8,128)S(1)}, u32[]{:S(2)}, u32[]{:S(2)}) collective-permute-start(f32[2,40,288]{2,1,0:T(8,128)} %get-tuple-element.62), channel_id=1, source_target_pairs={{0,2},{1,3},{2,0},{3,1},{4,6},{5,7},{6,4},{7,5},{8,10},{9,11},{10,... | collective-permute-start | bytes 276488 | tf_op jit(solution)/shard_map/ppermute | solution.py:43
  6.5 7.6 %collective-permute-start.2 = (f32[2,40,288]{2,1,0:T(8,128)S(1)}, f32[2,40,288]{2,1,0:T(8,128)S(1)}, u32[]{:S(2)}, u32[]{:S(2)}) collective-permute-start(f32[2,40,288]{2,1,0:T(8,128)S(1)} %get-tuple-element.60), channel_id=1, source_target_pairs={{0,3},{1,2},{2,1},{3,0},{4,7},{5,6},{6,5},{7,4},{8,11},{9,10},{10,... | collective-permute-start | bytes 276488 | tf_op jit(solution)/shard_map/ppermute | solution.py:43
  15.9 31.4 %all-to-all-start = ((bf16[16,40,1152]{2,1,0:T(8,128)(2,1)}), bf16[16,40,1152]{2,1,0:T(8,128)(2,1)S(1)}, u32[]{:S(2)}, u32[]{:S(2)}) async-start(bf16[16,40,1152]{2,1,0:T(8,128)(2,1)} %broadcast_in_dim.7), calls=%async_computation | async-start | bytes 2949120 | tf_op jit(solution)/shard_map/all_to_all | solution.py:18
  23.5 8.4 %collective-permute-start.3 = (bf16[40,1152]{1,0:T(8,128)(2,1)S(1)}, bf16[40,1152]{1,0:T(8,128)(2,1)S(1)}, u32[]{:S(2)}, u32[]{:S(2)}) collective-permute-start(bf16[40,1152]{1,0:T(8,128)(2,1)S(1)} %get-tuple-element.27.refs_8_), channel_id=1, source_target_pairs={{0,32},{32,64},{64,96},{96,128},{128,160},{160,192},{192,224},{224... | collective-permute-start | bytes 276488 | tf_op jit(solution)/shard_map/ppermute | solution.py:26
  25.4 6.5 %collective-permute-start.6 = (bf16[40,1152]{1,0:T(8,128)(2,1)S(1)}, bf16[40,1152]{1,0:T(8,128)(2,1)S(1)}, u32[]{:S(2)}, u32[]{:S(2)}) collective-permute-start(bf16[40,1152]{1,0:T(8,128)(2,1)S(1)} %get-tuple-element.27.refs_8_), channel_id=1, source_target_pairs={{0,224},{32,0},{64,32},{96,64},{128,96},{160,128},{192,160},{224,1... | collective-permute-start | bytes 276488 | tf_op jit(solution)/shard_map/ppermute | solution.py:26
  31.9 7.8 %collective-permute-start.4 = (bf16[40,1152]{1,0:T(8,128)(2,1)S(1)}, bf16[40,1152]{1,0:T(8,128)(2,1)S(1)}, u32[]{:S(2)}, u32[]{:S(2)}) collective-permute-start(bf16[40,1152]{1,0:T(8,128)(2,1)S(1)} %collective-permute-done.3.refs_9_), channel_id=1, source_target_pairs={{0,32},{32,64},{64,96},{96,128},{128,160},{160,192},{192,224},{224... | collective-permute-start | bytes 276488 | tf_op jit(solution)/shard_map/ppermute | solution.py:26
  31.9 7.8 %collective-permute-start.7 = (bf16[40,1152]{1,0:T(8,128)(2,1)S(1)}, bf16[40,1152]{1,0:T(8,128)(2,1)S(1)}, u32[]{:S(2)}, u32[]{:S(2)}) collective-permute-start(bf16[40,1152]{1,0:T(8,128)(2,1)S(1)} %collective-permute-done.6.refs_15_), channel_id=1, source_target_pairs={{0,224},{32,0},{64,32},{96,64},{128,96},{160,128},{192,160},{224,1... | collective-permute-start | bytes 276488 | tf_op jit(solution)/shard_map/ppermute | solution.py:26
  35.2 9.9 %collective-permute-start.13 = (bf16[40,1152]{1,0:T(8,128)(2,1)S(1)}, bf16[40,1152]{1,0:T(8,128)(2,1)S(1)}, u32[]{:S(2)}, u32[]{:S(2)}) collective-permute-start(bf16[40,1152]{1,0:T(8,128)(2,1)S(1)} %get-tuple-element.27.refs_8_), channel_id=1, source_target_pairs={{0,128},{32,160},{64,192},{96,224},{128,0},{160,32},{192,64},{224,... | collective-permute-start | bytes 276488 | tf_op jit(solution)/shard_map/ppermute | solution.py:26
  39.7 6.7 %collective-permute-start.5 = (bf16[40,1152]{1,0:T(8,128)(2,1)S(1)}, bf16[40,1152]{1,0:T(8,128)(2,1)}, u32[]{:S(2)}, u32[]{:S(2)}) collective-permute-start(bf16[40,1152]{1,0:T(8,128)(2,1)S(1)} %collective-permute-done.4.refs_10_), channel_id=1, source_target_pairs={{0,32},{32,64},{64,96},{96,128},{128,160},{160,192},{192,224},{224... | collective-permute-start | bytes 276488 | tf_op jit(solution)/shard_map/ppermute | solution.py:26
  39.7 7.3 %collective-permute-start.8 = (bf16[40,1152]{1,0:T(8,128)(2,1)S(1)}, bf16[40,1152]{1,0:T(8,128)(2,1)}, u32[]{:S(2)}, u32[]{:S(2)}) collective-permute-start(bf16[40,1152]{1,0:T(8,128)(2,1)S(1)} %collective-permute-done.7.refs_14_), channel_id=1, source_target_pairs={{0,224},{32,0},{64,32},{96,64},{128,96},{160,128},{192,160},{224,1... | collective-permute-start | bytes 276488 | tf_op jit(solution)/shard_map/ppermute | solution.py:26
  43.0 4.4 %collective-permute-start.9 = (bf16[40,1152]{1,0:T(8,128)(2,1)S(1)}, bf16[40,1152]{1,0:T(8,128)(2,1)}, u32[]{:S(2)}, u32[]{:S(2)}) collective-permute-start(bf16[40,1152]{1,0:T(8,128)(2,1)S(1)} %get-tuple-element.27.refs_8_), channel_id=1, source_target_pairs={{0,1},{1,0},{2,3},{3,2},{4,5},{5,4},{6,7},{7,6},{8,9},{9,8},{10,11... | collective-permute-start | bytes 276488 | tf_op jit(solution)/shard_map/ppermute | solution.py:22
  43.0 4.7 %collective-permute-start.10 = (bf16[40,1152]{1,0:T(8,128)(2,1)S(1)}, bf16[40,1152]{1,0:T(8,128)(2,1)}, u32[]{:S(2)}, u32[]{:S(2)}) collective-permute-start(bf16[40,1152]{1,0:T(8,128)(2,1)S(1)} %collective-permute-done.3.refs_9_), channel_id=1, source_target_pairs={{0,1},{1,0},{2,3},{3,2},{4,5},{5,4},{6,7},{7,6},{8,9},{9,8},{10,11... | collective-permute-start | bytes 276488 | tf_op jit(solution)/shard_map/ppermute | solution.py:22
  45.1 2.9 %collective-permute-start.14 = (bf16[40,1152]{1,0:T(8,128)(2,1)S(1)}, bf16[40,1152]{1,0:T(8,128)(2,1)}, u32[]{:S(2)}, u32[]{:S(2)}) collective-permute-start(bf16[40,1152]{1,0:T(8,128)(2,1)S(1)} %collective-permute-done.13.refs_12_), channel_id=1, source_target_pairs={{0,1},{1,0},{2,3},{3,2},{4,5},{5,4},{6,7},{7,6},{8,9},{9,8},{10,11... | collective-permute-start | bytes 276488 | tf_op jit(solution)/shard_map/ppermute | solution.py:22
  47.1 2.5 %collective-permute-start.11 = (bf16[40,1152]{1,0:T(8,128)(2,1)S(1)}, bf16[40,1152]{1,0:T(8,128)(2,1)}, u32[]{:S(2)}, u32[]{:S(2)}) collective-permute-start(bf16[40,1152]{1,0:T(8,128)(2,1)S(1)} %collective-permute-done.4.refs_10_), channel_id=1, source_target_pairs={{0,1},{1,0},{2,3},{3,2},{4,5},{5,4},{6,7},{7,6},{8,9},{9,8},{10,11... | collective-permute-start | bytes 276488 | tf_op jit(solution)/shard_map/ppermute | solution.py:22
  48.8 9.1 %collective-permute-start.18 = (bf16[160,576]{1,0:T(8,128)(2,1)S(1)}, bf16[160,576]{1,0:T(8,128)(2,1)}, u32[]{:S(2)}, u32[]{:S(2)}) collective-permute-start(bf16[160,576]{1,0:T(8,128)(2,1)S(1)} %copy-done.8), channel_id=1, source_target_pairs={{0,16},{16,0},{1,17},{17,1},{2,18},{18,2},{3,19},{19,3},{4,20},{20... | collective-permute-start | bytes 552968 | tf_op jit(solution)/shard_map/ppermute | solution.py:165
  57.9 8.0 %collective-permute-start.19 = (bf16[320,1152]{1,0:T(8,128)(2,1)}, bf16[320,1152]{1,0:T(8,128)(2,1)}, u32[]{:S(2)}, u32[]{:S(2)}) collective-permute-start(bf16[320,1152]{1,0:T(8,128)(2,1)} %get-tuple-element.37), channel_id=1, source_target_pairs={{0,1},{1,0},{2,3},{3,2},{4,5},{5,4},{6,7},{7,6},{8,9},{9,8},{10,11... | collective-permute-start | bytes 2211848 | tf_op jit(solution)/shard_map/ppermute | solution.py:22
  58.1 33.5 %all-to-all-start.1 = ((bf16[16,40,1152]{2,1,0:T(8,128)(2,1)}), bf16[16,40,1152]{2,1,0:T(8,128)(2,1)S(1)}, u32[]{:S(2)}, u32[]{:S(2)}) async-start(bf16[16,40,1152]{2,1,0:T(8,128)(2,1)} %bitcast.93), calls=%async_computation.1 | async-start | bytes 2949120 | tf_op jit(solution)/shard_map/all_to_all | solution.py:18
  65.9 4.4 %collective-permute-start.28 = (bf16[160,576]{1,0:T(8,128)(2,1)}, bf16[160,576]{1,0:T(8,128)(2,1)S(1)}, u32[]{:S(2)}, u32[]{:S(2)}) collective-permute-start(bf16[160,576]{1,0:T(8,128)(2,1)} %collective-permute-done.18), channel_id=1, source_target_pairs={{0,1},{1,0},{2,3},{3,2},{4,5},{5,4},{6,7},{7,6},{8,9},{9,8},{10,11... | collective-permute-start | bytes 552968 | tf_op jit(solution)/shard_map/ppermute | solution.py:22
  67.3 10.1 %collective-permute-start.20 = (bf16[80,1152]{1,0:T(8,128)(2,1)S(1)}, bf16[80,1152]{1,0:T(8,128)(2,1)S(1)}, u32[]{:S(2)}, u32[]{:S(2)}) collective-permute-start(bf16[80,1152]{1,0:T(8,128)(2,1)S(1)} %pad_maximum_fusion.13), channel_id=1, source_target_pairs={{0,192},{32,224},{64,0},{96,32},{128,64},{160,96},{192,128},{224,1... | collective-permute-start | bytes 552968 | tf_op jit(solution)/shard_map/ppermute | solution.py:26
  69.9 12.7 %collective-permute-start.21 = (bf16[80,1152]{1,0:T(8,128)(2,1)S(1)}, bf16[80,1152]{1,0:T(8,128)(2,1)S(1)}, u32[]{:S(2)}, u32[]{:S(2)}) collective-permute-start(bf16[80,1152]{1,0:T(8,128)(2,1)S(1)} %concatenate.72), channel_id=1, source_target_pairs={{0,64},{32,96},{64,128},{96,160},{128,192},{160,224},{192,0},{224,... | collective-permute-start | bytes 552968 | tf_op jit(solution)/shard_map/ppermute | solution.py:26
  82.7 7.9 %collective-permute-start.22 = (bf16[40,1152]{1,0:T(8,128)(2,1)S(1)}, bf16[40,1152]{1,0:T(8,128)(2,1)S(1)}, u32[]{:S(2)}, u32[]{:S(2)}) collective-permute-start(bf16[40,1152]{1,0:T(8,128)(2,1)S(1)} %get-tuple-element.44), channel_id=1, source_target_pairs={{0,64},{32,96},{64,128},{96,160},{128,192},{160,224},{192,0},{224,... | collective-permute-start | bytes 276488 | tf_op jit(solution)/shard_map/ppermute | solution.py:26
  82.8 8.7 %collective-permute-start.23 = (bf16[40,1152]{1,0:T(8,128)(2,1)S(1)}, bf16[40,1152]{1,0:T(8,128)(2,1)S(1)}, u32[]{:S(2)}, u32[]{:S(2)}) collective-permute-start(bf16[40,1152]{1,0:T(8,128)(2,1)S(1)} %get-tuple-element.45), channel_id=1, source_target_pairs={{0,32},{32,64},{64,96},{96,128},{128,160},{160,192},{192,224},{224... | collective-permute-start | bytes 276488 | tf_op jit(solution)/shard_map/ppermute | solution.py:26
  84.0 7.5 %collective-permute-start.24 = (bf16[40,1152]{1,0:T(8,128)(2,1)S(1)}, bf16[40,1152]{1,0:T(8,128)(2,1)S(1)}, u32[]{:S(2)}, u32[]{:S(2)}) collective-permute-start(bf16[40,1152]{1,0:T(8,128)(2,1)S(1)} %get-tuple-element.48), channel_id=1, source_target_pairs={{0,224},{32,0},{64,32},{96,64},{128,96},{160,128},{192,160},{224,1... | collective-permute-start | bytes 276488 | tf_op jit(solution)/shard_map/ppermute | solution.py:26
  93.4 11.9 %all-to-all-start.2 = ((bf16[8,200,128]{2,1,0:T(8,128)(2,1)}), bf16[8,200,128]{2,1,0:T(8,128)(2,1)S(1)}, u32[]{:S(2)}, u32[]{:S(2)}) async-start(bf16[8,200,128]{2,1,0:T(8,128)(2,1)} %bitcast.20), calls=%async_computation.2 | async-start | bytes 819200 | tf_op jit(solution)/shard_map/all_to_all | solution.py:18
  106.9 7.3 %collective-permute-start.30 = (bf16[144,640]{1,0:T(8,128)(2,1)S(1)}, bf16[144,640]{1,0:T(8,128)(2,1)S(1)}, u32[]{:S(2)}, u32[]{:S(2)}) collective-permute-start(bf16[144,640]{1,0:T(8,128)(2,1)S(1)} %get-tuple-element.47), channel_id=1, source_target_pairs={{0,4},{4,8},{8,12},{12,0},{1,5},{5,9},{9,13},{13,1},{2,6},{6,10},{... | collective-permute-start | bytes 552968 | tf_op jit(solution)/shard_map/ppermute | solution.py:26
  108.4 9.4 %collective-permute-start.29 = (bf16[144,640]{1,0:T(8,128)(2,1)S(1)}, bf16[144,640]{1,0:T(8,128)(2,1)S(1)}, u32[]{:S(2)}, u32[]{:S(2)}) collective-permute-start(bf16[144,640]{1,0:T(8,128)(2,1)S(1)} %get-tuple-element.46), channel_id=1, source_target_pairs={{0,12},{4,0},{8,4},{12,8},{1,13},{5,1},{9,5},{13,9},{2,14},{6,2},{... | collective-permute-start | bytes 552968 | tf_op jit(solution)/shard_map/ppermute | solution.py:26
  111.1 14.7 %collective-permute-start.25 = (bf16[2,160,288]{2,1,0:T(8,128)(2,1)S(1)}, bf16[2,160,288]{2,1,0:T(8,128)(2,1)S(1)}, u32[]{:S(2)}, u32[]{:S(2)}) collective-permute-start(bf16[2,160,288]{2,1,0:T(8,128)(2,1)S(1)} %pad_maximum_fusion.10), channel_id=1, source_target_pairs={{0,1},{1,0},{2,3},{3,2},{4,5},{5,4},{6,7},{7,6},{8,9},{9,8},{10,11... | collective-permute-start | bytes 552968 | tf_op jit(solution)/shard_map/ppermute | solution.py:43
  114.3 6.8 %collective-permute-start.31 = (bf16[144,640]{1,0:T(8,128)(2,1)S(1)}, bf16[144,640]{1,0:T(8,128)(2,1)S(1)}, u32[]{:S(2)}, u32[]{:S(2)}) collective-permute-start(bf16[144,640]{1,0:T(8,128)(2,1)S(1)} %fusion.20), channel_id=1, source_target_pairs={{0,4},{4,8},{8,12},{12,0},{1,5},{5,9},{9,13},{13,1},{2,6},{6,10},{... | collective-permute-start | bytes 552968 | tf_op jit(solution)/shard_map/ppermute | solution.py:26
  114.6 11.1 %collective-permute-start.26 = (bf16[2,160,288]{2,1,0:T(8,128)(2,1)S(1)}, bf16[2,160,288]{2,1,0:T(8,128)(2,1)S(1)}, u32[]{:S(2)}, u32[]{:S(2)}) collective-permute-start(bf16[2,160,288]{2,1,0:T(8,128)(2,1)S(1)} %pad_maximum_fusion.11), channel_id=1, source_target_pairs={{0,2},{1,3},{2,0},{3,1},{4,6},{5,7},{6,4},{7,5},{8,10},{9,11},{10,... | collective-permute-start | bytes 552968 | tf_op jit(solution)/shard_map/ppermute | solution.py:43
  117.1 9.9 %collective-permute-start.27 = (bf16[2,160,288]{2,1,0:T(8,128)(2,1)S(1)}, bf16[2,160,288]{2,1,0:T(8,128)(2,1)S(1)}, u32[]{:S(2)}, u32[]{:S(2)}) collective-permute-start(bf16[2,160,288]{2,1,0:T(8,128)(2,1)S(1)} %pad_maximum_fusion.12), channel_id=1, source_target_pairs={{0,3},{1,2},{2,1},{3,0},{4,7},{5,6},{6,5},{7,4},{8,11},{9,10},{10,... | collective-permute-start | bytes 552968 | tf_op jit(solution)/shard_map/ppermute | solution.py:43
  121.9 14.3 %all-to-all-start.3 = ((bf16[8,18,640]{2,1,0:T(8,128)(2,1)}), bf16[8,18,640]{2,1,0:T(8,128)(2,1)S(1)}, u32[]{:S(2)}, u32[]{:S(2)}) async-start(bf16[8,18,640]{2,1,0:T(8,128)(2,1)} %reshape.146), calls=%async_computation.3 | async-start | bytes 491520 | tf_op jit(solution)/shard_map/all_to_all | solution.py:18
  (21 other events, 156.9 us)
where the time goes:
time: 140 us; the launch traced here: 138 us
  starting transfers between devices  59.9 us (43%)
  waiting for transfers between devices  46.3 us (33%)
  matrix products  8.16 us (6%)
  Pallas kernels  7.66 us (5%)
  other arithmetic  6.59 us (5%)
  local copies, waits for them, and re-layouts  6.38 us (5%)
  between operations  2.64 us (2%)
    ppermute x15, starting transfers between devices, shift(): return lax.ppermute(x, axis, [(i, (i + step) % size) for i in range(size)])  27.4 us
    ppermute x15, waiting for transfers between devices, shift(): return lax.ppermute(x, axis, [(i, (i + step) % size) for i in range(size)])  25.8 us
    all_to_all x4, starting transfers between devices, a2a(): return lax.all_to_all(x, axes, 0, 0, tiled=True)  24 us
    all_to_all x4, waiting for transfers between devices, a2a(): return lax.all_to_all(x, axes, 0, 0, tiled=True)  15.3 us
    pallas_call x1, Pallas kernels, block_grads(): pl.pallas_call(block_kernel, out_shape=[jax.ShapeDtypeStruct((320, 1152),...  7.66 us
    ppermute x6, starting transfers between devices, mp_shift(): return lax.ppermute(x, MP, pairs)  5.28 us
    ppermute x6, waiting for transfers between devices, mp_shift(): return lax.ppermute(x, MP, pairs)  5.24 us
  transfers between devices with their start and end apart: 36, of which 13 were waited for; matrix products, arithmetic and copies ran while one was open for 7% of the time, Pallas kernels for 6%

commit v1 on v0

--- a/solution.py
+++ b/solution.py
@@ -43,21 +43,53 @@
     return lax.ppermute(x, MP, pairs)
 
 
-def rows_from_slices(pair, xh, c):
-    quarters = pair.reshape(2, 2, 2, 40, 288)
-    got = {}
-    for dx in range(2):
-        for dc in range(2):
-            to = lax.dynamic_index_in_dim(quarters, xh ^ dx, 1, keepdims=False)
-            to = lax.dynamic_index_in_dim(to, c ^ dc, 1, keepdims=False)
-            got[dx, dc] = mp_shift(to, dx, dc) if dx or dc else to
+def project_kernel(*refs):
+    xh, c = lax.axis_index("xh"), lax.axis_index("c")
+    ins, outs, held, flat, sems = refs[:4], refs[4:8], refs[8:12], refs[12], refs[13]
+    copies = [pltpu.make_async_copy(ins[i], held[i], sems.at[i]) for i in range(4)]
+    for copy in copies:
+        copy.start()
+    for i in range(2):
+        copies[2 * i].wait()
+        copies[2 * i + 1].wait()
+        p = lax.dot_general(
+            held[2 * i][...], held[2 * i + 1][...], (((1,), (1,)), ((), ())), preferred_element_type=F32
+        )
+        flat[i, :, :256] = p[:, :256]
+        flat[i, :, 256:384] = jnp.concatenate([p[:, 256:], jnp.zeros((160, 96), F32)], axis=1)
+    for d in range(4):
+        at = pl.multiple_of(((xh ^ (d // 2)) * 2 + (c ^ (d % 2))) * 40, 8)
+        for i in range(2):
+            outs[d][80 * i : 80 * i + 40, :] = flat[i, pl.ds(at, 40), :128]
+            outs[d][80 * i + 40 : 80 * i + 80, :] = flat[i, pl.ds(at, 40), 128:256]
+        outs[d][160:200, :] = flat[0, pl.ds(at, 40), 256:384] + pltpu.roll(flat[1, pl.ds(at, 40), 256:384], 32, 1)
+
+
+def project(image_features, image_proj, text_features, text_proj):
+    return pl.pallas_call(
+        project_kernel,
+        out_shape=[jax.ShapeDtypeStruct((200, 128), F32)] * 4,
+        in_specs=[pl.BlockSpec(memory_space=pltpu.HBM)] * 4,
+        scratch_shapes=[pltpu.VMEM((160, 1152), BF), pltpu.VMEM((288, 1152), BF)] * 2
+        + [pltpu.VMEM((2, 160, 384), F32), pltpu.SemaphoreType.DMA((4,))],
+        compiler_params=pltpu.CompilerParams(vmem_limit_bytes=60 * 2**20),
+        cost_estimate=pl.CostEstimate(flops=220000000, bytes_accessed=2500000, transcendentals=0),
+    )(image_features, image_proj.T, text_features, text_proj.T)
+
+
+def embed(pieces, xh, c):
     parts = []
     for a in range(2):
         for b in range(2):
-            near = jnp.where(c == b, got[0, 0], got[0, 1])
-            far = jnp.where(c == b, got[1, 0], got[1, 1])
+            near = jnp.where(c == b, pieces[0], pieces[1])
+            far = jnp.where(c == b, pieces[2], pieces[3])
             parts.append(jnp.where(xh == a, near, far))
-    return jnp.concatenate(parts, axis=2)
+    rows = []
+    for i in range(2):
+        cols = [part[80 * i + 40 * j : 80 * i + 40 * j + 40] for part in parts for j in range(2)]
+        cols += [part[160:, 32 * i : 32 * i + 32] for part in parts]
+        rows.append(jnp.concatenate(cols, axis=1))
+    return jnp.stack(rows)
 
 
 def block_kernel(scalars, place, img_in, *refs):
@@ -131,9 +163,8 @@
 
 def shards(image_features, text_features, image_proj, text_proj, log_scale, bias):
     xl, y, xh, c = (lax.axis_index(a) for a in AXES[1:])
-    p_img = jnp.dot(image_features, image_proj, preferred_element_type=F32)
-    p_txt = jnp.dot(text_features, text_proj, preferred_element_type=F32)
-    stacked = jnp.concatenate(lax.optimization_barrier((image_features, text_features, p_img, p_txt))[:2])
+    sent = project(image_features, image_proj, text_features, text_proj)
+    stacked = jnp.concatenate(lax.optimization_barrier((image_features, text_features, *sent))[:2])
     col = jnp.arange(576, dtype=jnp.int32)
     source = (col % 144) // 18 * 144 + col // 144 * 18 + col % 18
 
@@ -143,7 +174,7 @@
 
     keep = pick(xl, stacked)
     give = pick(1 - xl, lax.dynamic_slice_in_dim(stacked, c * 160, 160, 0))
-    own = rows_from_slices(jnp.stack([p_img, p_txt]), xh, c)
+    own = embed([sent[0], mp_shift(sent[1], 0, 1), mp_shift(sent[2], 1, 0), mp_shift(sent[3], 1, 1)], xh, c)
     r = lax.rsqrt(jnp.sum(own * own, axis=2, keepdims=True) + 1e-06)
     z = (own * r).astype(BF)
     z, keep, give = lax.optimization_barrier((z, keep, give))
@@ -184,12 +215,12 @@
     values = z.astype(F32)
     inner = jnp.sum(values * gz, axis=2, keepdims=True)
     gp_rows = (r * (gz - values * inner)).astype(BF)
-    cut = gp_rows.reshape(2, 40, 4, 288).transpose(2, 0, 1, 3)
-    rest = jnp.concatenate([cut[:, 0, :, 256:], cut[:, 1, :, 256:]], axis=2)
-    rest = jnp.concatenate([rest, rest], axis=2)
-    piece = jnp.concatenate(
-        [cut[:, :, :, :128].reshape(4, 80, 128), cut[:, :, :, 128:256].reshape(4, 80, 128), rest], axis=1
-    )
+    pieces = []
+    for k in range(4):
+        cols = [gp_rows[:, :, 256 * k + 128 * j : 256 * k + 128 * j + 128].reshape(80, 128) for j in range(2)]
+        rest = [gp_rows[i, :, 1024 + 32 * k : 1056 + 32 * k] for i in (0, 1, 0, 1)]
+        pieces.append(jnp.concatenate(cols + [jnp.concatenate(rest, axis=1)]))
+    piece = jnp.stack(pieces)
     got = a2a(jnp.broadcast_to(piece[None], (2, 4, 200, 128)).reshape(8, 200, 128), ("xl", "xh", "c"))
     a_img, a_txt, b_img, b_txt, rest = (got[:, 40 * i : 40 * i + 40].reshape(320, 128) for i in range(5))
 

time: 140 us -> 138 us (0.986)
  Pallas kernels: 7.66 us -> 10.8 us
  other arithmetic: 6.59 us -> 3.97 us
  matrix products: 8.16 us -> 6.3 us
    pallas_call x0 -> x1, Pallas kernels: none -> 3.1 us  [project(): pl.pallas_call(project_kernel, out_shape=[jax.ShapeDtypeStruct((200, 128)...]
    dot_general x2 -> x0, matrix products: 1.91 us -> none  [the longest x1 1.48 us: shards(): p_img = jnp.dot(image_features, image_proj, preferred_element_type=F32)]
  transfers between devices with their start and end apart: 36 -> 36, of which waited for: 13 -> 13; matrix products, arithmetic and copies ran while one was open for 7% -> 6% of each run, Pallas kernels for 6% -> 6%
where the time goes in v1:
time: 138 us; the launch traced here: 136 us
  starting transfers between devices  60.2 us (44%)
  waiting for transfers between devices  46.4 us (34%)
  Pallas kernels  10.8 us (8%)
  matrix products  6.3 us (5%)
  local copies, waits for them, and re-layouts  5.3 us (4%)
  other arithmetic  3.97 us (3%)
  between operations  2.83 us (2%)
    ppermute x15, starting transfers between devices, shift(): return lax.ppermute(x, axis, [(i, (i + step) % size) for i in range(size)])  27.6 us
    ppermute x15, waiting for transfers between devices, shift(): return lax.ppermute(x, axis, [(i, (i + step) % size) for i in range(size)])  26.6 us
    all_to_all x4, starting transfers between devices, a2a(): return lax.all_to_all(x, axes, 0, 0, tiled=True)  24.1 us
    all_to_all x4, waiting for transfers between devices, a2a(): return lax.all_to_all(x, axes, 0, 0, tiled=True)  15.8 us
    pallas_call x1, Pallas kernels, block_grads(): pl.pallas_call(block_kernel, out_shape=[jax.ShapeDtypeStruct((320, 1152),...  7.66 us
    ppermute x6, starting transfers between devices, mp_shift(): return lax.ppermute(x, MP, pairs)  5.38 us
    ppermute x6, waiting for transfers between devices, mp_shift(): return lax.ppermute(x, MP, pairs)  3.94 us
    pallas_call x1, Pallas kernels, project(): pl.pallas_call(project_kernel, out_shape=[jax.ShapeDtypeStruct((200, 128)...  3.1 us
  transfers between devices with their start and end apart: 36, of which 13 were waited for; matrix products, arithmetic and copies ran while one was open for 6% of the time, Pallas kernels for 6%

profile of v1, /device:TPU:2, one launch (start us, length us, event | category | flops | bytes accessed | tf_op | source)
XLA Modules:
  0.0 135.7 jit_solution(252214866887930535)
XLA Ops:
  0.7 3.1 %shard_map.93 = (f32[200,128]{1,0:T(8,128)}, f32[200,128]{1,0:T(8,128)}, f32[200,128]{1,0:T(8,128)}, f32[200,128]{1,0:T(8,128)}) custom-call(bf16[160,1152]{1,0:T(8,128)(2,1)} %refs_0_.1, bf16[288,1152]{1,0:T(8,128)(2,1)} %bitcast.105, bf16[160,1152]{1,0:T(8,128)(2,1)} %refs_2_.1, bf16[288,1152]{1,0:T(8,128)(2,1)} %bitcast.106), custom_call_target="tpu_custom_call" | custom-call | flops 220000000 | bytes 2500000 | tf_op jit(solution)/shard_map/pallas_call | solution.py:69
  3.9 2.2 %collective-permute-start.1 = (f32[200,128]{1,0:T(8,128)}, f32[200,128]{1,0:T(8,128)S(1)}, u32[]{:S(2)}, u32[]{:S(2)}) collective-permute-start(f32[200,128]{1,0:T(8,128)} %get-tuple-element.29), channel_id=1, source_target_pairs={{0,2},{1,3},{2,0},{3,1},{4,6},{5,7},{6,4},{7,5},{8,10},{9,11},{10,... | collective-permute-start | bytes 307208 | tf_op jit(solution)/shard_map/ppermute | solution.py:43
  6.1 1.2 collective-permute-start.2
  7.4 1.6 %fusion.9 = bf16[320,576]{1,0:T(8,128)(2,1)} fusion(bf16[320,1152]{1,0:T(8,128)(2,1)S(1)} %constant_dynamic-update-slice_fusion, s32[576]{0:T(1024)S(1)} %get-tuple-element.132), kind=kOutput, calls=%fused_computation.14 | convolution fusion | flops 425521152 | bytes 1108224 | tf_op jit(solution)/shard_map/dot_general | solution.py:173
  9.7 1.2 collective-permute-done.1
  10.9 1.9 %collective-permute-done.2 = f32[200,128]{1,0:T(8,128)S(1)} collective-permute-done((f32[200,128]{1,0:T(8,128)}, f32[200,128]{1,0:T(8,128)S(1)}, u32[]{:S(2)}, u32[]{:S(2)}) %collective-permute-start.2) | collective-permute-done | bytes 102432 | tf_op jit(solution)/shard_map/ppermute | solution.py:43
  13.5 1.3 broadcast_in_dim.7
  14.8 7.2 %all-to-all-start = ((bf16[16,40,1152]{2,1,0:T(8,128)(2,1)}), bf16[16,40,1152]{2,1,0:T(8,128)(2,1)S(1)}, u32[]{:S(2)}, u32[]{:S(2)}) async-start(bf16[16,40,1152]{2,1,0:T(8,128)(2,1)} %broadcast_in_dim.7), calls=%async_computation | async-start | bytes 2949120 | tf_op jit(solution)/shard_map/all_to_all | solution.py:18
  22.0 1.9 %collective-permute-start.3 = (bf16[40,1152]{1,0:T(8,128)(2,1)S(1)}, bf16[40,1152]{1,0:T(8,128)(2,1)S(1)}, u32[]{:S(2)}, u32[]{:S(2)}) collective-permute-start(bf16[40,1152]{1,0:T(8,128)(2,1)S(1)} %get-tuple-element.35.refs_8_), channel_id=1, source_target_pairs={{0,32},{32,64},{64,96},{96,128},{128,160},{160,192},{192,224},{224... | collective-permute-start | bytes 276488 | tf_op jit(solution)/shard_map/ppermute | solution.py:26
  24.0 4.0 %collective-permute-start.6 = (bf16[40,1152]{1,0:T(8,128)(2,1)S(1)}, bf16[40,1152]{1,0:T(8,128)(2,1)S(1)}, u32[]{:S(2)}, u32[]{:S(2)}) collective-permute-start(bf16[40,1152]{1,0:T(8,128)(2,1)S(1)} %get-tuple-element.35.refs_8_), channel_id=1, source_target_pairs={{0,224},{32,0},{64,32},{96,64},{128,96},{160,128},{192,160},{224,1... | collective-permute-start | bytes 276488 | tf_op jit(solution)/shard_map/ppermute | solution.py:26
  28.0 2.5 %collective-permute-done.3.refs_9_ = bf16[40,1152]{1,0:T(8,128)(2,1)S(1)} collective-permute-done((bf16[40,1152]{1,0:T(8,128)(2,1)S(1)}, bf16[40,1152]{1,0:T(8,128)(2,1)S(1)}, u32[]{:S(2)}, u32[]{:S(2)}) %collective-permute-start.3) | collective-permute-done | bytes 92192 | tf_op jit(solution)/shard_map/ppermute | solution.py:26
  30.5 3.3 %collective-permute-start.7 = (bf16[40,1152]{1,0:T(8,128)(2,1)S(1)}, bf16[40,1152]{1,0:T(8,128)(2,1)S(1)}, u32[]{:S(2)}, u32[]{:S(2)}) collective-permute-start(bf16[40,1152]{1,0:T(8,128)(2,1)S(1)} %collective-permute-done.6.refs_15_), channel_id=1, source_target_pairs={{0,224},{32,0},{64,32},{96,64},{128,96},{160,128},{192,160},{224,1... | collective-permute-start | bytes 276488 | tf_op jit(solution)/shard_map/ppermute | solution.py:26
  33.8 4.5 %collective-permute-start.13 = (bf16[40,1152]{1,0:T(8,128)(2,1)S(1)}, bf16[40,1152]{1,0:T(8,128)(2,1)S(1)}, u32[]{:S(2)}, u32[]{:S(2)}) collective-permute-start(bf16[40,1152]{1,0:T(8,128)(2,1)S(1)} %get-tuple-element.35.refs_8_), channel_id=1, source_target_pairs={{0,128},{32,160},{64,192},{96,224},{128,0},{160,32},{192,64},{224,... | collective-permute-start | bytes 276488 | tf_op jit(solution)/shard_map/ppermute | solution.py:26
  38.3 3.2 %collective-permute-start.8 = (bf16[40,1152]{1,0:T(8,128)(2,1)S(1)}, bf16[40,1152]{1,0:T(8,128)(2,1)S(1)}, u32[]{:S(2)}, u32[]{:S(2)}) collective-permute-start(bf16[40,1152]{1,0:T(8,128)(2,1)S(1)} %collective-permute-done.7.refs_14_), channel_id=1, source_target_pairs={{0,224},{32,0},{64,32},{96,64},{128,96},{160,128},{192,160},{224,1... | collective-permute-start | bytes 276488 | tf_op jit(solution)/shard_map/ppermute | solution.py:26
  42.0 1.8 %collective-permute-done.13.refs_12_ = bf16[40,1152]{1,0:T(8,128)(2,1)S(1)} collective-permute-done((bf16[40,1152]{1,0:T(8,128)(2,1)S(1)}, bf16[40,1152]{1,0:T(8,128)(2,1)S(1)}, u32[]{:S(2)}, u32[]{:S(2)}) %collective-permute-start.13) | collective-permute-done | bytes 92192 | tf_op jit(solution)/shard_map/ppermute | solution.py:26
  49.0 7.7 %shard_map.94 = (bf16[320,1152]{1,0:T(8,128)(2,1)}, bf16[320,1152]{1,0:T(8,128)(2,1)}, bf16[640,1152]{1,0:T(8,128)(2,1)}) custom-call(f32[2]{0:T(128)} %pad_maximum_fusion.20.scalars, s32[1]{0:T(128)} %bitcast.4.place, bf16[640,1152]{1,0:T(8,128)(2,1)} %bitcast.104, bf16[40,1152]{1,0:T(8,128)(2,1)} %copy-done.16, bf16[40,1152]{1,0:T(8,128)(2,1)} %copy-done.17, ...), custom_call_target="tpu_custom_call" | custom-call | flops 2900000000 | bytes 8000000 | tf_op jit(solution)/shard_map/pallas_call | solution.py:138
  56.9 7.8 %all-to-all-start.1 = ((bf16[16,40,1152]{2,1,0:T(8,128)(2,1)}), bf16[16,40,1152]{2,1,0:T(8,128)(2,1)S(1)}, u32[]{:S(2)}, u32[]{:S(2)}) async-start(bf16[16,40,1152]{2,1,0:T(8,128)(2,1)} %bitcast.103), calls=%async_computation.1 | async-start | bytes 2949120 | tf_op jit(solution)/shard_map/all_to_all | solution.py:18
  65.0 2.5 %collective-permute-start.20 = (bf16[80,1152]{1,0:T(8,128)(2,1)S(1)}, bf16[80,1152]{1,0:T(8,128)(2,1)S(1)}, u32[]{:S(2)}, u32[]{:S(2)}) collective-permute-start(bf16[80,1152]{1,0:T(8,128)(2,1)S(1)} %pad_maximum_fusion.15), channel_id=1, source_target_pairs={{0,192},{32,224},{64,0},{96,32},{128,64},{160,96},{192,128},{224,1... | collective-permute-start | bytes 552968 | tf_op jit(solution)/shard_map/ppermute | solution.py:26
  68.1 7.9 %collective-permute-done.20 = bf16[80,1152]{1,0:T(8,128)(2,1)S(1)} collective-permute-done((bf16[80,1152]{1,0:T(8,128)(2,1)S(1)}, bf16[80,1152]{1,0:T(8,128)(2,1)S(1)}, u32[]{:S(2)}, u32[]{:S(2)}) %collective-permute-start.20) | collective-permute-done | bytes 184352 | tf_op jit(solution)/shard_map/ppermute | solution.py:26
  76.0 4.0 %collective-permute-done.21 = bf16[80,1152]{1,0:T(8,128)(2,1)S(1)} collective-permute-done((bf16[80,1152]{1,0:T(8,128)(2,1)S(1)}, bf16[80,1152]{1,0:T(8,128)(2,1)S(1)}, u32[]{:S(2)}, u32[]{:S(2)}) %collective-permute-start.21) | collective-permute-done | bytes 184352 | tf_op jit(solution)/shard_map/ppermute | solution.py:26
  80.2 1.4 %collective-permute-start.23 = (bf16[40,1152]{1,0:T(8,128)(2,1)S(1)}, bf16[40,1152]{1,0:T(8,128)(2,1)S(1)}, u32[]{:S(2)}, u32[]{:S(2)}) collective-permute-start(bf16[40,1152]{1,0:T(8,128)(2,1)S(1)} %get-tuple-element.51), channel_id=1, source_target_pairs={{0,32},{32,64},{64,96},{96,128},{128,160},{160,192},{192,224},{224... | collective-permute-start | bytes 276488 | tf_op jit(solution)/shard_map/ppermute | solution.py:26
  81.6 2.6 %collective-permute-start.24 = (bf16[40,1152]{1,0:T(8,128)(2,1)S(1)}, bf16[40,1152]{1,0:T(8,128)(2,1)S(1)}, u32[]{:S(2)}, u32[]{:S(2)}) collective-permute-start(bf16[40,1152]{1,0:T(8,128)(2,1)S(1)} %get-tuple-element.54), channel_id=1, source_target_pairs={{0,224},{32,0},{64,32},{96,64},{128,96},{160,128},{192,160},{224,1... | collective-permute-start | bytes 276488 | tf_op jit(solution)/shard_map/ppermute | solution.py:26
  84.3 3.8 %collective-permute-done.22 = bf16[40,1152]{1,0:T(8,128)(2,1)S(1)} collective-permute-done((bf16[40,1152]{1,0:T(8,128)(2,1)S(1)}, bf16[40,1152]{1,0:T(8,128)(2,1)S(1)}, u32[]{:S(2)}, u32[]{:S(2)}) %collective-permute-start.22) | collective-permute-done | bytes 92192 | tf_op jit(solution)/shard_map/ppermute | solution.py:26
  91.0 4.8 %all-to-all-start.2 = ((bf16[8,200,128]{2,1,0:T(8,128)(2,1)}), bf16[8,200,128]{2,1,0:T(8,128)(2,1)S(1)}, u32[]{:S(2)}, u32[]{:S(2)}) async-start(bf16[8,200,128]{2,1,0:T(8,128)(2,1)} %bitcast.31), calls=%async_computation.2 | async-start | bytes 819200 | tf_op jit(solution)/shard_map/all_to_all | solution.py:18
  95.9 7.0 %all-to-all-done.2 = bf16[8,200,128]{2,1,0:T(8,128)(2,1)S(1)} async-done(((bf16[8,200,128]{2,1,0:T(8,128)(2,1)}), bf16[8,200,128]{2,1,0:T(8,128)(2,1)S(1)}, u32[]{:S(2)}, u32[]{:S(2)}) %all-to-all-start.2) | async-done | bytes 409632 | tf_op jit(solution)/shard_map/all_to_all | solution.py:18
  104.5 1.5 %collective-permute-start.30 = (bf16[144,640]{1,0:T(8,128)(2,1)S(1)}, bf16[144,640]{1,0:T(8,128)(2,1)S(1)}, u32[]{:S(2)}, u32[]{:S(2)}) collective-permute-start(bf16[144,640]{1,0:T(8,128)(2,1)S(1)} %get-tuple-element.53), channel_id=1, source_target_pairs={{0,4},{4,8},{8,12},{12,0},{1,5},{5,9},{9,13},{13,1},{2,6},{6,10},{... | collective-permute-start | bytes 552968 | tf_op jit(solution)/shard_map/ppermute | solution.py:26
  106.0 1.8 %collective-permute-start.29 = (bf16[144,640]{1,0:T(8,128)(2,1)S(1)}, bf16[144,640]{1,0:T(8,128)(2,1)S(1)}, u32[]{:S(2)}, u32[]{:S(2)}) collective-permute-start(bf16[144,640]{1,0:T(8,128)(2,1)S(1)} %get-tuple-element.52), channel_id=1, source_target_pairs={{0,12},{4,0},{8,4},{12,8},{1,13},{5,1},{9,5},{13,9},{2,14},{6,2},{... | collective-permute-start | bytes 552968 | tf_op jit(solution)/shard_map/ppermute | solution.py:26
  109.4 2.4 %collective-permute-done.30 = bf16[144,640]{1,0:T(8,128)(2,1)S(1)} collective-permute-done((bf16[144,640]{1,0:T(8,128)(2,1)S(1)}, bf16[144,640]{1,0:T(8,128)(2,1)S(1)}, u32[]{:S(2)}, u32[]{:S(2)}) %collective-permute-start.30) | collective-permute-done | bytes 184352 | tf_op jit(solution)/shard_map/ppermute | solution.py:26
  112.2 1.7 %collective-permute-start.26 = (bf16[2,160,288]{2,1,0:T(8,128)(2,1)S(1)}, bf16[2,160,288]{2,1,0:T(8,128)(2,1)S(1)}, u32[]{:S(2)}, u32[]{:S(2)}) collective-permute-start(bf16[2,160,288]{2,1,0:T(8,128)(2,1)S(1)} %pad_maximum_fusion.12), channel_id=1, source_target_pairs={{0,2},{1,3},{2,0},{3,1},{4,6},{5,7},{6,4},{7,5},{8,10},{9,11},{10,... | collective-permute-start | bytes 552968 | tf_op jit(solution)/shard_map/ppermute | solution.py:43
  115.5 3.2 %collective-permute-done.31 = bf16[144,640]{1,0:T(8,128)(2,1)S(1)} collective-permute-done((bf16[144,640]{1,0:T(8,128)(2,1)S(1)}, bf16[144,640]{1,0:T(8,128)(2,1)S(1)}, u32[]{:S(2)}, u32[]{:S(2)}) %collective-permute-start.31) | collective-permute-done | bytes 184352 | tf_op jit(solution)/shard_map/ppermute | solution.py:26
  119.5 4.2 %all-to-all-start.3 = ((bf16[8,18,640]{2,1,0:T(8,128)(2,1)}), bf16[8,18,640]{2,1,0:T(8,128)(2,1)S(1)}, u32[]{:S(2)}, u32[]{:S(2)}) async-start(bf16[8,18,640]{2,1,0:T(8,128)(2,1)} %reshape.153), calls=%async_computation.3 | async-start | bytes 491520 | tf_op jit(solution)/shard_map/all_to_all | solution.py:18
  125.5 8.8 %all-to-all-done.3 = bf16[8,18,640]{2,1,0:T(8,128)(2,1)S(1)} async-done(((bf16[8,18,640]{2,1,0:T(8,128)(2,1)}), bf16[8,18,640]{2,1,0:T(8,128)(2,1)S(1)}, u32[]{:S(2)}, u32[]{:S(2)}) %all-to-all-start.3) | async-done | bytes 184352 | tf_op jit(solution)/shard_map/all_to_all | solution.py:18
  (161 shorter events, 18.8 us)
Async XLA Ops:
  3.8 6.0 %collective-permute-start = (f32[200,128]{1,0:T(8,128)}, f32[200,128]{1,0:T(8,128)S(1)}, u32[]{:S(2)}, u32[]{:S(2)}) collective-permute-start(f32[200,128]{1,0:T(8,128)} %get-tuple-element.28), channel_id=1, source_target_pairs={{0,1},{1,0},{2,3},{3,2},{4,5},{5,4},{6,7},{7,6},{8,9},{9,8},{10,11... | collective-permute-start | bytes 307208 | tf_op jit(solution)/shard_map/ppermute | solution.py:43
  3.9 7.1 %collective-permute-start.1 = (f32[200,128]{1,0:T(8,128)}, f32[200,128]{1,0:T(8,128)S(1)}, u32[]{:S(2)}, u32[]{:S(2)}) collective-permute-start(f32[200,128]{1,0:T(8,128)} %get-tuple-element.29), channel_id=1, source_target_pairs={{0,2},{1,3},{2,0},{3,1},{4,6},{5,7},{6,4},{7,5},{8,10},{9,11},{10,... | collective-permute-start | bytes 307208 | tf_op jit(solution)/shard_map/ppermute | solution.py:43
  6.1 6.8 %collective-permute-start.2 = (f32[200,128]{1,0:T(8,128)}, f32[200,128]{1,0:T(8,128)S(1)}, u32[]{:S(2)}, u32[]{:S(2)}) collective-permute-start(f32[200,128]{1,0:T(8,128)} %get-tuple-element.30), channel_id=1, source_target_pairs={{0,3},{1,2},{2,1},{3,0},{4,7},{5,6},{6,5},{7,4},{8,11},{9,10},{10,... | collective-permute-start | bytes 307208 | tf_op jit(solution)/shard_map/ppermute | solution.py:43
  14.8 31.3 %all-to-all-start = ((bf16[16,40,1152]{2,1,0:T(8,128)(2,1)}), bf16[16,40,1152]{2,1,0:T(8,128)(2,1)S(1)}, u32[]{:S(2)}, u32[]{:S(2)}) async-start(bf16[16,40,1152]{2,1,0:T(8,128)(2,1)} %broadcast_in_dim.7), calls=%async_computation | async-start | bytes 2949120 | tf_op jit(solution)/shard_map/all_to_all | solution.py:18
  22.0 8.4 %collective-permute-start.3 = (bf16[40,1152]{1,0:T(8,128)(2,1)S(1)}, bf16[40,1152]{1,0:T(8,128)(2,1)S(1)}, u32[]{:S(2)}, u32[]{:S(2)}) collective-permute-start(bf16[40,1152]{1,0:T(8,128)(2,1)S(1)} %get-tuple-element.35.refs_8_), channel_id=1, source_target_pairs={{0,32},{32,64},{64,96},{96,128},{128,160},{160,192},{192,224},{224... | collective-permute-start | bytes 276488 | tf_op jit(solution)/shard_map/ppermute | solution.py:26
  24.0 6.5 %collective-permute-start.6 = (bf16[40,1152]{1,0:T(8,128)(2,1)S(1)}, bf16[40,1152]{1,0:T(8,128)(2,1)S(1)}, u32[]{:S(2)}, u32[]{:S(2)}) collective-permute-start(bf16[40,1152]{1,0:T(8,128)(2,1)S(1)} %get-tuple-element.35.refs_8_), channel_id=1, source_target_pairs={{0,224},{32,0},{64,32},{96,64},{128,96},{160,128},{192,160},{224,1... | collective-permute-start | bytes 276488 | tf_op jit(solution)/shard_map/ppermute | solution.py:26
  30.5 7.8 %collective-permute-start.4 = (bf16[40,1152]{1,0:T(8,128)(2,1)S(1)}, bf16[40,1152]{1,0:T(8,128)(2,1)S(1)}, u32[]{:S(2)}, u32[]{:S(2)}) collective-permute-start(bf16[40,1152]{1,0:T(8,128)(2,1)S(1)} %collective-permute-done.3.refs_9_), channel_id=1, source_target_pairs={{0,32},{32,64},{64,96},{96,128},{128,160},{160,192},{192,224},{224... | collective-permute-start | bytes 276488 | tf_op jit(solution)/shard_map/ppermute | solution.py:26
  30.5 7.8 %collective-permute-start.7 = (bf16[40,1152]{1,0:T(8,128)(2,1)S(1)}, bf16[40,1152]{1,0:T(8,128)(2,1)S(1)}, u32[]{:S(2)}, u32[]{:S(2)}) collective-permute-start(bf16[40,1152]{1,0:T(8,128)(2,1)S(1)} %collective-permute-done.6.refs_15_), channel_id=1, source_target_pairs={{0,224},{32,0},{64,32},{96,64},{128,96},{160,128},{192,160},{224,1... | collective-permute-start | bytes 276488 | tf_op jit(solution)/shard_map/ppermute | solution.py:26
  33.8 10.1 %collective-permute-start.13 = (bf16[40,1152]{1,0:T(8,128)(2,1)S(1)}, bf16[40,1152]{1,0:T(8,128)(2,1)S(1)}, u32[]{:S(2)}, u32[]{:S(2)}) collective-permute-start(bf16[40,1152]{1,0:T(8,128)(2,1)S(1)} %get-tuple-element.35.refs_8_), channel_id=1, source_target_pairs={{0,128},{32,160},{64,192},{96,224},{128,0},{160,32},{192,64},{224,... | collective-permute-start | bytes 276488 | tf_op jit(solution)/shard_map/ppermute | solution.py:26
  38.2 6.9 %collective-permute-start.5 = (bf16[40,1152]{1,0:T(8,128)(2,1)S(1)}, bf16[40,1152]{1,0:T(8,128)(2,1)S(1)}, u32[]{:S(2)}, u32[]{:S(2)}) collective-permute-start(bf16[40,1152]{1,0:T(8,128)(2,1)S(1)} %collective-permute-done.4.refs_10_), channel_id=1, source_target_pairs={{0,32},{32,64},{64,96},{96,128},{128,160},{160,192},{192,224},{224... | collective-permute-start | bytes 276488 | tf_op jit(solution)/shard_map/ppermute | solution.py:26
  38.3 7.5 %collective-permute-start.8 = (bf16[40,1152]{1,0:T(8,128)(2,1)S(1)}, bf16[40,1152]{1,0:T(8,128)(2,1)S(1)}, u32[]{:S(2)}, u32[]{:S(2)}) collective-permute-start(bf16[40,1152]{1,0:T(8,128)(2,1)S(1)} %collective-permute-done.7.refs_14_), channel_id=1, source_target_pairs={{0,224},{32,0},{64,32},{96,64},{128,96},{160,128},{192,160},{224,1... | collective-permute-start | bytes 276488 | tf_op jit(solution)/shard_map/ppermute | solution.py:26
  41.5 4.6 %collective-permute-start.9 = (bf16[40,1152]{1,0:T(8,128)(2,1)S(1)}, bf16[40,1152]{1,0:T(8,128)(2,1)S(1)}, u32[]{:S(2)}, u32[]{:S(2)}) collective-permute-start(bf16[40,1152]{1,0:T(8,128)(2,1)S(1)} %get-tuple-element.35.refs_8_), channel_id=1, source_target_pairs={{0,1},{1,0},{2,3},{3,2},{4,5},{5,4},{6,7},{7,6},{8,9},{9,8},{10,11... | collective-permute-start | bytes 276488 | tf_op jit(solution)/shard_map/ppermute | solution.py:22
  41.5 4.9 %collective-permute-start.10 = (bf16[40,1152]{1,0:T(8,128)(2,1)S(1)}, bf16[40,1152]{1,0:T(8,128)(2,1)S(1)}, u32[]{:S(2)}, u32[]{:S(2)}) collective-permute-start(bf16[40,1152]{1,0:T(8,128)(2,1)S(1)} %collective-permute-done.3.refs_9_), channel_id=1, source_target_pairs={{0,1},{1,0},{2,3},{3,2},{4,5},{5,4},{6,7},{7,6},{8,9},{9,8},{10,11... | collective-permute-start | bytes 276488 | tf_op jit(solution)/shard_map/ppermute | solution.py:22
  43.8 2.9 %collective-permute-start.14 = (bf16[40,1152]{1,0:T(8,128)(2,1)S(1)}, bf16[40,1152]{1,0:T(8,128)(2,1)S(1)}, u32[]{:S(2)}, u32[]{:S(2)}) collective-permute-start(bf16[40,1152]{1,0:T(8,128)(2,1)S(1)} %collective-permute-done.13.refs_12_), channel_id=1, source_target_pairs={{0,1},{1,0},{2,3},{3,2},{4,5},{5,4},{6,7},{7,6},{8,9},{9,8},{10,11... | collective-permute-start | bytes 276488 | tf_op jit(solution)/shard_map/ppermute | solution.py:22
  45.8 2.5 %collective-permute-start.11 = (bf16[40,1152]{1,0:T(8,128)(2,1)S(1)}, bf16[40,1152]{1,0:T(8,128)(2,1)S(1)}, u32[]{:S(2)}, u32[]{:S(2)}) collective-permute-start(bf16[40,1152]{1,0:T(8,128)(2,1)S(1)} %collective-permute-done.4.refs_10_), channel_id=1, source_target_pairs={{0,1},{1,0},{2,3},{3,2},{4,5},{5,4},{6,7},{7,6},{8,9},{9,8},{10,11... | collective-permute-start | bytes 276488 | tf_op jit(solution)/shard_map/ppermute | solution.py:22
  47.5 9.2 %collective-permute-start.18 = (bf16[160,576]{1,0:T(8,128)(2,1)S(1)}, bf16[160,576]{1,0:T(8,128)(2,1)S(1)}, u32[]{:S(2)}, u32[]{:S(2)}) collective-permute-start(bf16[160,576]{1,0:T(8,128)(2,1)S(1)} %fusion.10), channel_id=1, source_target_pairs={{0,16},{16,0},{1,17},{17,1},{2,18},{18,2},{3,19},{19,3},{4,20},{20... | collective-permute-start | bytes 552968 | tf_op jit(solution)/shard_map/ppermute | solution.py:196
  56.7 8.0 %collective-permute-start.19 = (bf16[320,1152]{1,0:T(8,128)(2,1)}, bf16[320,1152]{1,0:T(8,128)(2,1)S(1)}, u32[]{:S(2)}, u32[]{:S(2)}) collective-permute-start(bf16[320,1152]{1,0:T(8,128)(2,1)} %get-tuple-element.45), channel_id=1, source_target_pairs={{0,1},{1,0},{2,3},{3,2},{4,5},{5,4},{6,7},{7,6},{8,9},{9,8},{10,11... | collective-permute-start | bytes 2211848 | tf_op jit(solution)/shard_map/ppermute | solution.py:22
  56.9 32.3 %all-to-all-start.1 = ((bf16[16,40,1152]{2,1,0:T(8,128)(2,1)}), bf16[16,40,1152]{2,1,0:T(8,128)(2,1)S(1)}, u32[]{:S(2)}, u32[]{:S(2)}) async-start(bf16[16,40,1152]{2,1,0:T(8,128)(2,1)} %bitcast.103), calls=%async_computation.1 | async-start | bytes 2949120 | tf_op jit(solution)/shard_map/all_to_all | solution.py:18
  64.7 3.3 %collective-permute-start.28 = (bf16[160,576]{1,0:T(8,128)(2,1)S(1)}, bf16[160,576]{1,0:T(8,128)(2,1)S(1)}, u32[]{:S(2)}, u32[]{:S(2)}) collective-permute-start(bf16[160,576]{1,0:T(8,128)(2,1)S(1)} %collective-permute-done.18), channel_id=1, source_target_pairs={{0,1},{1,0},{2,3},{3,2},{4,5},{5,4},{6,7},{7,6},{8,9},{9,8},{10,11... | collective-permute-start | bytes 552968 | tf_op jit(solution)/shard_map/ppermute | solution.py:22
  65.0 11.0 %collective-permute-start.20 = (bf16[80,1152]{1,0:T(8,128)(2,1)S(1)}, bf16[80,1152]{1,0:T(8,128)(2,1)S(1)}, u32[]{:S(2)}, u32[]{:S(2)}) collective-permute-start(bf16[80,1152]{1,0:T(8,128)(2,1)S(1)} %pad_maximum_fusion.15), channel_id=1, source_target_pairs={{0,192},{32,224},{64,0},{96,32},{128,64},{160,96},{192,128},{224,1... | collective-permute-start | bytes 552968 | tf_op jit(solution)/shard_map/ppermute | solution.py:26
  67.5 12.5 %collective-permute-start.21 = (bf16[80,1152]{1,0:T(8,128)(2,1)S(1)}, bf16[80,1152]{1,0:T(8,128)(2,1)S(1)}, u32[]{:S(2)}, u32[]{:S(2)}) collective-permute-start(bf16[80,1152]{1,0:T(8,128)(2,1)S(1)} %concatenate.97), channel_id=1, source_target_pairs={{0,64},{32,96},{64,128},{96,160},{128,192},{160,224},{192,0},{224,... | collective-permute-start | bytes 552968 | tf_op jit(solution)/shard_map/ppermute | solution.py:26
  80.1 8.1 %collective-permute-start.22 = (bf16[40,1152]{1,0:T(8,128)(2,1)S(1)}, bf16[40,1152]{1,0:T(8,128)(2,1)S(1)}, u32[]{:S(2)}, u32[]{:S(2)}) collective-permute-start(bf16[40,1152]{1,0:T(8,128)(2,1)S(1)} %get-tuple-element.50), channel_id=1, source_target_pairs={{0,64},{32,96},{64,128},{96,160},{128,192},{160,224},{192,0},{224,... | collective-permute-start | bytes 276488 | tf_op jit(solution)/shard_map/ppermute | solution.py:26
  80.2 9.0 %collective-permute-start.23 = (bf16[40,1152]{1,0:T(8,128)(2,1)S(1)}, bf16[40,1152]{1,0:T(8,128)(2,1)S(1)}, u32[]{:S(2)}, u32[]{:S(2)}) collective-permute-start(bf16[40,1152]{1,0:T(8,128)(2,1)S(1)} %get-tuple-element.51), channel_id=1, source_target_pairs={{0,32},{32,64},{64,96},{96,128},{128,160},{160,192},{192,224},{224... | collective-permute-start | bytes 276488 | tf_op jit(solution)/shard_map/ppermute | solution.py:26
  81.6 7.6 %collective-permute-start.24 = (bf16[40,1152]{1,0:T(8,128)(2,1)S(1)}, bf16[40,1152]{1,0:T(8,128)(2,1)S(1)}, u32[]{:S(2)}, u32[]{:S(2)}) collective-permute-start(bf16[40,1152]{1,0:T(8,128)(2,1)S(1)} %get-tuple-element.54), channel_id=1, source_target_pairs={{0,224},{32,0},{64,32},{96,64},{128,96},{160,128},{192,160},{224,1... | collective-permute-start | bytes 276488 | tf_op jit(solution)/shard_map/ppermute | solution.py:26
  91.0 11.9 %all-to-all-start.2 = ((bf16[8,200,128]{2,1,0:T(8,128)(2,1)}), bf16[8,200,128]{2,1,0:T(8,128)(2,1)S(1)}, u32[]{:S(2)}, u32[]{:S(2)}) async-start(bf16[8,200,128]{2,1,0:T(8,128)(2,1)} %bitcast.31), calls=%async_computation.2 | async-start | bytes 819200 | tf_op jit(solution)/shard_map/all_to_all | solution.py:18
  104.5 7.3 %collective-permute-start.30 = (bf16[144,640]{1,0:T(8,128)(2,1)S(1)}, bf16[144,640]{1,0:T(8,128)(2,1)S(1)}, u32[]{:S(2)}, u32[]{:S(2)}) collective-permute-start(bf16[144,640]{1,0:T(8,128)(2,1)S(1)} %get-tuple-element.53), channel_id=1, source_target_pairs={{0,4},{4,8},{8,12},{12,0},{1,5},{5,9},{9,13},{13,1},{2,6},{6,10},{... | collective-permute-start | bytes 552968 | tf_op jit(solution)/shard_map/ppermute | solution.py:26
  106.0 9.4 %collective-permute-start.29 = (bf16[144,640]{1,0:T(8,128)(2,1)S(1)}, bf16[144,640]{1,0:T(8,128)(2,1)S(1)}, u32[]{:S(2)}, u32[]{:S(2)}) collective-permute-start(bf16[144,640]{1,0:T(8,128)(2,1)S(1)} %get-tuple-element.52), channel_id=1, source_target_pairs={{0,12},{4,0},{8,4},{12,8},{1,13},{5,1},{9,5},{13,9},{2,14},{6,2},{... | collective-permute-start | bytes 552968 | tf_op jit(solution)/shard_map/ppermute | solution.py:26
  108.6 15.1 %collective-permute-start.25 = (bf16[2,160,288]{2,1,0:T(8,128)(2,1)S(1)}, bf16[2,160,288]{2,1,0:T(8,128)(2,1)S(1)}, u32[]{:S(2)}, u32[]{:S(2)}) collective-permute-start(bf16[2,160,288]{2,1,0:T(8,128)(2,1)S(1)} %pad_maximum_fusion.11), channel_id=1, source_target_pairs={{0,1},{1,0},{2,3},{3,2},{4,5},{5,4},{6,7},{7,6},{8,9},{9,8},{10,11... | collective-permute-start | bytes 552968 | tf_op jit(solution)/shard_map/ppermute | solution.py:43
  111.8 6.8 %collective-permute-start.31 = (bf16[144,640]{1,0:T(8,128)(2,1)S(1)}, bf16[144,640]{1,0:T(8,128)(2,1)S(1)}, u32[]{:S(2)}, u32[]{:S(2)}) collective-permute-start(bf16[144,640]{1,0:T(8,128)(2,1)S(1)} %fusion.20), channel_id=1, source_target_pairs={{0,4},{4,8},{8,12},{12,0},{1,5},{5,9},{9,13},{13,1},{2,6},{6,10},{... | collective-permute-start | bytes 552968 | tf_op jit(solution)/shard_map/ppermute | solution.py:26
  112.2 11.5 %collective-permute-start.26 = (bf16[2,160,288]{2,1,0:T(8,128)(2,1)S(1)}, bf16[2,160,288]{2,1,0:T(8,128)(2,1)S(1)}, u32[]{:S(2)}, u32[]{:S(2)}) collective-permute-start(bf16[2,160,288]{2,1,0:T(8,128)(2,1)S(1)} %pad_maximum_fusion.12), channel_id=1, source_target_pairs={{0,2},{1,3},{2,0},{3,1},{4,6},{5,7},{6,4},{7,5},{8,10},{9,11},{10,... | collective-permute-start | bytes 552968 | tf_op jit(solution)/shard_map/ppermute | solution.py:43
  114.7 9.9 %collective-permute-start.27 = (bf16[2,160,288]{2,1,0:T(8,128)(2,1)S(1)}, bf16[2,160,288]{2,1,0:T(8,128)(2,1)S(1)}, u32[]{:S(2)}, u32[]{:S(2)}) collective-permute-start(bf16[2,160,288]{2,1,0:T(8,128)(2,1)S(1)} %pad_maximum_fusion.13), channel_id=1, source_target_pairs={{0,3},{1,2},{2,1},{3,0},{4,7},{5,6},{6,5},{7,4},{8,11},{9,10},{10,... | collective-permute-start | bytes 552968 | tf_op jit(solution)/shard_map/ppermute | solution.py:43
  119.5 14.8 %all-to-all-start.3 = ((bf16[8,18,640]{2,1,0:T(8,128)(2,1)}), bf16[8,18,640]{2,1,0:T(8,128)(2,1)S(1)}, u32[]{:S(2)}, u32[]{:S(2)}) async-start(bf16[8,18,640]{2,1,0:T(8,128)(2,1)} %reshape.153), calls=%async_computation.3 | async-start | bytes 491520 | tf_op jit(solution)/shard_map/all_to_all | solution.py:18
  (28 other events, 165.7 us)

commit v2 on v1

--- a/solution.py
+++ b/solution.py
@@ -205,8 +205,11 @@
     fi = jnp.concatenate([first[:160], second[:160]])
     ft = jnp.concatenate([first[160:], second[160:]])
 
-    t_sum = t_own.astype(F32) + t_got.astype(F32)
-    to = {k: t_sum[40 * (-k % 8) : 40 * (-k % 8) + 40] for k in range(-3, 5)}
+    def block_sum(k):
+        at = 40 * (-k % 8)
+        return t_own[at : at + 40].astype(F32) + t_got[at : at + 40].astype(F32)
+
+    to = {k: block_sum(k) for k in range(-3, 5)}
     gz_txt = ring_sum(to)
     g_img = g_img.reshape(16, 40, 1152)
     gz_img = jnp.sum(a2a(g_img, PLANE).astype(F32), axis=0)

time: 138 us -> 138 us (level)
  waiting for transfers between devices: 46.4 us -> 40.3 us
  starting transfers between devices: 60.2 us -> 65.1 us
  other arithmetic: 3.97 us -> 5.8 us
    ppermute x15, waiting for transfers between devices: 26.6 us -> 20.6 us  [shift(): return lax.ppermute(x, axis, [(i, (i + step) % size) for i in range(size)])]
    ppermute x15, starting transfers between devices: 27.6 us -> 32.3 us  [shift(): return lax.ppermute(x, axis, [(i, (i + step) % size) for i in range(size)])]
  transfers between devices with their start and end apart: 36 -> 36, of which waited for: 13 -> 13; matrix products, arithmetic and copies ran while one was open for 6% -> 7% of each run, Pallas kernels for 6% -> 6%
where the time goes in v2:
time: 138 us; the launch traced here: 136 us
  starting transfers between devices  65.1 us (47%)
  waiting for transfers between devices  40.3 us (29%)
  Pallas kernels  10.8 us (8%)
  matrix products  6.31 us (5%)
  other arithmetic  5.8 us (4%)
  local copies, waits for them, and re-layouts  5.27 us (4%)
  between operations  2.82 us (2%)
    ppermute x15, starting transfers between devices, shift(): return lax.ppermute(x, axis, [(i, (i + step) % size) for i in range(size)])  32.3 us
    all_to_all x4, starting transfers between devices, a2a(): return lax.all_to_all(x, axes, 0, 0, tiled=True)  24.4 us
    ppermute x15, waiting for transfers between devices, shift(): return lax.ppermute(x, axis, [(i, (i + step) % size) for i in range(size)])  20.6 us
    all_to_all x4, waiting for transfers between devices, a2a(): return lax.all_to_all(x, axes, 0, 0, tiled=True)  16.1 us
    pallas_call x1, Pallas kernels, block_grads(): pl.pallas_call(block_kernel, out_shape=[jax.ShapeDtypeStruct((320, 1152),...  7.66 us
    ppermute x6, starting transfers between devices, mp_shift(): return lax.ppermute(x, MP, pairs)  5.38 us
    ppermute x6, waiting for transfers between devices, mp_shift(): return lax.ppermute(x, MP, pairs)  3.63 us
    pallas_call x1, Pallas kernels, project(): pl.pallas_call(project_kernel, out_shape=[jax.ShapeDtypeStruct((200, 128)...  3.1 us
  transfers between devices with their start and end apart: 36, of which 13 were waited for; matrix products, arithmetic and copies ran while one was open for 7% of the time, Pallas kernels for 6%

profile of v2, /device:TPU:2, one launch (start us, length us, event | category | flops | bytes accessed | tf_op | source)
XLA Modules:
  0.0 136.4 jit_solution(6907615935614270172)
XLA Ops:
  0.7 3.1 %shard_map.93 = (f32[200,128]{1,0:T(8,128)}, f32[200,128]{1,0:T(8,128)}, f32[200,128]{1,0:T(8,128)}, f32[200,128]{1,0:T(8,128)}) custom-call(bf16[160,1152]{1,0:T(8,128)(2,1)} %refs_0_.1, bf16[288,1152]{1,0:T(8,128)(2,1)} %bitcast.105, bf16[160,1152]{1,0:T(8,128)(2,1)} %refs_2_.1, bf16[288,1152]{1,0:T(8,128)(2,1)} %bitcast.106), custom_call_target="tpu_custom_call" | custom-call | flops 220000000 | bytes 2500000 | tf_op jit(solution)/shard_map/pallas_call | solution.py:69
  3.9 2.2 %collective-permute-start.1 = (f32[200,128]{1,0:T(8,128)}, f32[200,128]{1,0:T(8,128)S(1)}, u32[]{:S(2)}, u32[]{:S(2)}) collective-permute-start(f32[200,128]{1,0:T(8,128)} %get-tuple-element.29), channel_id=1, source_target_pairs={{0,2},{1,3},{2,0},{3,1},{4,6},{5,7},{6,4},{7,5},{8,10},{9,11},{10,... | collective-permute-start | bytes 307208 | tf_op jit(solution)/shard_map/ppermute | solution.py:43
  6.1 1.2 collective-permute-start.2
  7.4 1.6 %fusion.9 = bf16[320,576]{1,0:T(8,128)(2,1)} fusion(bf16[320,1152]{1,0:T(8,128)(2,1)S(1)} %constant_dynamic-update-slice_fusion, s32[576]{0:T(1024)S(1)} %get-tuple-element.132), kind=kOutput, calls=%fused_computation.13 | convolution fusion | flops 425521152 | bytes 1108224 | tf_op jit(solution)/shard_map/dot_general | solution.py:173
  9.7 1.2 collective-permute-done.1
  10.9 1.9 %collective-permute-done.2 = f32[200,128]{1,0:T(8,128)S(1)} collective-permute-done((f32[200,128]{1,0:T(8,128)}, f32[200,128]{1,0:T(8,128)S(1)}, u32[]{:S(2)}, u32[]{:S(2)}) %collective-permute-start.2) | collective-permute-done | bytes 102432 | tf_op jit(solution)/shard_map/ppermute | solution.py:43
  13.5 1.3 broadcast_in_dim.7
  14.8 7.2 %all-to-all-start = ((bf16[16,40,1152]{2,1,0:T(8,128)(2,1)}), bf16[16,40,1152]{2,1,0:T(8,128)(2,1)S(1)}, u32[]{:S(2)}, u32[]{:S(2)}) async-start(bf16[16,40,1152]{2,1,0:T(8,128)(2,1)} %broadcast_in_dim.7), calls=%async_computation | async-start | bytes 2949120 | tf_op jit(solution)/shard_map/all_to_all | solution.py:18
  22.0 1.9 %collective-permute-start.3 = (bf16[40,1152]{1,0:T(8,128)(2,1)S(1)}, bf16[40,1152]{1,0:T(8,128)(2,1)S(1)}, u32[]{:S(2)}, u32[]{:S(2)}) collective-permute-start(bf16[40,1152]{1,0:T(8,128)(2,1)S(1)} %get-tuple-element.35.refs_8_), channel_id=1, source_target_pairs={{0,32},{32,64},{64,96},{96,128},{128,160},{160,192},{192,224},{224... | collective-permute-start | bytes 276488 | tf_op jit(solution)/shard_map/ppermute | solution.py:26
  24.0 4.0 %collective-permute-start.6 = (bf16[40,1152]{1,0:T(8,128)(2,1)S(1)}, bf16[40,1152]{1,0:T(8,128)(2,1)S(1)}, u32[]{:S(2)}, u32[]{:S(2)}) collective-permute-start(bf16[40,1152]{1,0:T(8,128)(2,1)S(1)} %get-tuple-element.35.refs_8_), channel_id=1, source_target_pairs={{0,224},{32,0},{64,32},{96,64},{128,96},{160,128},{192,160},{224,1... | collective-permute-start | bytes 276488 | tf_op jit(solution)/shard_map/ppermute | solution.py:26
  28.0 2.5 %collective-permute-done.3.refs_9_ = bf16[40,1152]{1,0:T(8,128)(2,1)S(1)} collective-permute-done((bf16[40,1152]{1,0:T(8,128)(2,1)S(1)}, bf16[40,1152]{1,0:T(8,128)(2,1)S(1)}, u32[]{:S(2)}, u32[]{:S(2)}) %collective-permute-start.3) | collective-permute-done | bytes 92192 | tf_op jit(solution)/shard_map/ppermute | solution.py:26
  30.5 3.3 %collective-permute-start.7 = (bf16[40,1152]{1,0:T(8,128)(2,1)S(1)}, bf16[40,1152]{1,0:T(8,128)(2,1)S(1)}, u32[]{:S(2)}, u32[]{:S(2)}) collective-permute-start(bf16[40,1152]{1,0:T(8,128)(2,1)S(1)} %collective-permute-done.6.refs_15_), channel_id=1, source_target_pairs={{0,224},{32,0},{64,32},{96,64},{128,96},{160,128},{192,160},{224,1... | collective-permute-start | bytes 276488 | tf_op jit(solution)/shard_map/ppermute | solution.py:26
  33.8 4.5 %collective-permute-start.13 = (bf16[40,1152]{1,0:T(8,128)(2,1)S(1)}, bf16[40,1152]{1,0:T(8,128)(2,1)S(1)}, u32[]{:S(2)}, u32[]{:S(2)}) collective-permute-start(bf16[40,1152]{1,0:T(8,128)(2,1)S(1)} %get-tuple-element.35.refs_8_), channel_id=1, source_target_pairs={{0,128},{32,160},{64,192},{96,224},{128,0},{160,32},{192,64},{224,... | collective-permute-start | bytes 276488 | tf_op jit(solution)/shard_map/ppermute | solution.py:26
  38.3 3.2 %collective-permute-start.8 = (bf16[40,1152]{1,0:T(8,128)(2,1)S(1)}, bf16[40,1152]{1,0:T(8,128)(2,1)S(1)}, u32[]{:S(2)}, u32[]{:S(2)}) collective-permute-start(bf16[40,1152]{1,0:T(8,128)(2,1)S(1)} %collective-permute-done.7.refs_14_), channel_id=1, source_target_pairs={{0,224},{32,0},{64,32},{96,64},{128,96},{160,128},{192,160},{224,1... | collective-permute-start | bytes 276488 | tf_op jit(solution)/shard_map/ppermute | solution.py:26
  42.0 1.8 %collective-permute-done.13.refs_12_ = bf16[40,1152]{1,0:T(8,128)(2,1)S(1)} collective-permute-done((bf16[40,1152]{1,0:T(8,128)(2,1)S(1)}, bf16[40,1152]{1,0:T(8,128)(2,1)S(1)}, u32[]{:S(2)}, u32[]{:S(2)}) %collective-permute-start.13) | collective-permute-done | bytes 92192 | tf_op jit(solution)/shard_map/ppermute | solution.py:26
  49.0 7.7 %shard_map.94 = (bf16[320,1152]{1,0:T(8,128)(2,1)}, bf16[320,1152]{1,0:T(8,128)(2,1)}, bf16[640,1152]{1,0:T(8,128)(2,1)}) custom-call(f32[2]{0:T(128)} %pad_maximum_fusion.21.scalars, s32[1]{0:T(128)} %bitcast.4.place, bf16[640,1152]{1,0:T(8,128)(2,1)} %bitcast.104, bf16[40,1152]{1,0:T(8,128)(2,1)} %copy-done.17, bf16[40,1152]{1,0:T(8,128)(2,1)} %copy-done.18, ...), custom_call_target="tpu_custom_call" | custom-call | flops 2900000000 | bytes 8000000 | tf_op jit(solution)/shard_map/pallas_call | solution.py:138
  56.9 7.8 %all-to-all-start.1 = ((bf16[16,40,1152]{2,1,0:T(8,128)(2,1)}), bf16[16,40,1152]{2,1,0:T(8,128)(2,1)S(1)}, u32[]{:S(2)}, u32[]{:S(2)}) async-start(bf16[16,40,1152]{2,1,0:T(8,128)(2,1)} %bitcast.103), calls=%async_computation.1 | async-start | bytes 2949120 | tf_op jit(solution)/shard_map/all_to_all | solution.py:18
  65.3 3.9 %collective-permute-start.20 = (bf16[80,1152]{1,0:T(8,128)(2,1)S(1)}, bf16[80,1152]{1,0:T(8,128)(2,1)S(1)}, u32[]{:S(2)}, u32[]{:S(2)}) collective-permute-start(bf16[80,1152]{1,0:T(8,128)(2,1)S(1)} %pad_maximum_fusion.15), channel_id=1, source_target_pairs={{0,192},{32,224},{64,0},{96,32},{128,64},{160,96},{192,128},{224,1... | collective-permute-start | bytes 552968 | tf_op jit(solution)/shard_map/ppermute | solution.py:26
  69.3 7.8 %collective-permute-done.21 = bf16[80,1152]{1,0:T(8,128)(2,1)S(1)} collective-permute-done((bf16[80,1152]{1,0:T(8,128)(2,1)S(1)}, bf16[80,1152]{1,0:T(8,128)(2,1)S(1)}, u32[]{:S(2)}, u32[]{:S(2)}) %collective-permute-start.21) | collective-permute-done | bytes 184352 | tf_op jit(solution)/shard_map/ppermute | solution.py:26
  78.5 4.2 %collective-permute-start.22 = (bf16[40,1152]{1,0:T(8,128)(2,1)S(1)}, bf16[40,1152]{1,0:T(8,128)(2,1)S(1)}, u32[]{:S(2)}, u32[]{:S(2)}) collective-permute-start(bf16[40,1152]{1,0:T(8,128)(2,1)S(1)} %get-tuple-element.50), channel_id=1, source_target_pairs={{0,64},{32,96},{64,128},{96,160},{128,192},{160,224},{192,0},{224,... | collective-permute-start | bytes 276488 | tf_op jit(solution)/shard_map/ppermute | solution.py:26
  83.5 2.4 %collective-permute-start.24 = (bf16[40,1152]{1,0:T(8,128)(2,1)S(1)}, bf16[40,1152]{1,0:T(8,128)(2,1)S(1)}, u32[]{:S(2)}, u32[]{:S(2)}) collective-permute-start(bf16[40,1152]{1,0:T(8,128)(2,1)S(1)} %get-tuple-element.54), channel_id=1, source_target_pairs={{0,224},{32,0},{64,32},{96,64},{128,96},{160,128},{192,160},{224,1... | collective-permute-start | bytes 276488 | tf_op jit(solution)/shard_map/ppermute | solution.py:26
  86.1 1.1 collective-permute-done.22
  87.2 1.4 %collective-permute-done.23 = bf16[40,1152]{1,0:T(8,128)(2,1)S(1)} collective-permute-done((bf16[40,1152]{1,0:T(8,128)(2,1)S(1)}, bf16[40,1152]{1,0:T(8,128)(2,1)S(1)}, u32[]{:S(2)}, u32[]{:S(2)}) %collective-permute-start.23) | collective-permute-done | bytes 92192 | tf_op jit(solution)/shard_map/ppermute | solution.py:26
  91.4 4.8 %all-to-all-start.2 = ((bf16[8,200,128]{2,1,0:T(8,128)(2,1)}), bf16[8,200,128]{2,1,0:T(8,128)(2,1)S(1)}, u32[]{:S(2)}, u32[]{:S(2)}) async-start(bf16[8,200,128]{2,1,0:T(8,128)(2,1)} %bitcast.31), calls=%async_computation.2 | async-start | bytes 819200 | tf_op jit(solution)/shard_map/all_to_all | solution.py:18
  96.3 7.0 %all-to-all-done.2 = bf16[8,200,128]{2,1,0:T(8,128)(2,1)S(1)} async-done(((bf16[8,200,128]{2,1,0:T(8,128)(2,1)}), bf16[8,200,128]{2,1,0:T(8,128)(2,1)S(1)}, u32[]{:S(2)}, u32[]{:S(2)}) %all-to-all-start.2) | async-done | bytes 409632 | tf_op jit(solution)/shard_map/all_to_all | solution.py:18
  104.9 1.5 %collective-permute-start.30 = (bf16[144,640]{1,0:T(8,128)(2,1)S(1)}, bf16[144,640]{1,0:T(8,128)(2,1)S(1)}, u32[]{:S(2)}, u32[]{:S(2)}) collective-permute-start(bf16[144,640]{1,0:T(8,128)(2,1)S(1)} %get-tuple-element.53), channel_id=1, source_target_pairs={{0,4},{4,8},{8,12},{12,0},{1,5},{5,9},{9,13},{13,1},{2,6},{6,10},{... | collective-permute-start | bytes 552968 | tf_op jit(solution)/shard_map/ppermute | solution.py:26
  106.4 1.8 %collective-permute-start.29 = (bf16[144,640]{1,0:T(8,128)(2,1)S(1)}, bf16[144,640]{1,0:T(8,128)(2,1)S(1)}, u32[]{:S(2)}, u32[]{:S(2)}) collective-permute-start(bf16[144,640]{1,0:T(8,128)(2,1)S(1)} %get-tuple-element.52), channel_id=1, source_target_pairs={{0,12},{4,0},{8,4},{12,8},{1,13},{5,1},{9,5},{13,9},{2,14},{6,2},{... | collective-permute-start | bytes 552968 | tf_op jit(solution)/shard_map/ppermute | solution.py:26
  109.8 2.4 %collective-permute-done.30 = bf16[144,640]{1,0:T(8,128)(2,1)S(1)} collective-permute-done((bf16[144,640]{1,0:T(8,128)(2,1)S(1)}, bf16[144,640]{1,0:T(8,128)(2,1)S(1)}, u32[]{:S(2)}, u32[]{:S(2)}) %collective-permute-start.30) | collective-permute-done | bytes 184352 | tf_op jit(solution)/shard_map/ppermute | solution.py:26
  112.6 1.7 %collective-permute-start.26 = (bf16[2,160,288]{2,1,0:T(8,128)(2,1)S(1)}, bf16[2,160,288]{2,1,0:T(8,128)(2,1)S(1)}, u32[]{:S(2)}, u32[]{:S(2)}) collective-permute-start(bf16[2,160,288]{2,1,0:T(8,128)(2,1)S(1)} %pad_maximum_fusion.12), channel_id=1, source_target_pairs={{0,2},{1,3},{2,0},{3,1},{4,6},{5,7},{6,4},{7,5},{8,10},{9,11},{10,... | collective-permute-start | bytes 552968 | tf_op jit(solution)/shard_map/ppermute | solution.py:43
  115.9 3.2 %collective-permute-done.31 = bf16[144,640]{1,0:T(8,128)(2,1)S(1)} collective-permute-done((bf16[144,640]{1,0:T(8,128)(2,1)S(1)}, bf16[144,640]{1,0:T(8,128)(2,1)S(1)}, u32[]{:S(2)}, u32[]{:S(2)}) %collective-permute-start.31) | collective-permute-done | bytes 184352 | tf_op jit(solution)/shard_map/ppermute | solution.py:26
  119.9 4.6 %all-to-all-start.3 = ((bf16[8,18,640]{2,1,0:T(8,128)(2,1)}), bf16[8,18,640]{2,1,0:T(8,128)(2,1)S(1)}, u32[]{:S(2)}, u32[]{:S(2)}) async-start(bf16[8,18,640]{2,1,0:T(8,128)(2,1)} %reshape.153), calls=%async_computation.3 | async-start | bytes 491520 | tf_op jit(solution)/shard_map/all_to_all | solution.py:18
  125.9 9.1 %all-to-all-done.3 = bf16[8,18,640]{2,1,0:T(8,128)(2,1)S(1)} async-done(((bf16[8,18,640]{2,1,0:T(8,128)(2,1)}), bf16[8,18,640]{2,1,0:T(8,128)(2,1)S(1)}, u32[]{:S(2)}, u32[]{:S(2)}) %all-to-all-start.3) | async-done | bytes 184352 | tf_op jit(solution)/shard_map/all_to_all | solution.py:18
  (162 shorter events, 20.3 us)
Async XLA Ops:
  3.8 6.0 %collective-permute-start = (f32[200,128]{1,0:T(8,128)}, f32[200,128]{1,0:T(8,128)S(1)}, u32[]{:S(2)}, u32[]{:S(2)}) collective-permute-start(f32[200,128]{1,0:T(8,128)} %get-tuple-element.28), channel_id=1, source_target_pairs={{0,1},{1,0},{2,3},{3,2},{4,5},{5,4},{6,7},{7,6},{8,9},{9,8},{10,11... | collective-permute-start | bytes 307208 | tf_op jit(solution)/shard_map/ppermute | solution.py:43
  3.9 7.1 %collective-permute-start.1 = (f32[200,128]{1,0:T(8,128)}, f32[200,128]{1,0:T(8,128)S(1)}, u32[]{:S(2)}, u32[]{:S(2)}) collective-permute-start(f32[200,128]{1,0:T(8,128)} %get-tuple-element.29), channel_id=1, source_target_pairs={{0,2},{1,3},{2,0},{3,1},{4,6},{5,7},{6,4},{7,5},{8,10},{9,11},{10,... | collective-permute-start | bytes 307208 | tf_op jit(solution)/shard_map/ppermute | solution.py:43
  6.1 6.8 %collective-permute-start.2 = (f32[200,128]{1,0:T(8,128)}, f32[200,128]{1,0:T(8,128)S(1)}, u32[]{:S(2)}, u32[]{:S(2)}) collective-permute-start(f32[200,128]{1,0:T(8,128)} %get-tuple-element.30), channel_id=1, source_target_pairs={{0,3},{1,2},{2,1},{3,0},{4,7},{5,6},{6,5},{7,4},{8,11},{9,10},{10,... | collective-permute-start | bytes 307208 | tf_op jit(solution)/shard_map/ppermute | solution.py:43
  14.8 31.3 %all-to-all-start = ((bf16[16,40,1152]{2,1,0:T(8,128)(2,1)}), bf16[16,40,1152]{2,1,0:T(8,128)(2,1)S(1)}, u32[]{:S(2)}, u32[]{:S(2)}) async-start(bf16[16,40,1152]{2,1,0:T(8,128)(2,1)} %broadcast_in_dim.7), calls=%async_computation | async-start | bytes 2949120 | tf_op jit(solution)/shard_map/all_to_all | solution.py:18
  22.0 8.4 %collective-permute-start.3 = (bf16[40,1152]{1,0:T(8,128)(2,1)S(1)}, bf16[40,1152]{1,0:T(8,128)(2,1)S(1)}, u32[]{:S(2)}, u32[]{:S(2)}) collective-permute-start(bf16[40,1152]{1,0:T(8,128)(2,1)S(1)} %get-tuple-element.35.refs_8_), channel_id=1, source_target_pairs={{0,32},{32,64},{64,96},{96,128},{128,160},{160,192},{192,224},{224... | collective-permute-start | bytes 276488 | tf_op jit(solution)/shard_map/ppermute | solution.py:26
  24.0 6.5 %collective-permute-start.6 = (bf16[40,1152]{1,0:T(8,128)(2,1)S(1)}, bf16[40,1152]{1,0:T(8,128)(2,1)S(1)}, u32[]{:S(2)}, u32[]{:S(2)}) collective-permute-start(bf16[40,1152]{1,0:T(8,128)(2,1)S(1)} %get-tuple-element.35.refs_8_), channel_id=1, source_target_pairs={{0,224},{32,0},{64,32},{96,64},{128,96},{160,128},{192,160},{224,1... | collective-permute-start | bytes 276488 | tf_op jit(solution)/shard_map/ppermute | solution.py:26
  30.5 7.8 %collective-permute-start.4 = (bf16[40,1152]{1,0:T(8,128)(2,1)S(1)}, bf16[40,1152]{1,0:T(8,128)(2,1)S(1)}, u32[]{:S(2)}, u32[]{:S(2)}) collective-permute-start(bf16[40,1152]{1,0:T(8,128)(2,1)S(1)} %collective-permute-done.3.refs_9_), channel_id=1, source_target_pairs={{0,32},{32,64},{64,96},{96,128},{128,160},{160,192},{192,224},{224... | collective-permute-start | bytes 276488 | tf_op jit(solution)/shard_map/ppermute | solution.py:26
  30.5 7.8 %collective-permute-start.7 = (bf16[40,1152]{1,0:T(8,128)(2,1)S(1)}, bf16[40,1152]{1,0:T(8,128)(2,1)S(1)}, u32[]{:S(2)}, u32[]{:S(2)}) collective-permute-start(bf16[40,1152]{1,0:T(8,128)(2,1)S(1)} %collective-permute-done.6.refs_15_), channel_id=1, source_target_pairs={{0,224},{32,0},{64,32},{96,64},{128,96},{160,128},{192,160},{224,1... | collective-permute-start | bytes 276488 | tf_op jit(solution)/shard_map/ppermute | solution.py:26
  33.8 10.1 %collective-permute-start.13 = (bf16[40,1152]{1,0:T(8,128)(2,1)S(1)}, bf16[40,1152]{1,0:T(8,128)(2,1)S(1)}, u32[]{:S(2)}, u32[]{:S(2)}) collective-permute-start(bf16[40,1152]{1,0:T(8,128)(2,1)S(1)} %get-tuple-element.35.refs_8_), channel_id=1, source_target_pairs={{0,128},{32,160},{64,192},{96,224},{128,0},{160,32},{192,64},{224,... | collective-permute-start | bytes 276488 | tf_op jit(solution)/shard_map/ppermute | solution.py:26
  38.2 6.9 %collective-permute-start.5 = (bf16[40,1152]{1,0:T(8,128)(2,1)S(1)}, bf16[40,1152]{1,0:T(8,128)(2,1)S(1)}, u32[]{:S(2)}, u32[]{:S(2)}) collective-permute-start(bf16[40,1152]{1,0:T(8,128)(2,1)S(1)} %collective-permute-done.4.refs_10_), channel_id=1, source_target_pairs={{0,32},{32,64},{64,96},{96,128},{128,160},{160,192},{192,224},{224... | collective-permute-start | bytes 276488 | tf_op jit(solution)/shard_map/ppermute | solution.py:26
  38.3 7.5 %collective-permute-start.8 = (bf16[40,1152]{1,0:T(8,128)(2,1)S(1)}, bf16[40,1152]{1,0:T(8,128)(2,1)S(1)}, u32[]{:S(2)}, u32[]{:S(2)}) collective-permute-start(bf16[40,1152]{1,0:T(8,128)(2,1)S(1)} %collective-permute-done.7.refs_14_), channel_id=1, source_target_pairs={{0,224},{32,0},{64,32},{96,64},{128,96},{160,128},{192,160},{224,1... | collective-permute-start | bytes 276488 | tf_op jit(solution)/shard_map/ppermute | solution.py:26
  41.5 4.6 %collective-permute-start.9 = (bf16[40,1152]{1,0:T(8,128)(2,1)S(1)}, bf16[40,1152]{1,0:T(8,128)(2,1)S(1)}, u32[]{:S(2)}, u32[]{:S(2)}) collective-permute-start(bf16[40,1152]{1,0:T(8,128)(2,1)S(1)} %get-tuple-element.35.refs_8_), channel_id=1, source_target_pairs={{0,1},{1,0},{2,3},{3,2},{4,5},{5,4},{6,7},{7,6},{8,9},{9,8},{10,11... | collective-permute-start | bytes 276488 | tf_op jit(solution)/shard_map/ppermute | solution.py:22
  41.5 4.9 %collective-permute-start.10 = (bf16[40,1152]{1,0:T(8,128)(2,1)S(1)}, bf16[40,1152]{1,0:T(8,128)(2,1)S(1)}, u32[]{:S(2)}, u32[]{:S(2)}) collective-permute-start(bf16[40,1152]{1,0:T(8,128)(2,1)S(1)} %collective-permute-done.3.refs_9_), channel_id=1, source_target_pairs={{0,1},{1,0},{2,3},{3,2},{4,5},{5,4},{6,7},{7,6},{8,9},{9,8},{10,11... | collective-permute-start | bytes 276488 | tf_op jit(solution)/shard_map/ppermute | solution.py:22
  43.8 2.9 %collective-permute-start.14 = (bf16[40,1152]{1,0:T(8,128)(2,1)S(1)}, bf16[40,1152]{1,0:T(8,128)(2,1)S(1)}, u32[]{:S(2)}, u32[]{:S(2)}) collective-permute-start(bf16[40,1152]{1,0:T(8,128)(2,1)S(1)} %collective-permute-done.13.refs_12_), channel_id=1, source_target_pairs={{0,1},{1,0},{2,3},{3,2},{4,5},{5,4},{6,7},{7,6},{8,9},{9,8},{10,11... | collective-permute-start | bytes 276488 | tf_op jit(solution)/shard_map/ppermute | solution.py:22
  45.8 2.5 %collective-permute-start.11 = (bf16[40,1152]{1,0:T(8,128)(2,1)S(1)}, bf16[40,1152]{1,0:T(8,128)(2,1)S(1)}, u32[]{:S(2)}, u32[]{:S(2)}) collective-permute-start(bf16[40,1152]{1,0:T(8,128)(2,1)S(1)} %collective-permute-done.4.refs_10_), channel_id=1, source_target_pairs={{0,1},{1,0},{2,3},{3,2},{4,5},{5,4},{6,7},{7,6},{8,9},{9,8},{10,11... | collective-permute-start | bytes 276488 | tf_op jit(solution)/shard_map/ppermute | solution.py:22
  47.5 9.2 %collective-permute-start.18 = (bf16[160,576]{1,0:T(8,128)(2,1)S(1)}, bf16[160,576]{1,0:T(8,128)(2,1)S(1)}, u32[]{:S(2)}, u32[]{:S(2)}) collective-permute-start(bf16[160,576]{1,0:T(8,128)(2,1)S(1)} %fusion.10), channel_id=1, source_target_pairs={{0,16},{16,0},{1,17},{17,1},{2,18},{18,2},{3,19},{19,3},{4,20},{20... | collective-permute-start | bytes 552968 | tf_op jit(solution)/shard_map/ppermute | solution.py:196
  56.7 8.0 %collective-permute-start.19 = (bf16[320,1152]{1,0:T(8,128)(2,1)}, bf16[320,1152]{1,0:T(8,128)(2,1)S(1)}, u32[]{:S(2)}, u32[]{:S(2)}) collective-permute-start(bf16[320,1152]{1,0:T(8,128)(2,1)} %get-tuple-element.45), channel_id=1, source_target_pairs={{0,1},{1,0},{2,3},{3,2},{4,5},{5,4},{6,7},{7,6},{8,9},{9,8},{10,11... | collective-permute-start | bytes 2211848 | tf_op jit(solution)/shard_map/ppermute | solution.py:22
  56.9 32.7 %all-to-all-start.1 = ((bf16[16,40,1152]{2,1,0:T(8,128)(2,1)}), bf16[16,40,1152]{2,1,0:T(8,128)(2,1)S(1)}, u32[]{:S(2)}, u32[]{:S(2)}) async-start(bf16[16,40,1152]{2,1,0:T(8,128)(2,1)} %bitcast.103), calls=%async_computation.1 | async-start | bytes 2949120 | tf_op jit(solution)/shard_map/all_to_all | solution.py:18
  64.7 4.5 %collective-permute-start.28 = (bf16[160,576]{1,0:T(8,128)(2,1)S(1)}, bf16[160,576]{1,0:T(8,128)(2,1)S(1)}, u32[]{:S(2)}, u32[]{:S(2)}) collective-permute-start(bf16[160,576]{1,0:T(8,128)(2,1)S(1)} %collective-permute-done.18), channel_id=1, source_target_pairs={{0,1},{1,0},{2,3},{3,2},{4,5},{5,4},{6,7},{7,6},{8,9},{9,8},{10,11... | collective-permute-start | bytes 552968 | tf_op jit(solution)/shard_map/ppermute | solution.py:22
  64.9 12.2 %collective-permute-start.21 = (bf16[80,1152]{1,0:T(8,128)(2,1)S(1)}, bf16[80,1152]{1,0:T(8,128)(2,1)S(1)}, u32[]{:S(2)}, u32[]{:S(2)}) collective-permute-start(bf16[80,1152]{1,0:T(8,128)(2,1)S(1)} %pad_maximum_fusion.16), channel_id=1, source_target_pairs={{0,64},{32,96},{64,128},{96,160},{128,192},{160,224},{192,0},{224,... | collective-permute-start | bytes 552968 | tf_op jit(solution)/shard_map/ppermute | solution.py:26
  65.3 12.1 %collective-permute-start.20 = (bf16[80,1152]{1,0:T(8,128)(2,1)S(1)}, bf16[80,1152]{1,0:T(8,128)(2,1)S(1)}, u32[]{:S(2)}, u32[]{:S(2)}) collective-permute-start(bf16[80,1152]{1,0:T(8,128)(2,1)S(1)} %pad_maximum_fusion.15), channel_id=1, source_target_pairs={{0,192},{32,224},{64,0},{96,32},{128,64},{160,96},{192,128},{224,1... | collective-permute-start | bytes 552968 | tf_op jit(solution)/shard_map/ppermute | solution.py:26
  78.5 8.7 %collective-permute-start.22 = (bf16[40,1152]{1,0:T(8,128)(2,1)S(1)}, bf16[40,1152]{1,0:T(8,128)(2,1)S(1)}, u32[]{:S(2)}, u32[]{:S(2)}) collective-permute-start(bf16[40,1152]{1,0:T(8,128)(2,1)S(1)} %get-tuple-element.50), channel_id=1, source_target_pairs={{0,64},{32,96},{64,128},{96,160},{128,192},{160,224},{192,0},{224,... | collective-permute-start | bytes 276488 | tf_op jit(solution)/shard_map/ppermute | solution.py:26
  82.7 5.9 %collective-permute-start.23 = (bf16[40,1152]{1,0:T(8,128)(2,1)S(1)}, bf16[40,1152]{1,0:T(8,128)(2,1)S(1)}, u32[]{:S(2)}, u32[]{:S(2)}) collective-permute-start(bf16[40,1152]{1,0:T(8,128)(2,1)S(1)} %get-tuple-element.51), channel_id=1, source_target_pairs={{0,32},{32,64},{64,96},{96,128},{128,160},{160,192},{192,224},{224... | collective-permute-start | bytes 276488 | tf_op jit(solution)/shard_map/ppermute | solution.py:26
  83.5 5.1 %collective-permute-start.24 = (bf16[40,1152]{1,0:T(8,128)(2,1)S(1)}, bf16[40,1152]{1,0:T(8,128)(2,1)S(1)}, u32[]{:S(2)}, u32[]{:S(2)}) collective-permute-start(bf16[40,1152]{1,0:T(8,128)(2,1)S(1)} %get-tuple-element.54), channel_id=1, source_target_pairs={{0,224},{32,0},{64,32},{96,64},{128,96},{160,128},{192,160},{224,1... | collective-permute-start | bytes 276488 | tf_op jit(solution)/shard_map/ppermute | solution.py:26
  91.4 11.9 %all-to-all-start.2 = ((bf16[8,200,128]{2,1,0:T(8,128)(2,1)}), bf16[8,200,128]{2,1,0:T(8,128)(2,1)S(1)}, u32[]{:S(2)}, u32[]{:S(2)}) async-start(bf16[8,200,128]{2,1,0:T(8,128)(2,1)} %bitcast.31), calls=%async_computation.2 | async-start | bytes 819200 | tf_op jit(solution)/shard_map/all_to_all | solution.py:18
  104.9 7.3 %collective-permute-start.30 = (bf16[144,640]{1,0:T(8,128)(2,1)S(1)}, bf16[144,640]{1,0:T(8,128)(2,1)S(1)}, u32[]{:S(2)}, u32[]{:S(2)}) collective-permute-start(bf16[144,640]{1,0:T(8,128)(2,1)S(1)} %get-tuple-element.53), channel_id=1, source_target_pairs={{0,4},{4,8},{8,12},{12,0},{1,5},{5,9},{9,13},{13,1},{2,6},{6,10},{... | collective-permute-start | bytes 552968 | tf_op jit(solution)/shard_map/ppermute | solution.py:26
  106.4 9.4 %collective-permute-start.29 = (bf16[144,640]{1,0:T(8,128)(2,1)S(1)}, bf16[144,640]{1,0:T(8,128)(2,1)S(1)}, u32[]{:S(2)}, u32[]{:S(2)}) collective-permute-start(bf16[144,640]{1,0:T(8,128)(2,1)S(1)} %get-tuple-element.52), channel_id=1, source_target_pairs={{0,12},{4,0},{8,4},{12,8},{1,13},{5,1},{9,5},{13,9},{2,14},{6,2},{... | collective-permute-start | bytes 552968 | tf_op jit(solution)/shard_map/ppermute | solution.py:26
  109.0 15.4 %collective-permute-start.25 = (bf16[2,160,288]{2,1,0:T(8,128)(2,1)S(1)}, bf16[2,160,288]{2,1,0:T(8,128)(2,1)S(1)}, u32[]{:S(2)}, u32[]{:S(2)}) collective-permute-start(bf16[2,160,288]{2,1,0:T(8,128)(2,1)S(1)} %pad_maximum_fusion.11), channel_id=1, source_target_pairs={{0,1},{1,0},{2,3},{3,2},{4,5},{5,4},{6,7},{7,6},{8,9},{9,8},{10,11... | collective-permute-start | bytes 552968 | tf_op jit(solution)/shard_map/ppermute | solution.py:43
  112.2 6.8 %collective-permute-start.31 = (bf16[144,640]{1,0:T(8,128)(2,1)S(1)}, bf16[144,640]{1,0:T(8,128)(2,1)S(1)}, u32[]{:S(2)}, u32[]{:S(2)}) collective-permute-start(bf16[144,640]{1,0:T(8,128)(2,1)S(1)} %fusion.20), channel_id=1, source_target_pairs={{0,4},{4,8},{8,12},{12,0},{1,5},{5,9},{9,13},{13,1},{2,6},{6,10},{... | collective-permute-start | bytes 552968 | tf_op jit(solution)/shard_map/ppermute | solution.py:26
  112.6 11.9 %collective-permute-start.26 = (bf16[2,160,288]{2,1,0:T(8,128)(2,1)S(1)}, bf16[2,160,288]{2,1,0:T(8,128)(2,1)S(1)}, u32[]{:S(2)}, u32[]{:S(2)}) collective-permute-start(bf16[2,160,288]{2,1,0:T(8,128)(2,1)S(1)} %pad_maximum_fusion.12), channel_id=1, source_target_pairs={{0,2},{1,3},{2,0},{3,1},{4,6},{5,7},{6,4},{7,5},{8,10},{9,11},{10,... | collective-permute-start | bytes 552968 | tf_op jit(solution)/shard_map/ppermute | solution.py:43
  115.1 9.9 %collective-permute-start.27 = (bf16[2,160,288]{2,1,0:T(8,128)(2,1)S(1)}, bf16[2,160,288]{2,1,0:T(8,128)(2,1)S(1)}, u32[]{:S(2)}, u32[]{:S(2)}) collective-permute-start(bf16[2,160,288]{2,1,0:T(8,128)(2,1)S(1)} %pad_maximum_fusion.13), channel_id=1, source_target_pairs={{0,3},{1,2},{2,1},{3,0},{4,7},{5,6},{6,5},{7,4},{8,11},{9,10},{10,... | collective-permute-start | bytes 552968 | tf_op jit(solution)/shard_map/ppermute | solution.py:43
  119.9 15.1 %all-to-all-start.3 = ((bf16[8,18,640]{2,1,0:T(8,128)(2,1)}), bf16[8,18,640]{2,1,0:T(8,128)(2,1)S(1)}, u32[]{:S(2)}, u32[]{:S(2)}) async-start(bf16[8,18,640]{2,1,0:T(8,128)(2,1)} %reshape.153), calls=%async_computation.3 | async-start | bytes 491520 | tf_op jit(solution)/shard_map/all_to_all | solution.py:18
  (29 other events, 171.6 us)

commit v3 on v1

--- a/solution.py
+++ b/solution.py
@@ -184,11 +184,12 @@
     img = jnp.broadcast_to(z_img[None], (16, 40, 1152))
     img, z_near = lax.optimization_barrier((img, z_txt))
     img = a2a(img, PLANE).reshape(640, 1152)
-    four = shift(z_near, "z", 8, 4)
     up, down = [z_near], [z_near]
     for d in range(3):
         up.append(shift(up[-1], "z", 8, 1))
         down.append(shift(down[-1], "z", 8, -1))
+    z_four, up[2], down[2] = lax.optimization_barrier((z_near, up[2], down[2]))
+    four = shift(z_four, "z", 8, 4)
     txt_own = up + [four] + down[:0:-1]
     last_up, last_down, img = lax.optimization_barrier((up[3], down[3], img))
     txt_oth = [swap_core(piece) for piece in up[:3] + [last_up, four, last_down] + down[2:0:-1]]

time: 138 us -> 140 us (1.014)
  starting transfers between devices: 60.2 us -> 64.3 us
    ppermute x15, starting transfers between devices: 27.6 us -> 30.9 us  [shift(): return lax.ppermute(x, axis, [(i, (i + step) % size) for i in range(size)])]
    ppermute x15, waiting for transfers between devices: 26.6 us -> 25.1 us  [shift(): return lax.ppermute(x, axis, [(i, (i + step) % size) for i in range(size)])]
    all_to_all x4, starting transfers between devices: 24.1 us -> 25.5 us  [a2a(): return lax.all_to_all(x, axes, 0, 0, tiled=True)]
  transfers between devices with their start and end apart: 36 -> 36, of which waited for: 13 -> 12; matrix products, arithmetic and copies ran while one was open for 6% -> 6% of each run, Pallas kernels for 6% -> 6%
where the time goes in v3:
time: 140 us; the launch traced here: 138 us
  starting transfers between devices  64.3 us (46%)
  waiting for transfers between devices  45.2 us (32%)
  Pallas kernels  10.8 us (8%)
  matrix products  6.3 us (4%)
  local copies, waits for them, and re-layouts  5.25 us (4%)
  other arithmetic  3.97 us (3%)
  between operations  2.73 us (2%)
    ppermute x15, starting transfers between devices, shift(): return lax.ppermute(x, axis, [(i, (i + step) % size) for i in range(size)])  30.9 us
    all_to_all x4, starting transfers between devices, a2a(): return lax.all_to_all(x, axes, 0, 0, tiled=True)  25.5 us
    ppermute x15, waiting for transfers between devices, shift(): return lax.ppermute(x, axis, [(i, (i + step) % size) for i in range(size)])  25.1 us
    all_to_all x4, waiting for transfers between devices, a2a(): return lax.all_to_all(x, axes, 0, 0, tiled=True)  16.6 us
    pallas_call x1, Pallas kernels, block_grads(): pl.pallas_call(block_kernel, out_shape=[jax.ShapeDtypeStruct((320, 1152),...  7.66 us
    ppermute x6, starting transfers between devices, mp_shift(): return lax.ppermute(x, MP, pairs)  5.39 us
    ppermute x6, waiting for transfers between devices, mp_shift(): return lax.ppermute(x, MP, pairs)  3.13 us
    pallas_call x1, Pallas kernels, project(): pl.pallas_call(project_kernel, out_shape=[jax.ShapeDtypeStruct((200, 128)...  3.1 us
  transfers between devices with their start and end apart: 36, of which 12 were waited for; matrix products, arithmetic and copies ran while one was open for 6% of the time, Pallas kernels for 6%

profile of v3, /device:TPU:2, one launch (start us, length us, event | category | flops | bytes accessed | tf_op | source)
XLA Modules:
  0.0 138.5 jit_solution(7455608832357852448)
XLA Ops:
  0.7 3.1 %shard_map.93 = (f32[200,128]{1,0:T(8,128)}, f32[200,128]{1,0:T(8,128)}, f32[200,128]{1,0:T(8,128)}, f32[200,128]{1,0:T(8,128)}) custom-call(bf16[160,1152]{1,0:T(8,128)(2,1)} %refs_0_.1, bf16[288,1152]{1,0:T(8,128)(2,1)} %bitcast.105, bf16[160,1152]{1,0:T(8,128)(2,1)} %refs_2_.1, bf16[288,1152]{1,0:T(8,128)(2,1)} %bitcast.106), custom_call_target="tpu_custom_call" | custom-call | flops 220000000 | bytes 2500000 | tf_op jit(solution)/shard_map/pallas_call | solution.py:69
  3.9 2.2 %collective-permute-start.1 = (f32[200,128]{1,0:T(8,128)}, f32[200,128]{1,0:T(8,128)S(1)}, u32[]{:S(2)}, u32[]{:S(2)}) collective-permute-start(f32[200,128]{1,0:T(8,128)} %get-tuple-element.32), channel_id=1, source_target_pairs={{0,2},{1,3},{2,0},{3,1},{4,6},{5,7},{6,4},{7,5},{8,10},{9,11},{10,... | collective-permute-start | bytes 307208 | tf_op jit(solution)/shard_map/ppermute | solution.py:43
  6.1 1.2 collective-permute-start.2
  7.4 1.6 %fusion.9 = bf16[320,576]{1,0:T(8,128)(2,1)} fusion(bf16[320,1152]{1,0:T(8,128)(2,1)S(1)} %constant_dynamic-update-slice_fusion, s32[576]{0:T(1024)S(1)} %get-tuple-element.138), kind=kOutput, calls=%fused_computation.14 | convolution fusion | flops 425521152 | bytes 1108224 | tf_op jit(solution)/shard_map/dot_general | solution.py:173
  9.7 1.2 collective-permute-done.1
  10.9 1.9 %collective-permute-done.2 = f32[200,128]{1,0:T(8,128)S(1)} collective-permute-done((f32[200,128]{1,0:T(8,128)}, f32[200,128]{1,0:T(8,128)S(1)}, u32[]{:S(2)}, u32[]{:S(2)}) %collective-permute-start.2) | collective-permute-done | bytes 102432 | tf_op jit(solution)/shard_map/ppermute | solution.py:43
  13.5 1.3 broadcast_in_dim.7
  14.8 7.2 %all-to-all-start = ((bf16[16,40,1152]{2,1,0:T(8,128)(2,1)}), bf16[16,40,1152]{2,1,0:T(8,128)(2,1)S(1)}, u32[]{:S(2)}, u32[]{:S(2)}) async-start(bf16[16,40,1152]{2,1,0:T(8,128)(2,1)} %broadcast_in_dim.7), calls=%async_computation | async-start | bytes 2949120 | tf_op jit(solution)/shard_map/all_to_all | solution.py:18
  22.0 1.9 %collective-permute-start.3 = (bf16[40,1152]{1,0:T(8,128)(2,1)S(1)}, bf16[40,1152]{1,0:T(8,128)(2,1)S(1)}, u32[]{:S(2)}, u32[]{:S(2)}) collective-permute-start(bf16[40,1152]{1,0:T(8,128)(2,1)S(1)} %get-tuple-element.44.refs_8_), channel_id=1, source_target_pairs={{0,32},{32,64},{64,96},{96,128},{128,160},{160,192},{192,224},{224... | collective-permute-start | bytes 276488 | tf_op jit(solution)/shard_map/ppermute | solution.py:26
  24.0 4.0 %collective-permute-start.6 = (bf16[40,1152]{1,0:T(8,128)(2,1)S(1)}, bf16[40,1152]{1,0:T(8,128)(2,1)S(1)}, u32[]{:S(2)}, u32[]{:S(2)}) collective-permute-start(bf16[40,1152]{1,0:T(8,128)(2,1)S(1)} %get-tuple-element.44.refs_8_), channel_id=1, source_target_pairs={{0,224},{32,0},{64,32},{96,64},{128,96},{160,128},{192,160},{224,1... | collective-permute-start | bytes 276488 | tf_op jit(solution)/shard_map/ppermute | solution.py:26
  28.0 2.5 %collective-permute-done.3.refs_9_ = bf16[40,1152]{1,0:T(8,128)(2,1)S(1)} collective-permute-done((bf16[40,1152]{1,0:T(8,128)(2,1)S(1)}, bf16[40,1152]{1,0:T(8,128)(2,1)S(1)}, u32[]{:S(2)}, u32[]{:S(2)}) %collective-permute-start.3) | collective-permute-done | bytes 92192 | tf_op jit(solution)/shard_map/ppermute | solution.py:26
  30.5 3.3 %collective-permute-start.7 = (bf16[40,1152]{1,0:T(8,128)(2,1)S(1)}, bf16[40,1152]{1,0:T(8,128)(2,1)S(1)}, u32[]{:S(2)}, u32[]{:S(2)}) collective-permute-start(bf16[40,1152]{1,0:T(8,128)(2,1)S(1)} %collective-permute-done.6.refs_15_), channel_id=1, source_target_pairs={{0,224},{32,0},{64,32},{96,64},{128,96},{160,128},{192,160},{224,1... | collective-permute-start | bytes 276488 | tf_op jit(solution)/shard_map/ppermute | solution.py:26
  33.8 2.5 %collective-permute-done.4.refs_10_ = bf16[40,1152]{1,0:T(8,128)(2,1)S(1)} collective-permute-done((bf16[40,1152]{1,0:T(8,128)(2,1)S(1)}, bf16[40,1152]{1,0:T(8,128)(2,1)S(1)}, u32[]{:S(2)}, u32[]{:S(2)}) %collective-permute-start.4) | collective-permute-done | bytes 92192 | tf_op jit(solution)/shard_map/ppermute | solution.py:26
  36.3 3.3 %collective-permute-start.8 = (bf16[40,1152]{1,0:T(8,128)(2,1)S(1)}, bf16[40,1152]{1,0:T(8,128)(2,1)S(1)}, u32[]{:S(2)}, u32[]{:S(2)}) collective-permute-start(bf16[40,1152]{1,0:T(8,128)(2,1)S(1)} %collective-permute-done.7.refs_14_), channel_id=1, source_target_pairs={{0,224},{32,0},{64,32},{96,64},{128,96},{160,128},{192,160},{224,1... | collective-permute-start | bytes 276488 | tf_op jit(solution)/shard_map/ppermute | solution.py:26
  39.5 4.5 %collective-permute-start.13 = (bf16[40,1152]{1,0:T(8,128)(2,1)S(1)}, bf16[40,1152]{1,0:T(8,128)(2,1)S(1)}, u32[]{:S(2)}, u32[]{:S(2)}) collective-permute-start(bf16[40,1152]{1,0:T(8,128)(2,1)S(1)} %get-tuple-element.44.refs_8_), channel_id=1, source_target_pairs={{0,128},{32,160},{64,192},{96,224},{128,0},{160,32},{192,64},{224,... | collective-permute-start | bytes 276488 | tf_op jit(solution)/shard_map/ppermute | solution.py:26
  46.8 3.1 %collective-permute-done.13.refs_12_ = bf16[40,1152]{1,0:T(8,128)(2,1)S(1)} collective-permute-done((bf16[40,1152]{1,0:T(8,128)(2,1)S(1)}, bf16[40,1152]{1,0:T(8,128)(2,1)S(1)}, u32[]{:S(2)}, u32[]{:S(2)}) %collective-permute-start.13) | collective-permute-done | bytes 92192 | tf_op jit(solution)/shard_map/ppermute | solution.py:26
  52.4 7.7 %shard_map.94 = (bf16[320,1152]{1,0:T(8,128)(2,1)}, bf16[320,1152]{1,0:T(8,128)(2,1)}, bf16[640,1152]{1,0:T(8,128)(2,1)}) custom-call(f32[2]{0:T(128)} %pad_maximum_fusion.20.scalars, s32[1]{0:T(128)} %bitcast.4.place, bf16[640,1152]{1,0:T(8,128)(2,1)} %bitcast.104, bf16[40,1152]{1,0:T(8,128)(2,1)} %copy-done.15, bf16[40,1152]{1,0:T(8,128)(2,1)} %copy-done.17, ...), custom_call_target="tpu_custom_call" | custom-call | flops 2900000000 | bytes 8000000 | tf_op jit(solution)/shard_map/pallas_call | solution.py:138
  60.3 8.1 %all-to-all-start.1 = ((bf16[16,40,1152]{2,1,0:T(8,128)(2,1)}), bf16[16,40,1152]{2,1,0:T(8,128)(2,1)S(1)}, u32[]{:S(2)}, u32[]{:S(2)}) async-start(bf16[16,40,1152]{2,1,0:T(8,128)(2,1)} %bitcast.103), calls=%async_computation.1 | async-start | bytes 2949120 | tf_op jit(solution)/shard_map/all_to_all | solution.py:18
  68.7 2.9 %collective-permute-start.21 = (bf16[80,1152]{1,0:T(8,128)(2,1)S(1)}, bf16[80,1152]{1,0:T(8,128)(2,1)S(1)}, u32[]{:S(2)}, u32[]{:S(2)}) collective-permute-start(bf16[80,1152]{1,0:T(8,128)(2,1)S(1)} %concatenate.97), channel_id=1, source_target_pairs={{0,64},{32,96},{64,128},{96,160},{128,192},{160,224},{192,0},{224,... | collective-permute-start | bytes 552968 | tf_op jit(solution)/shard_map/ppermute | solution.py:26
  71.7 6.9 %collective-permute-done.20 = bf16[80,1152]{1,0:T(8,128)(2,1)S(1)} collective-permute-done((bf16[80,1152]{1,0:T(8,128)(2,1)S(1)}, bf16[80,1152]{1,0:T(8,128)(2,1)S(1)}, u32[]{:S(2)}, u32[]{:S(2)}) %collective-permute-start.20) | collective-permute-done | bytes 184352 | tf_op jit(solution)/shard_map/ppermute | solution.py:26
  78.8 1.5 %collective-permute-start.22 = (bf16[40,1152]{1,0:T(8,128)(2,1)S(1)}, bf16[40,1152]{1,0:T(8,128)(2,1)S(1)}, u32[]{:S(2)}, u32[]{:S(2)}) collective-permute-start(bf16[40,1152]{1,0:T(8,128)(2,1)S(1)} %get-tuple-element.56), channel_id=1, source_target_pairs={{0,64},{32,96},{64,128},{96,160},{128,192},{160,224},{192,0},{224,... | collective-permute-start | bytes 276488 | tf_op jit(solution)/shard_map/ppermute | solution.py:26
  80.3 4.6 %collective-permute-start.23 = (bf16[40,1152]{1,0:T(8,128)(2,1)S(1)}, bf16[40,1152]{1,0:T(8,128)(2,1)S(1)}, u32[]{:S(2)}, u32[]{:S(2)}) collective-permute-start(bf16[40,1152]{1,0:T(8,128)(2,1)S(1)} %get-tuple-element.57), channel_id=1, source_target_pairs={{0,32},{32,64},{64,96},{96,128},{128,160},{160,192},{192,224},{224... | collective-permute-start | bytes 276488 | tf_op jit(solution)/shard_map/ppermute | solution.py:26
  84.8 1.5 %collective-permute-start.24 = (bf16[40,1152]{1,0:T(8,128)(2,1)S(1)}, bf16[40,1152]{1,0:T(8,128)(2,1)S(1)}, u32[]{:S(2)}, u32[]{:S(2)}) collective-permute-start(bf16[40,1152]{1,0:T(8,128)(2,1)S(1)} %get-tuple-element.60), channel_id=1, source_target_pairs={{0,224},{32,0},{64,32},{96,64},{128,96},{160,128},{192,160},{224,1... | collective-permute-start | bytes 276488 | tf_op jit(solution)/shard_map/ppermute | solution.py:26
  86.5 4.3 %collective-permute-done.23 = bf16[40,1152]{1,0:T(8,128)(2,1)S(1)} collective-permute-done((bf16[40,1152]{1,0:T(8,128)(2,1)S(1)}, bf16[40,1152]{1,0:T(8,128)(2,1)S(1)}, u32[]{:S(2)}, u32[]{:S(2)}) %collective-permute-start.23) | collective-permute-done | bytes 92192 | tf_op jit(solution)/shard_map/ppermute | solution.py:26
  92.6 5.4 %all-to-all-start.2 = ((bf16[8,200,128]{2,1,0:T(8,128)(2,1)}), bf16[8,200,128]{2,1,0:T(8,128)(2,1)S(1)}, u32[]{:S(2)}, u32[]{:S(2)}) async-start(bf16[8,200,128]{2,1,0:T(8,128)(2,1)} %bitcast.31), calls=%async_computation.2 | async-start | bytes 819200 | tf_op jit(solution)/shard_map/all_to_all | solution.py:18
  98.1 7.0 %all-to-all-done.2 = bf16[8,200,128]{2,1,0:T(8,128)(2,1)S(1)} async-done(((bf16[8,200,128]{2,1,0:T(8,128)(2,1)}), bf16[8,200,128]{2,1,0:T(8,128)(2,1)S(1)}, u32[]{:S(2)}, u32[]{:S(2)}) %all-to-all-start.2) | async-done | bytes 409632 | tf_op jit(solution)/shard_map/all_to_all | solution.py:18
  107.6 2.4 %collective-permute-start.29 = (bf16[144,640]{1,0:T(8,128)(2,1)S(1)}, bf16[144,640]{1,0:T(8,128)(2,1)S(1)}, u32[]{:S(2)}, u32[]{:S(2)}) collective-permute-start(bf16[144,640]{1,0:T(8,128)(2,1)S(1)} %get-tuple-element.58), channel_id=1, source_target_pairs={{0,12},{4,0},{8,4},{12,8},{1,13},{5,1},{9,5},{13,9},{2,14},{6,2},{... | collective-permute-start | bytes 552968 | tf_op jit(solution)/shard_map/ppermute | solution.py:26
  111.6 2.4 %collective-permute-done.30 = bf16[144,640]{1,0:T(8,128)(2,1)S(1)} collective-permute-done((bf16[144,640]{1,0:T(8,128)(2,1)S(1)}, bf16[144,640]{1,0:T(8,128)(2,1)S(1)}, u32[]{:S(2)}, u32[]{:S(2)}) %collective-permute-start.30) | collective-permute-done | bytes 184352 | tf_op jit(solution)/shard_map/ppermute | solution.py:26
  114.2 1.7 %collective-permute-start.26 = (bf16[2,160,288]{2,1,0:T(8,128)(2,1)S(1)}, bf16[2,160,288]{2,1,0:T(8,128)(2,1)S(1)}, u32[]{:S(2)}, u32[]{:S(2)}) collective-permute-start(bf16[2,160,288]{2,1,0:T(8,128)(2,1)S(1)} %pad_maximum_fusion.12), channel_id=1, source_target_pairs={{0,2},{1,3},{2,0},{3,1},{4,6},{5,7},{6,4},{7,5},{8,10},{9,11},{10,... | collective-permute-start | bytes 552968 | tf_op jit(solution)/shard_map/ppermute | solution.py:43
  117.4 3.4 %collective-permute-done.31 = bf16[144,640]{1,0:T(8,128)(2,1)S(1)} collective-permute-done((bf16[144,640]{1,0:T(8,128)(2,1)S(1)}, bf16[144,640]{1,0:T(8,128)(2,1)S(1)}, u32[]{:S(2)}, u32[]{:S(2)}) %collective-permute-start.31) | collective-permute-done | bytes 184352 | tf_op jit(solution)/shard_map/ppermute | solution.py:26
  121.7 4.8 %all-to-all-start.3 = ((bf16[8,18,640]{2,1,0:T(8,128)(2,1)}), bf16[8,18,640]{2,1,0:T(8,128)(2,1)S(1)}, u32[]{:S(2)}, u32[]{:S(2)}) async-start(bf16[8,18,640]{2,1,0:T(8,128)(2,1)} %reshape.153), calls=%async_computation.3 | async-start | bytes 491520 | tf_op jit(solution)/shard_map/all_to_all | solution.py:18
  127.5 9.6 %all-to-all-done.3 = bf16[8,18,640]{2,1,0:T(8,128)(2,1)S(1)} async-done(((bf16[8,18,640]{2,1,0:T(8,128)(2,1)}), bf16[8,18,640]{2,1,0:T(8,128)(2,1)S(1)}, u32[]{:S(2)}, u32[]{:S(2)}) %all-to-all-start.3) | async-done | bytes 184352 | tf_op jit(solution)/shard_map/all_to_all | solution.py:18
  (161 shorter events, 16.9 us)
Async XLA Ops:
  3.8 6.0 %collective-permute-start = (f32[200,128]{1,0:T(8,128)}, f32[200,128]{1,0:T(8,128)S(1)}, u32[]{:S(2)}, u32[]{:S(2)}) collective-permute-start(f32[200,128]{1,0:T(8,128)} %get-tuple-element.31), channel_id=1, source_target_pairs={{0,1},{1,0},{2,3},{3,2},{4,5},{5,4},{6,7},{7,6},{8,9},{9,8},{10,11... | collective-permute-start | bytes 307208 | tf_op jit(solution)/shard_map/ppermute | solution.py:43
  3.9 7.1 %collective-permute-start.1 = (f32[200,128]{1,0:T(8,128)}, f32[200,128]{1,0:T(8,128)S(1)}, u32[]{:S(2)}, u32[]{:S(2)}) collective-permute-start(f32[200,128]{1,0:T(8,128)} %get-tuple-element.32), channel_id=1, source_target_pairs={{0,2},{1,3},{2,0},{3,1},{4,6},{5,7},{6,4},{7,5},{8,10},{9,11},{10,... | collective-permute-start | bytes 307208 | tf_op jit(solution)/shard_map/ppermute | solution.py:43
  6.1 6.8 %collective-permute-start.2 = (f32[200,128]{1,0:T(8,128)}, f32[200,128]{1,0:T(8,128)S(1)}, u32[]{:S(2)}, u32[]{:S(2)}) collective-permute-start(f32[200,128]{1,0:T(8,128)} %get-tuple-element.33), channel_id=1, source_target_pairs={{0,3},{1,2},{2,1},{3,0},{4,7},{5,6},{6,5},{7,4},{8,11},{9,10},{10,... | collective-permute-start | bytes 307208 | tf_op jit(solution)/shard_map/ppermute | solution.py:43
  14.8 31.4 %all-to-all-start = ((bf16[16,40,1152]{2,1,0:T(8,128)(2,1)}), bf16[16,40,1152]{2,1,0:T(8,128)(2,1)S(1)}, u32[]{:S(2)}, u32[]{:S(2)}) async-start(bf16[16,40,1152]{2,1,0:T(8,128)(2,1)} %broadcast_in_dim.7), calls=%async_computation | async-start | bytes 2949120 | tf_op jit(solution)/shard_map/all_to_all | solution.py:18
  22.0 8.4 %collective-permute-start.3 = (bf16[40,1152]{1,0:T(8,128)(2,1)S(1)}, bf16[40,1152]{1,0:T(8,128)(2,1)S(1)}, u32[]{:S(2)}, u32[]{:S(2)}) collective-permute-start(bf16[40,1152]{1,0:T(8,128)(2,1)S(1)} %get-tuple-element.44.refs_8_), channel_id=1, source_target_pairs={{0,32},{32,64},{64,96},{96,128},{128,160},{160,192},{192,224},{224... | collective-permute-start | bytes 276488 | tf_op jit(solution)/shard_map/ppermute | solution.py:26
  24.0 6.5 %collective-permute-start.6 = (bf16[40,1152]{1,0:T(8,128)(2,1)S(1)}, bf16[40,1152]{1,0:T(8,128)(2,1)S(1)}, u32[]{:S(2)}, u32[]{:S(2)}) collective-permute-start(bf16[40,1152]{1,0:T(8,128)(2,1)S(1)} %get-tuple-element.44.refs_8_), channel_id=1, source_target_pairs={{0,224},{32,0},{64,32},{96,64},{128,96},{160,128},{192,160},{224,1... | collective-permute-start | bytes 276488 | tf_op jit(solution)/shard_map/ppermute | solution.py:26
  30.5 5.8 %collective-permute-start.4 = (bf16[40,1152]{1,0:T(8,128)(2,1)S(1)}, bf16[40,1152]{1,0:T(8,128)(2,1)S(1)}, u32[]{:S(2)}, u32[]{:S(2)}) collective-permute-start(bf16[40,1152]{1,0:T(8,128)(2,1)S(1)} %collective-permute-done.3.refs_9_), channel_id=1, source_target_pairs={{0,32},{32,64},{64,96},{96,128},{128,160},{160,192},{192,224},{224... | collective-permute-start | bytes 276488 | tf_op jit(solution)/shard_map/ppermute | solution.py:26
  30.5 5.8 %collective-permute-start.7 = (bf16[40,1152]{1,0:T(8,128)(2,1)S(1)}, bf16[40,1152]{1,0:T(8,128)(2,1)S(1)}, u32[]{:S(2)}, u32[]{:S(2)}) collective-permute-start(bf16[40,1152]{1,0:T(8,128)(2,1)S(1)} %collective-permute-done.6.refs_15_), channel_id=1, source_target_pairs={{0,224},{32,0},{64,32},{96,64},{128,96},{160,128},{192,160},{224,1... | collective-permute-start | bytes 276488 | tf_op jit(solution)/shard_map/ppermute | solution.py:26
  36.2 8.0 %collective-permute-start.5 = (bf16[40,1152]{1,0:T(8,128)(2,1)S(1)}, bf16[40,1152]{1,0:T(8,128)(2,1)S(1)}, u32[]{:S(2)}, u32[]{:S(2)}) collective-permute-start(bf16[40,1152]{1,0:T(8,128)(2,1)S(1)} %collective-permute-done.4.refs_10_), channel_id=1, source_target_pairs={{0,32},{32,64},{64,96},{96,128},{128,160},{160,192},{192,224},{224... | collective-permute-start | bytes 276488 | tf_op jit(solution)/shard_map/ppermute | solution.py:26
  36.3 9.6 %collective-permute-start.8 = (bf16[40,1152]{1,0:T(8,128)(2,1)S(1)}, bf16[40,1152]{1,0:T(8,128)(2,1)S(1)}, u32[]{:S(2)}, u32[]{:S(2)}) collective-permute-start(bf16[40,1152]{1,0:T(8,128)(2,1)S(1)} %collective-permute-done.7.refs_14_), channel_id=1, source_target_pairs={{0,224},{32,0},{64,32},{96,64},{128,96},{160,128},{192,160},{224,1... | collective-permute-start | bytes 276488 | tf_op jit(solution)/shard_map/ppermute | solution.py:26
  39.5 6.7 %collective-permute-start.9 = (bf16[40,1152]{1,0:T(8,128)(2,1)S(1)}, bf16[40,1152]{1,0:T(8,128)(2,1)S(1)}, u32[]{:S(2)}, u32[]{:S(2)}) collective-permute-start(bf16[40,1152]{1,0:T(8,128)(2,1)S(1)} %get-tuple-element.44.refs_8_), channel_id=1, source_target_pairs={{0,1},{1,0},{2,3},{3,2},{4,5},{5,4},{6,7},{7,6},{8,9},{9,8},{10,11... | collective-permute-start | bytes 276488 | tf_op jit(solution)/shard_map/ppermute | solution.py:22
  39.5 10.4 %collective-permute-start.13 = (bf16[40,1152]{1,0:T(8,128)(2,1)S(1)}, bf16[40,1152]{1,0:T(8,128)(2,1)S(1)}, u32[]{:S(2)}, u32[]{:S(2)}) collective-permute-start(bf16[40,1152]{1,0:T(8,128)(2,1)S(1)} %get-tuple-element.44.refs_8_), channel_id=1, source_target_pairs={{0,128},{32,160},{64,192},{96,224},{128,0},{160,32},{192,64},{224,... | collective-permute-start | bytes 276488 | tf_op jit(solution)/shard_map/ppermute | solution.py:26
  44.0 6.0 %collective-permute-start.10 = (bf16[40,1152]{1,0:T(8,128)(2,1)S(1)}, bf16[40,1152]{1,0:T(8,128)(2,1)S(1)}, u32[]{:S(2)}, u32[]{:S(2)}) collective-permute-start(bf16[40,1152]{1,0:T(8,128)(2,1)S(1)} %collective-permute-done.3.refs_9_), channel_id=1, source_target_pairs={{0,1},{1,0},{2,3},{3,2},{4,5},{5,4},{6,7},{7,6},{8,9},{9,8},{10,11... | collective-permute-start | bytes 276488 | tf_op jit(solution)/shard_map/ppermute | solution.py:22
  44.2 6.2 %collective-permute-start.17 = (bf16[40,1152]{1,0:T(8,128)(2,1)S(1)}, bf16[40,1152]{1,0:T(8,128)(2,1)S(1)}, u32[]{:S(2)}, u32[]{:S(2)}) collective-permute-start(bf16[40,1152]{1,0:T(8,128)(2,1)S(1)} %collective-permute-done.6.refs_15_), channel_id=1, source_target_pairs={{0,1},{1,0},{2,3},{3,2},{4,5},{5,4},{6,7},{7,6},{8,9},{9,8},{10,11... | collective-permute-start | bytes 276488 | tf_op jit(solution)/shard_map/ppermute | solution.py:22
  45.9 5.2 %collective-permute-start.11 = (bf16[40,1152]{1,0:T(8,128)(2,1)S(1)}, bf16[40,1152]{1,0:T(8,128)(2,1)S(1)}, u32[]{:S(2)}, u32[]{:S(2)}) collective-permute-start(bf16[40,1152]{1,0:T(8,128)(2,1)S(1)} %collective-permute-done.4.refs_10_), channel_id=1, source_target_pairs={{0,1},{1,0},{2,3},{3,2},{4,5},{5,4},{6,7},{7,6},{8,9},{9,8},{10,11... | collective-permute-start | bytes 276488 | tf_op jit(solution)/shard_map/ppermute | solution.py:22
  46.2 5.1 %collective-permute-start.16 = (bf16[40,1152]{1,0:T(8,128)(2,1)S(1)}, bf16[40,1152]{1,0:T(8,128)(2,1)S(1)}, u32[]{:S(2)}, u32[]{:S(2)}) collective-permute-start(bf16[40,1152]{1,0:T(8,128)(2,1)S(1)} %collective-permute-done.7.refs_14_), channel_id=1, source_target_pairs={{0,1},{1,0},{2,3},{3,2},{4,5},{5,4},{6,7},{7,6},{8,9},{9,8},{10,11... | collective-permute-start | bytes 276488 | tf_op jit(solution)/shard_map/ppermute | solution.py:22
  51.1 8.9 %collective-permute-start.18 = (bf16[160,576]{1,0:T(8,128)(2,1)S(1)}, bf16[160,576]{1,0:T(8,128)(2,1)S(1)}, u32[]{:S(2)}, u32[]{:S(2)}) collective-permute-start(bf16[160,576]{1,0:T(8,128)(2,1)S(1)} %fusion.10), channel_id=1, source_target_pairs={{0,16},{16,0},{1,17},{17,1},{2,18},{18,2},{3,19},{19,3},{4,20},{20... | collective-permute-start | bytes 552968 | tf_op jit(solution)/shard_map/ppermute | solution.py:197
  60.0 8.3 %collective-permute-start.19 = (bf16[320,1152]{1,0:T(8,128)(2,1)}, bf16[320,1152]{1,0:T(8,128)(2,1)S(1)}, u32[]{:S(2)}, u32[]{:S(2)}) collective-permute-start(bf16[320,1152]{1,0:T(8,128)(2,1)} %get-tuple-element.51), channel_id=1, source_target_pairs={{0,1},{1,0},{2,3},{3,2},{4,5},{5,4},{6,7},{7,6},{8,9},{9,8},{10,11... | collective-permute-start | bytes 2211848 | tf_op jit(solution)/shard_map/ppermute | solution.py:22
  60.3 30.6 %all-to-all-start.1 = ((bf16[16,40,1152]{2,1,0:T(8,128)(2,1)}), bf16[16,40,1152]{2,1,0:T(8,128)(2,1)S(1)}, u32[]{:S(2)}, u32[]{:S(2)}) async-start(bf16[16,40,1152]{2,1,0:T(8,128)(2,1)} %bitcast.103), calls=%async_computation.1 | async-start | bytes 2949120 | tf_op jit(solution)/shard_map/all_to_all | solution.py:18
  68.6 10.0 %collective-permute-start.20 = (bf16[80,1152]{1,0:T(8,128)(2,1)S(1)}, bf16[80,1152]{1,0:T(8,128)(2,1)S(1)}, u32[]{:S(2)}, u32[]{:S(2)}) collective-permute-start(bf16[80,1152]{1,0:T(8,128)(2,1)S(1)} %pad_maximum_fusion.15), channel_id=1, source_target_pairs={{0,192},{32,224},{64,0},{96,32},{128,64},{160,96},{192,128},{224,1... | collective-permute-start | bytes 552968 | tf_op jit(solution)/shard_map/ppermute | solution.py:26
  68.7 9.9 %collective-permute-start.21 = (bf16[80,1152]{1,0:T(8,128)(2,1)S(1)}, bf16[80,1152]{1,0:T(8,128)(2,1)S(1)}, u32[]{:S(2)}, u32[]{:S(2)}) collective-permute-start(bf16[80,1152]{1,0:T(8,128)(2,1)S(1)} %concatenate.97), channel_id=1, source_target_pairs={{0,64},{32,96},{64,128},{96,160},{128,192},{160,224},{192,0},{224,... | collective-permute-start | bytes 552968 | tf_op jit(solution)/shard_map/ppermute | solution.py:26
  78.8 7.7 %collective-permute-start.22 = (bf16[40,1152]{1,0:T(8,128)(2,1)S(1)}, bf16[40,1152]{1,0:T(8,128)(2,1)S(1)}, u32[]{:S(2)}, u32[]{:S(2)}) collective-permute-start(bf16[40,1152]{1,0:T(8,128)(2,1)S(1)} %get-tuple-element.56), channel_id=1, source_target_pairs={{0,64},{32,96},{64,128},{96,160},{128,192},{160,224},{192,0},{224,... | collective-permute-start | bytes 276488 | tf_op jit(solution)/shard_map/ppermute | solution.py:26
  80.3 10.5 %collective-permute-start.23 = (bf16[40,1152]{1,0:T(8,128)(2,1)S(1)}, bf16[40,1152]{1,0:T(8,128)(2,1)S(1)}, u32[]{:S(2)}, u32[]{:S(2)}) collective-permute-start(bf16[40,1152]{1,0:T(8,128)(2,1)S(1)} %get-tuple-element.57), channel_id=1, source_target_pairs={{0,32},{32,64},{64,96},{96,128},{128,160},{160,192},{192,224},{224... | collective-permute-start | bytes 276488 | tf_op jit(solution)/shard_map/ppermute | solution.py:26
  84.8 6.0 %collective-permute-start.24 = (bf16[40,1152]{1,0:T(8,128)(2,1)S(1)}, bf16[40,1152]{1,0:T(8,128)(2,1)S(1)}, u32[]{:S(2)}, u32[]{:S(2)}) collective-permute-start(bf16[40,1152]{1,0:T(8,128)(2,1)S(1)} %get-tuple-element.60), channel_id=1, source_target_pairs={{0,224},{32,0},{64,32},{96,64},{128,96},{160,128},{192,160},{224,1... | collective-permute-start | bytes 276488 | tf_op jit(solution)/shard_map/ppermute | solution.py:26
  92.6 12.4 %all-to-all-start.2 = ((bf16[8,200,128]{2,1,0:T(8,128)(2,1)}), bf16[8,200,128]{2,1,0:T(8,128)(2,1)S(1)}, u32[]{:S(2)}, u32[]{:S(2)}) async-start(bf16[8,200,128]{2,1,0:T(8,128)(2,1)} %bitcast.31), calls=%async_computation.2 | async-start | bytes 819200 | tf_op jit(solution)/shard_map/all_to_all | solution.py:18
  106.7 7.3 %collective-permute-start.30 = (bf16[144,640]{1,0:T(8,128)(2,1)S(1)}, bf16[144,640]{1,0:T(8,128)(2,1)S(1)}, u32[]{:S(2)}, u32[]{:S(2)}) collective-permute-start(bf16[144,640]{1,0:T(8,128)(2,1)S(1)} %get-tuple-element.59), channel_id=1, source_target_pairs={{0,4},{4,8},{8,12},{12,0},{1,5},{5,9},{9,13},{13,1},{2,6},{6,10},{... | collective-permute-start | bytes 552968 | tf_op jit(solution)/shard_map/ppermute | solution.py:26
  107.6 9.8 %collective-permute-start.29 = (bf16[144,640]{1,0:T(8,128)(2,1)S(1)}, bf16[144,640]{1,0:T(8,128)(2,1)S(1)}, u32[]{:S(2)}, u32[]{:S(2)}) collective-permute-start(bf16[144,640]{1,0:T(8,128)(2,1)S(1)} %get-tuple-element.58), channel_id=1, source_target_pairs={{0,12},{4,0},{8,4},{12,8},{1,13},{5,1},{9,5},{13,9},{2,14},{6,2},{... | collective-permute-start | bytes 552968 | tf_op jit(solution)/shard_map/ppermute | solution.py:26
  110.9 15.7 %collective-permute-start.25 = (bf16[2,160,288]{2,1,0:T(8,128)(2,1)S(1)}, bf16[2,160,288]{2,1,0:T(8,128)(2,1)S(1)}, u32[]{:S(2)}, u32[]{:S(2)}) collective-permute-start(bf16[2,160,288]{2,1,0:T(8,128)(2,1)S(1)} %pad_maximum_fusion.11), channel_id=1, source_target_pairs={{0,1},{1,0},{2,3},{3,2},{4,5},{5,4},{6,7},{7,6},{8,9},{9,8},{10,11... | collective-permute-start | bytes 552968 | tf_op jit(solution)/shard_map/ppermute | solution.py:43
  114.1 6.8 %collective-permute-start.31 = (bf16[144,640]{1,0:T(8,128)(2,1)S(1)}, bf16[144,640]{1,0:T(8,128)(2,1)S(1)}, u32[]{:S(2)}, u32[]{:S(2)}) collective-permute-start(bf16[144,640]{1,0:T(8,128)(2,1)S(1)} %fusion.20), channel_id=1, source_target_pairs={{0,4},{4,8},{8,12},{12,0},{1,5},{5,9},{9,13},{13,1},{2,6},{6,10},{... | collective-permute-start | bytes 552968 | tf_op jit(solution)/shard_map/ppermute | solution.py:26
  114.2 12.4 %collective-permute-start.26 = (bf16[2,160,288]{2,1,0:T(8,128)(2,1)S(1)}, bf16[2,160,288]{2,1,0:T(8,128)(2,1)S(1)}, u32[]{:S(2)}, u32[]{:S(2)}) collective-permute-start(bf16[2,160,288]{2,1,0:T(8,128)(2,1)S(1)} %pad_maximum_fusion.12), channel_id=1, source_target_pairs={{0,2},{1,3},{2,0},{3,1},{4,6},{5,7},{6,4},{7,5},{8,10},{9,11},{10,... | collective-permute-start | bytes 552968 | tf_op jit(solution)/shard_map/ppermute | solution.py:43
  116.7 9.9 %collective-permute-start.27 = (bf16[2,160,288]{2,1,0:T(8,128)(2,1)S(1)}, bf16[2,160,288]{2,1,0:T(8,128)(2,1)S(1)}, u32[]{:S(2)}, u32[]{:S(2)}) collective-permute-start(bf16[2,160,288]{2,1,0:T(8,128)(2,1)S(1)} %pad_maximum_fusion.13), channel_id=1, source_target_pairs={{0,3},{1,2},{2,1},{3,0},{4,7},{5,6},{6,5},{7,4},{8,11},{9,10},{10,... | collective-permute-start | bytes 552968 | tf_op jit(solution)/shard_map/ppermute | solution.py:43
  121.7 15.4 %all-to-all-start.3 = ((bf16[8,18,640]{2,1,0:T(8,128)(2,1)}), bf16[8,18,640]{2,1,0:T(8,128)(2,1)S(1)}, u32[]{:S(2)}, u32[]{:S(2)}) async-start(bf16[8,18,640]{2,1,0:T(8,128)(2,1)} %reshape.153), calls=%async_computation.3 | async-start | bytes 491520 | tf_op jit(solution)/shard_map/all_to_all | solution.py:18
  (28 other events, 190.2 us)

commit v4 on v1

--- a/solution.py
+++ b/solution.py
@@ -174,10 +174,11 @@
 
     keep = pick(xl, stacked)
     give = pick(1 - xl, lax.dynamic_slice_in_dim(stacked, c * 160, 160, 0))
+    scalars = jnp.concatenate([jnp.exp(log_scale), bias])
     own = embed([sent[0], mp_shift(sent[1], 0, 1), mp_shift(sent[2], 1, 0), mp_shift(sent[3], 1, 1)], xh, c)
     r = lax.rsqrt(jnp.sum(own * own, axis=2, keepdims=True) + 1e-06)
     z = (own * r).astype(BF)
-    z, keep, give = lax.optimization_barrier((z, keep, give))
+    z, keep, give, scalars = lax.optimization_barrier((z, keep, give, scalars))
     z_img, z_txt = z[0], z[1]
     r_img, r_txt = r[0], r[1]
 
@@ -195,7 +196,6 @@
     give, img = lax.optimization_barrier((give, img))
     come = lax.ppermute(give, "xl", [(0, 1), (1, 0)])
     place = (xl * 4 + y) * 2 + xh
-    scalars = jnp.concatenate([jnp.exp(log_scale), bias])
     t_oth, t_own, g_img = block_grads(scalars, place.astype(jnp.int32).reshape(1), img, txt_oth + txt_own)
     t_oth, come = lax.optimization_barrier((t_oth, come))
     t_got = swap_core(t_oth)

time: 138 us -> 137 us (level)
    ppermute x6, waiting for transfers between devices: 3.94 us -> 1.62 us  [mp_shift(): return lax.ppermute(x, MP, pairs)]
where the time goes in v4:
time: 137 us; the launch traced here: 135 us
  starting transfers between devices  61.1 us (45%)
  waiting for transfers between devices  45.2 us (33%)
  Pallas kernels  10.8 us (8%)
  matrix products  6.3 us (5%)
  local copies, waits for them, and re-layouts  5.3 us (4%)
  other arithmetic  3.97 us (3%)
  between operations  2.73 us (2%)
    ppermute x15, starting transfers between devices, shift(): return lax.ppermute(x, axis, [(i, (i + step) % size) for i in range(size)])  28.5 us
    ppermute x15, waiting for transfers between devices, shift(): return lax.ppermute(x, axis, [(i, (i + step) % size) for i in range(size)])  27.6 us
    all_to_all x4, starting transfers between devices, a2a(): return lax.all_to_all(x, axes, 0, 0, tiled=True)  24.1 us
    all_to_all x4, waiting for transfers between devices, a2a(): return lax.all_to_all(x, axes, 0, 0, tiled=True)  16 us
    pallas_call x1, Pallas kernels, block_grads(): pl.pallas_call(block_kernel, out_shape=[jax.ShapeDtypeStruct((320, 1152),...  7.66 us
    ppermute x6, starting transfers between devices, mp_shift(): return lax.ppermute(x, MP, pairs)  5.38 us
    pallas_call x1, Pallas kernels, project(): pl.pallas_call(project_kernel, out_shape=[jax.ShapeDtypeStruct((200, 128)...  3.1 us
  transfers between devices with their start and end apart: 36, of which 13 were waited for; matrix products, arithmetic and copies ran while one was open for 6% of the time, Pallas kernels for 6%

profile of v4, /device:TPU:2, one launch (start us, length us, event | category | flops | bytes accessed | tf_op | source)
XLA Modules:
  0.0 135.4 jit_solution(8868114940023030418)
XLA Ops:
  0.7 3.1 %shard_map.93 = (f32[200,128]{1,0:T(8,128)}, f32[200,128]{1,0:T(8,128)}, f32[200,128]{1,0:T(8,128)}, f32[200,128]{1,0:T(8,128)}) custom-call(bf16[160,1152]{1,0:T(8,128)(2,1)} %refs_0_.1, bf16[288,1152]{1,0:T(8,128)(2,1)} %bitcast.105, bf16[160,1152]{1,0:T(8,128)(2,1)} %refs_2_.1, bf16[288,1152]{1,0:T(8,128)(2,1)} %bitcast.106), custom_call_target="tpu_custom_call" | custom-call | flops 220000000 | bytes 2500000 | tf_op jit(solution)/shard_map/pallas_call | solution.py:69
  3.9 2.2 %collective-permute-start.1 = (f32[200,128]{1,0:T(8,128)}, f32[200,128]{1,0:T(8,128)S(1)}, u32[]{:S(2)}, u32[]{:S(2)}) collective-permute-start(f32[200,128]{1,0:T(8,128)} %get-tuple-element.30), channel_id=1, source_target_pairs={{0,2},{1,3},{2,0},{3,1},{4,6},{5,7},{6,4},{7,5},{8,10},{9,11},{10,... | collective-permute-start | bytes 307208 | tf_op jit(solution)/shard_map/ppermute | solution.py:43
  6.1 1.2 collective-permute-start.2
  8.7 1.6 %fusion.9 = bf16[320,576]{1,0:T(8,128)(2,1)} fusion(bf16[320,1152]{1,0:T(8,128)(2,1)S(1)} %constant_dynamic-update-slice_fusion, s32[576]{0:T(1024)S(1)} %get-tuple-element.134), kind=kOutput, calls=%fused_computation.14 | convolution fusion | flops 425521152 | bytes 1108224 | tf_op jit(solution)/shard_map/dot_general | solution.py:173
  11.6 1.2 collective-permute-done.2
  13.5 1.3 broadcast_in_dim.7
  14.8 7.2 %all-to-all-start = ((bf16[16,40,1152]{2,1,0:T(8,128)(2,1)}), bf16[16,40,1152]{2,1,0:T(8,128)(2,1)S(1)}, u32[]{:S(2)}, u32[]{:S(2)}) async-start(bf16[16,40,1152]{2,1,0:T(8,128)(2,1)} %broadcast_in_dim.7), calls=%async_computation | async-start | bytes 2949120 | tf_op jit(solution)/shard_map/all_to_all | solution.py:18
  22.0 1.9 %collective-permute-start.3 = (bf16[40,1152]{1,0:T(8,128)(2,1)S(1)}, bf16[40,1152]{1,0:T(8,128)(2,1)S(1)}, u32[]{:S(2)}, u32[]{:S(2)}) collective-permute-start(bf16[40,1152]{1,0:T(8,128)(2,1)S(1)} %get-tuple-element.37.refs_8_), channel_id=1, source_target_pairs={{0,32},{32,64},{64,96},{96,128},{128,160},{160,192},{192,224},{224... | collective-permute-start | bytes 276488 | tf_op jit(solution)/shard_map/ppermute | solution.py:26
  24.0 4.0 %collective-permute-start.6 = (bf16[40,1152]{1,0:T(8,128)(2,1)S(1)}, bf16[40,1152]{1,0:T(8,128)(2,1)S(1)}, u32[]{:S(2)}, u32[]{:S(2)}) collective-permute-start(bf16[40,1152]{1,0:T(8,128)(2,1)S(1)} %get-tuple-element.37.refs_8_), channel_id=1, source_target_pairs={{0,224},{32,0},{64,32},{96,64},{128,96},{160,128},{192,160},{224,1... | collective-permute-start | bytes 276488 | tf_op jit(solution)/shard_map/ppermute | solution.py:26
  28.0 2.5 %collective-permute-done.3.refs_9_ = bf16[40,1152]{1,0:T(8,128)(2,1)S(1)} collective-permute-done((bf16[40,1152]{1,0:T(8,128)(2,1)S(1)}, bf16[40,1152]{1,0:T(8,128)(2,1)S(1)}, u32[]{:S(2)}, u32[]{:S(2)}) %collective-permute-start.3) | collective-permute-done | bytes 92192 | tf_op jit(solution)/shard_map/ppermute | solution.py:26
  30.5 3.3 %collective-permute-start.7 = (bf16[40,1152]{1,0:T(8,128)(2,1)S(1)}, bf16[40,1152]{1,0:T(8,128)(2,1)S(1)}, u32[]{:S(2)}, u32[]{:S(2)}) collective-permute-start(bf16[40,1152]{1,0:T(8,128)(2,1)S(1)} %collective-permute-done.6.refs_15_), channel_id=1, source_target_pairs={{0,224},{32,0},{64,32},{96,64},{128,96},{160,128},{192,160},{224,1... | collective-permute-start | bytes 276488 | tf_op jit(solution)/shard_map/ppermute | solution.py:26
  33.8 4.5 %collective-permute-start.13 = (bf16[40,1152]{1,0:T(8,128)(2,1)S(1)}, bf16[40,1152]{1,0:T(8,128)(2,1)S(1)}, u32[]{:S(2)}, u32[]{:S(2)}) collective-permute-start(bf16[40,1152]{1,0:T(8,128)(2,1)S(1)} %get-tuple-element.37.refs_8_), channel_id=1, source_target_pairs={{0,128},{32,160},{64,192},{96,224},{128,0},{160,32},{192,64},{224,... | collective-permute-start | bytes 276488 | tf_op jit(solution)/shard_map/ppermute | solution.py:26
  38.3 3.2 %collective-permute-start.8 = (bf16[40,1152]{1,0:T(8,128)(2,1)S(1)}, bf16[40,1152]{1,0:T(8,128)(2,1)S(1)}, u32[]{:S(2)}, u32[]{:S(2)}) collective-permute-start(bf16[40,1152]{1,0:T(8,128)(2,1)S(1)} %collective-permute-done.7.refs_14_), channel_id=1, source_target_pairs={{0,224},{32,0},{64,32},{96,64},{128,96},{160,128},{192,160},{224,1... | collective-permute-start | bytes 276488 | tf_op jit(solution)/shard_map/ppermute | solution.py:26
  42.0 1.8 %collective-permute-done.13.refs_12_ = bf16[40,1152]{1,0:T(8,128)(2,1)S(1)} collective-permute-done((bf16[40,1152]{1,0:T(8,128)(2,1)S(1)}, bf16[40,1152]{1,0:T(8,128)(2,1)S(1)}, u32[]{:S(2)}, u32[]{:S(2)}) %collective-permute-start.13) | collective-permute-done | bytes 92192 | tf_op jit(solution)/shard_map/ppermute | solution.py:26
  46.0 1.1 collective-permute-start.18
  47.8 7.7 %shard_map.94 = (bf16[320,1152]{1,0:T(8,128)(2,1)}, bf16[320,1152]{1,0:T(8,128)(2,1)}, bf16[640,1152]{1,0:T(8,128)(2,1)}) custom-call(f32[2]{0:T(128)} %pad_maximum_fusion.20.scalars, s32[1]{0:T(128)} %bitcast.4.place, bf16[640,1152]{1,0:T(8,128)(2,1)} %bitcast.104, bf16[40,1152]{1,0:T(8,128)(2,1)} %copy-done.16, bf16[40,1152]{1,0:T(8,128)(2,1)} %copy-done.17, ...), custom_call_target="tpu_custom_call" | custom-call | flops 2900000000 | bytes 8000000 | tf_op jit(solution)/shard_map/pallas_call | solution.py:138
  55.7 7.5 %all-to-all-start.1 = ((bf16[16,40,1152]{2,1,0:T(8,128)(2,1)}), bf16[16,40,1152]{2,1,0:T(8,128)(2,1)S(1)}, u32[]{:S(2)}, u32[]{:S(2)}) async-start(bf16[16,40,1152]{2,1,0:T(8,128)(2,1)} %bitcast.103), calls=%async_computation.1 | async-start | bytes 2949120 | tf_op jit(solution)/shard_map/all_to_all | solution.py:18
  63.5 3.7 %collective-permute-start.20 = (bf16[80,1152]{1,0:T(8,128)(2,1)S(1)}, bf16[80,1152]{1,0:T(8,128)(2,1)S(1)}, u32[]{:S(2)}, u32[]{:S(2)}) collective-permute-start(bf16[80,1152]{1,0:T(8,128)(2,1)S(1)} %pad_maximum_fusion.15), channel_id=1, source_target_pairs={{0,192},{32,224},{64,0},{96,32},{128,64},{160,96},{192,128},{224,1... | collective-permute-start | bytes 552968 | tf_op jit(solution)/shard_map/ppermute | solution.py:26
  67.2 8.5 %collective-permute-done.20 = bf16[80,1152]{1,0:T(8,128)(2,1)S(1)} collective-permute-done((bf16[80,1152]{1,0:T(8,128)(2,1)S(1)}, bf16[80,1152]{1,0:T(8,128)(2,1)S(1)}, u32[]{:S(2)}, u32[]{:S(2)}) %collective-permute-start.20) | collective-permute-done | bytes 184352 | tf_op jit(solution)/shard_map/ppermute | solution.py:26
  75.7 3.8 %collective-permute-done.21 = bf16[80,1152]{1,0:T(8,128)(2,1)S(1)} collective-permute-done((bf16[80,1152]{1,0:T(8,128)(2,1)S(1)}, bf16[80,1152]{1,0:T(8,128)(2,1)S(1)}, u32[]{:S(2)}, u32[]{:S(2)}) %collective-permute-start.21) | collective-permute-done | bytes 184352 | tf_op jit(solution)/shard_map/ppermute | solution.py:26
  79.7 1.5 %collective-permute-start.23 = (bf16[40,1152]{1,0:T(8,128)(2,1)S(1)}, bf16[40,1152]{1,0:T(8,128)(2,1)S(1)}, u32[]{:S(2)}, u32[]{:S(2)}) collective-permute-start(bf16[40,1152]{1,0:T(8,128)(2,1)S(1)} %get-tuple-element.53), channel_id=1, source_target_pairs={{0,32},{32,64},{64,96},{96,128},{128,160},{160,192},{192,224},{224... | collective-permute-start | bytes 276488 | tf_op jit(solution)/shard_map/ppermute | solution.py:26
  81.2 2.6 %collective-permute-start.24 = (bf16[40,1152]{1,0:T(8,128)(2,1)S(1)}, bf16[40,1152]{1,0:T(8,128)(2,1)S(1)}, u32[]{:S(2)}, u32[]{:S(2)}) collective-permute-start(bf16[40,1152]{1,0:T(8,128)(2,1)S(1)} %get-tuple-element.56), channel_id=1, source_target_pairs={{0,224},{32,0},{64,32},{96,64},{128,96},{160,128},{192,160},{224,1... | collective-permute-start | bytes 276488 | tf_op jit(solution)/shard_map/ppermute | solution.py:26
  83.9 4.2 %collective-permute-done.22 = bf16[40,1152]{1,0:T(8,128)(2,1)S(1)} collective-permute-done((bf16[40,1152]{1,0:T(8,128)(2,1)S(1)}, bf16[40,1152]{1,0:T(8,128)(2,1)S(1)}, u32[]{:S(2)}, u32[]{:S(2)}) %collective-permute-start.22) | collective-permute-done | bytes 92192 | tf_op jit(solution)/shard_map/ppermute | solution.py:26
  90.6 4.8 %all-to-all-start.2 = ((bf16[8,200,128]{2,1,0:T(8,128)(2,1)}), bf16[8,200,128]{2,1,0:T(8,128)(2,1)S(1)}, u32[]{:S(2)}, u32[]{:S(2)}) async-start(bf16[8,200,128]{2,1,0:T(8,128)(2,1)} %bitcast.31), calls=%async_computation.2 | async-start | bytes 819200 | tf_op jit(solution)/shard_map/all_to_all | solution.py:18
  95.4 7.0 %all-to-all-done.2 = bf16[8,200,128]{2,1,0:T(8,128)(2,1)S(1)} async-done(((bf16[8,200,128]{2,1,0:T(8,128)(2,1)}), bf16[8,200,128]{2,1,0:T(8,128)(2,1)S(1)}, u32[]{:S(2)}, u32[]{:S(2)}) %all-to-all-start.2) | async-done | bytes 409632 | tf_op jit(solution)/shard_map/all_to_all | solution.py:18
  104.0 1.6 %collective-permute-start.30 = (bf16[144,640]{1,0:T(8,128)(2,1)S(1)}, bf16[144,640]{1,0:T(8,128)(2,1)S(1)}, u32[]{:S(2)}, u32[]{:S(2)}) collective-permute-start(bf16[144,640]{1,0:T(8,128)(2,1)S(1)} %get-tuple-element.55), channel_id=1, source_target_pairs={{0,4},{4,8},{8,12},{12,0},{1,5},{5,9},{9,13},{13,1},{2,6},{6,10},{... | collective-permute-start | bytes 552968 | tf_op jit(solution)/shard_map/ppermute | solution.py:26
  105.6 1.8 %collective-permute-start.29 = (bf16[144,640]{1,0:T(8,128)(2,1)S(1)}, bf16[144,640]{1,0:T(8,128)(2,1)S(1)}, u32[]{:S(2)}, u32[]{:S(2)}) collective-permute-start(bf16[144,640]{1,0:T(8,128)(2,1)S(1)} %get-tuple-element.54), channel_id=1, source_target_pairs={{0,12},{4,0},{8,4},{12,8},{1,13},{5,1},{9,5},{13,9},{2,14},{6,2},{... | collective-permute-start | bytes 552968 | tf_op jit(solution)/shard_map/ppermute | solution.py:26
  109.0 2.4 %collective-permute-done.30 = bf16[144,640]{1,0:T(8,128)(2,1)S(1)} collective-permute-done((bf16[144,640]{1,0:T(8,128)(2,1)S(1)}, bf16[144,640]{1,0:T(8,128)(2,1)S(1)}, u32[]{:S(2)}, u32[]{:S(2)}) %collective-permute-start.30) | collective-permute-done | bytes 184352 | tf_op jit(solution)/shard_map/ppermute | solution.py:26
  111.8 1.7 %collective-permute-start.26 = (bf16[2,160,288]{2,1,0:T(8,128)(2,1)S(1)}, bf16[2,160,288]{2,1,0:T(8,128)(2,1)S(1)}, u32[]{:S(2)}, u32[]{:S(2)}) collective-permute-start(bf16[2,160,288]{2,1,0:T(8,128)(2,1)S(1)} %pad_maximum_fusion.12), channel_id=1, source_target_pairs={{0,2},{1,3},{2,0},{3,1},{4,6},{5,7},{6,4},{7,5},{8,10},{9,11},{10,... | collective-permute-start | bytes 552968 | tf_op jit(solution)/shard_map/ppermute | solution.py:43
  115.0 3.2 %collective-permute-done.31 = bf16[144,640]{1,0:T(8,128)(2,1)S(1)} collective-permute-done((bf16[144,640]{1,0:T(8,128)(2,1)S(1)}, bf16[144,640]{1,0:T(8,128)(2,1)S(1)}, u32[]{:S(2)}, u32[]{:S(2)}) %collective-permute-start.31) | collective-permute-done | bytes 184352 | tf_op jit(solution)/shard_map/ppermute | solution.py:26
  119.1 4.7 %all-to-all-start.3 = ((bf16[8,18,640]{2,1,0:T(8,128)(2,1)}), bf16[8,18,640]{2,1,0:T(8,128)(2,1)S(1)}, u32[]{:S(2)}, u32[]{:S(2)}) async-start(bf16[8,18,640]{2,1,0:T(8,128)(2,1)} %reshape.153), calls=%async_computation.3 | async-start | bytes 491520 | tf_op jit(solution)/shard_map/all_to_all | solution.py:18
  125.1 9.0 %all-to-all-done.3 = bf16[8,18,640]{2,1,0:T(8,128)(2,1)S(1)} async-done(((bf16[8,18,640]{2,1,0:T(8,128)(2,1)}), bf16[8,18,640]{2,1,0:T(8,128)(2,1)S(1)}, u32[]{:S(2)}, u32[]{:S(2)}) %all-to-all-start.3) | async-done | bytes 184352 | tf_op jit(solution)/shard_map/all_to_all | solution.py:18
  (161 shorter events, 17.2 us)
Async XLA Ops:
  3.8 7.9 %collective-permute-start = (f32[200,128]{1,0:T(8,128)}, f32[200,128]{1,0:T(8,128)S(1)}, u32[]{:S(2)}, u32[]{:S(2)}) collective-permute-start(f32[200,128]{1,0:T(8,128)} %get-tuple-element.29), channel_id=1, source_target_pairs={{0,1},{1,0},{2,3},{3,2},{4,5},{5,4},{6,7},{7,6},{8,9},{9,8},{10,11... | collective-permute-start | bytes 307208 | tf_op jit(solution)/shard_map/ppermute | solution.py:43
  3.9 7.8 %collective-permute-start.1 = (f32[200,128]{1,0:T(8,128)}, f32[200,128]{1,0:T(8,128)S(1)}, u32[]{:S(2)}, u32[]{:S(2)}) collective-permute-start(f32[200,128]{1,0:T(8,128)} %get-tuple-element.30), channel_id=1, source_target_pairs={{0,2},{1,3},{2,0},{3,1},{4,6},{5,7},{6,4},{7,5},{8,10},{9,11},{10,... | collective-permute-start | bytes 307208 | tf_op jit(solution)/shard_map/ppermute | solution.py:43
  6.1 6.8 %collective-permute-start.2 = (f32[200,128]{1,0:T(8,128)}, f32[200,128]{1,0:T(8,128)S(1)}, u32[]{:S(2)}, u32[]{:S(2)}) collective-permute-start(f32[200,128]{1,0:T(8,128)} %get-tuple-element.31), channel_id=1, source_target_pairs={{0,3},{1,2},{2,1},{3,0},{4,7},{5,6},{6,5},{7,4},{8,11},{9,10},{10,... | collective-permute-start | bytes 307208 | tf_op jit(solution)/shard_map/ppermute | solution.py:43
  14.8 30.2 %all-to-all-start = ((bf16[16,40,1152]{2,1,0:T(8,128)(2,1)}), bf16[16,40,1152]{2,1,0:T(8,128)(2,1)S(1)}, u32[]{:S(2)}, u32[]{:S(2)}) async-start(bf16[16,40,1152]{2,1,0:T(8,128)(2,1)} %broadcast_in_dim.7), calls=%async_computation | async-start | bytes 2949120 | tf_op jit(solution)/shard_map/all_to_all | solution.py:18
  22.0 8.4 %collective-permute-start.3 = (bf16[40,1152]{1,0:T(8,128)(2,1)S(1)}, bf16[40,1152]{1,0:T(8,128)(2,1)S(1)}, u32[]{:S(2)}, u32[]{:S(2)}) collective-permute-start(bf16[40,1152]{1,0:T(8,128)(2,1)S(1)} %get-tuple-element.37.refs_8_), channel_id=1, source_target_pairs={{0,32},{32,64},{64,96},{96,128},{128,160},{160,192},{192,224},{224... | collective-permute-start | bytes 276488 | tf_op jit(solution)/shard_map/ppermute | solution.py:26
  24.0 6.5 %collective-permute-start.6 = (bf16[40,1152]{1,0:T(8,128)(2,1)S(1)}, bf16[40,1152]{1,0:T(8,128)(2,1)S(1)}, u32[]{:S(2)}, u32[]{:S(2)}) collective-permute-start(bf16[40,1152]{1,0:T(8,128)(2,1)S(1)} %get-tuple-element.37.refs_8_), channel_id=1, source_target_pairs={{0,224},{32,0},{64,32},{96,64},{128,96},{160,128},{192,160},{224,1... | collective-permute-start | bytes 276488 | tf_op jit(solution)/shard_map/ppermute | solution.py:26
  30.5 7.8 %collective-permute-start.4 = (bf16[40,1152]{1,0:T(8,128)(2,1)S(1)}, bf16[40,1152]{1,0:T(8,128)(2,1)S(1)}, u32[]{:S(2)}, u32[]{:S(2)}) collective-permute-start(bf16[40,1152]{1,0:T(8,128)(2,1)S(1)} %collective-permute-done.3.refs_9_), channel_id=1, source_target_pairs={{0,32},{32,64},{64,96},{96,128},{128,160},{160,192},{192,224},{224... | collective-permute-start | bytes 276488 | tf_op jit(solution)/shard_map/ppermute | solution.py:26
  30.5 7.8 %collective-permute-start.7 = (bf16[40,1152]{1,0:T(8,128)(2,1)S(1)}, bf16[40,1152]{1,0:T(8,128)(2,1)S(1)}, u32[]{:S(2)}, u32[]{:S(2)}) collective-permute-start(bf16[40,1152]{1,0:T(8,128)(2,1)S(1)} %collective-permute-done.6.refs_15_), channel_id=1, source_target_pairs={{0,224},{32,0},{64,32},{96,64},{128,96},{160,128},{192,160},{224,1... | collective-permute-start | bytes 276488 | tf_op jit(solution)/shard_map/ppermute | solution.py:26
  33.8 10.1 %collective-permute-start.13 = (bf16[40,1152]{1,0:T(8,128)(2,1)S(1)}, bf16[40,1152]{1,0:T(8,128)(2,1)S(1)}, u32[]{:S(2)}, u32[]{:S(2)}) collective-permute-start(bf16[40,1152]{1,0:T(8,128)(2,1)S(1)} %get-tuple-element.37.refs_8_), channel_id=1, source_target_pairs={{0,128},{32,160},{64,192},{96,224},{128,0},{160,32},{192,64},{224,... | collective-permute-start | bytes 276488 | tf_op jit(solution)/shard_map/ppermute | solution.py:26
  38.2 6.3 %collective-permute-start.5 = (bf16[40,1152]{1,0:T(8,128)(2,1)S(1)}, bf16[40,1152]{1,0:T(8,128)(2,1)S(1)}, u32[]{:S(2)}, u32[]{:S(2)}) collective-permute-start(bf16[40,1152]{1,0:T(8,128)(2,1)S(1)} %collective-permute-done.4.refs_10_), channel_id=1, source_target_pairs={{0,32},{32,64},{64,96},{96,128},{128,160},{160,192},{192,224},{224... | collective-permute-start | bytes 276488 | tf_op jit(solution)/shard_map/ppermute | solution.py:26
  38.3 6.2 %collective-permute-start.8 = (bf16[40,1152]{1,0:T(8,128)(2,1)S(1)}, bf16[40,1152]{1,0:T(8,128)(2,1)S(1)}, u32[]{:S(2)}, u32[]{:S(2)}) collective-permute-start(bf16[40,1152]{1,0:T(8,128)(2,1)S(1)} %collective-permute-done.7.refs_14_), channel_id=1, source_target_pairs={{0,224},{32,0},{64,32},{96,64},{128,96},{160,128},{192,160},{224,1... | collective-permute-start | bytes 276488 | tf_op jit(solution)/shard_map/ppermute | solution.py:26
  41.5 3.5 %collective-permute-start.9 = (bf16[40,1152]{1,0:T(8,128)(2,1)S(1)}, bf16[40,1152]{1,0:T(8,128)(2,1)S(1)}, u32[]{:S(2)}, u32[]{:S(2)}) collective-permute-start(bf16[40,1152]{1,0:T(8,128)(2,1)S(1)} %get-tuple-element.37.refs_8_), channel_id=1, source_target_pairs={{0,1},{1,0},{2,3},{3,2},{4,5},{5,4},{6,7},{7,6},{8,9},{9,8},{10,11... | collective-permute-start | bytes 276488 | tf_op jit(solution)/shard_map/ppermute | solution.py:22
  41.5 3.9 %collective-permute-start.10 = (bf16[40,1152]{1,0:T(8,128)(2,1)S(1)}, bf16[40,1152]{1,0:T(8,128)(2,1)S(1)}, u32[]{:S(2)}, u32[]{:S(2)}) collective-permute-start(bf16[40,1152]{1,0:T(8,128)(2,1)S(1)} %collective-permute-done.3.refs_9_), channel_id=1, source_target_pairs={{0,1},{1,0},{2,3},{3,2},{4,5},{5,4},{6,7},{7,6},{8,9},{9,8},{10,11... | collective-permute-start | bytes 276488 | tf_op jit(solution)/shard_map/ppermute | solution.py:22
  44.5 2.5 %collective-permute-start.11 = (bf16[40,1152]{1,0:T(8,128)(2,1)S(1)}, bf16[40,1152]{1,0:T(8,128)(2,1)S(1)}, u32[]{:S(2)}, u32[]{:S(2)}) collective-permute-start(bf16[40,1152]{1,0:T(8,128)(2,1)S(1)} %collective-permute-done.4.refs_10_), channel_id=1, source_target_pairs={{0,1},{1,0},{2,3},{3,2},{4,5},{5,4},{6,7},{7,6},{8,9},{9,8},{10,11... | collective-permute-start | bytes 276488 | tf_op jit(solution)/shard_map/ppermute | solution.py:22
  45.1 2.0 %collective-permute-start.16 = (bf16[40,1152]{1,0:T(8,128)(2,1)S(1)}, bf16[40,1152]{1,0:T(8,128)(2,1)S(1)}, u32[]{:S(2)}, u32[]{:S(2)}) collective-permute-start(bf16[40,1152]{1,0:T(8,128)(2,1)S(1)} %collective-permute-done.7.refs_14_), channel_id=1, source_target_pairs={{0,1},{1,0},{2,3},{3,2},{4,5},{5,4},{6,7},{7,6},{8,9},{9,8},{10,11... | collective-permute-start | bytes 276488 | tf_op jit(solution)/shard_map/ppermute | solution.py:22
  46.0 9.5 %collective-permute-start.18 = (bf16[160,576]{1,0:T(8,128)(2,1)S(1)}, bf16[160,576]{1,0:T(8,128)(2,1)S(1)}, u32[]{:S(2)}, u32[]{:S(2)}) collective-permute-start(bf16[160,576]{1,0:T(8,128)(2,1)S(1)} %fusion.10), channel_id=1, source_target_pairs={{0,16},{16,0},{1,17},{17,1},{2,18},{18,2},{3,19},{19,3},{4,20},{20... | collective-permute-start | bytes 552968 | tf_op jit(solution)/shard_map/ppermute | solution.py:197
  55.5 7.7 %collective-permute-start.19 = (bf16[320,1152]{1,0:T(8,128)(2,1)}, bf16[320,1152]{1,0:T(8,128)(2,1)S(1)}, u32[]{:S(2)}, u32[]{:S(2)}) collective-permute-start(bf16[320,1152]{1,0:T(8,128)(2,1)} %get-tuple-element.47), channel_id=1, source_target_pairs={{0,1},{1,0},{2,3},{3,2},{4,5},{5,4},{6,7},{7,6},{8,9},{9,8},{10,11... | collective-permute-start | bytes 2211848 | tf_op jit(solution)/shard_map/ppermute | solution.py:22
  55.7 33.1 %all-to-all-start.1 = ((bf16[16,40,1152]{2,1,0:T(8,128)(2,1)}), bf16[16,40,1152]{2,1,0:T(8,128)(2,1)S(1)}, u32[]{:S(2)}, u32[]{:S(2)}) async-start(bf16[16,40,1152]{2,1,0:T(8,128)(2,1)} %bitcast.103), calls=%async_computation.1 | async-start | bytes 2949120 | tf_op jit(solution)/shard_map/all_to_all | solution.py:18
  63.2 4.0 %collective-permute-start.28 = (bf16[160,576]{1,0:T(8,128)(2,1)S(1)}, bf16[160,576]{1,0:T(8,128)(2,1)S(1)}, u32[]{:S(2)}, u32[]{:S(2)}) collective-permute-start(bf16[160,576]{1,0:T(8,128)(2,1)S(1)} %collective-permute-done.18), channel_id=1, source_target_pairs={{0,1},{1,0},{2,3},{3,2},{4,5},{5,4},{6,7},{7,6},{8,9},{9,8},{10,11... | collective-permute-start | bytes 552968 | tf_op jit(solution)/shard_map/ppermute | solution.py:22
  63.5 12.2 %collective-permute-start.20 = (bf16[80,1152]{1,0:T(8,128)(2,1)S(1)}, bf16[80,1152]{1,0:T(8,128)(2,1)S(1)}, u32[]{:S(2)}, u32[]{:S(2)}) collective-permute-start(bf16[80,1152]{1,0:T(8,128)(2,1)S(1)} %pad_maximum_fusion.15), channel_id=1, source_target_pairs={{0,192},{32,224},{64,0},{96,32},{128,64},{160,96},{192,128},{224,1... | collective-permute-start | bytes 552968 | tf_op jit(solution)/shard_map/ppermute | solution.py:26
  67.2 12.3 %collective-permute-start.21 = (bf16[80,1152]{1,0:T(8,128)(2,1)S(1)}, bf16[80,1152]{1,0:T(8,128)(2,1)S(1)}, u32[]{:S(2)}, u32[]{:S(2)}) collective-permute-start(bf16[80,1152]{1,0:T(8,128)(2,1)S(1)} %concatenate.97), channel_id=1, source_target_pairs={{0,64},{32,96},{64,128},{96,160},{128,192},{160,224},{192,0},{224,... | collective-permute-start | bytes 552968 | tf_op jit(solution)/shard_map/ppermute | solution.py:26
  79.6 8.6 %collective-permute-start.22 = (bf16[40,1152]{1,0:T(8,128)(2,1)S(1)}, bf16[40,1152]{1,0:T(8,128)(2,1)S(1)}, u32[]{:S(2)}, u32[]{:S(2)}) collective-permute-start(bf16[40,1152]{1,0:T(8,128)(2,1)S(1)} %get-tuple-element.52), channel_id=1, source_target_pairs={{0,64},{32,96},{64,128},{96,160},{128,192},{160,224},{192,0},{224,... | collective-permute-start | bytes 276488 | tf_op jit(solution)/shard_map/ppermute | solution.py:26
  79.7 9.1 %collective-permute-start.23 = (bf16[40,1152]{1,0:T(8,128)(2,1)S(1)}, bf16[40,1152]{1,0:T(8,128)(2,1)S(1)}, u32[]{:S(2)}, u32[]{:S(2)}) collective-permute-start(bf16[40,1152]{1,0:T(8,128)(2,1)S(1)} %get-tuple-element.53), channel_id=1, source_target_pairs={{0,32},{32,64},{64,96},{96,128},{128,160},{160,192},{192,224},{224... | collective-permute-start | bytes 276488 | tf_op jit(solution)/shard_map/ppermute | solution.py:26
  81.2 7.6 %collective-permute-start.24 = (bf16[40,1152]{1,0:T(8,128)(2,1)S(1)}, bf16[40,1152]{1,0:T(8,128)(2,1)S(1)}, u32[]{:S(2)}, u32[]{:S(2)}) collective-permute-start(bf16[40,1152]{1,0:T(8,128)(2,1)S(1)} %get-tuple-element.56), channel_id=1, source_target_pairs={{0,224},{32,0},{64,32},{96,64},{128,96},{160,128},{192,160},{224,1... | collective-permute-start | bytes 276488 | tf_op jit(solution)/shard_map/ppermute | solution.py:26
  90.6 11.8 %all-to-all-start.2 = ((bf16[8,200,128]{2,1,0:T(8,128)(2,1)}), bf16[8,200,128]{2,1,0:T(8,128)(2,1)S(1)}, u32[]{:S(2)}, u32[]{:S(2)}) async-start(bf16[8,200,128]{2,1,0:T(8,128)(2,1)} %bitcast.31), calls=%async_computation.2 | async-start | bytes 819200 | tf_op jit(solution)/shard_map/all_to_all | solution.py:18
  104.0 7.3 %collective-permute-start.30 = (bf16[144,640]{1,0:T(8,128)(2,1)S(1)}, bf16[144,640]{1,0:T(8,128)(2,1)S(1)}, u32[]{:S(2)}, u32[]{:S(2)}) collective-permute-start(bf16[144,640]{1,0:T(8,128)(2,1)S(1)} %get-tuple-element.55), channel_id=1, source_target_pairs={{0,4},{4,8},{8,12},{12,0},{1,5},{5,9},{9,13},{13,1},{2,6},{6,10},{... | collective-permute-start | bytes 552968 | tf_op jit(solution)/shard_map/ppermute | solution.py:26
  105.6 9.4 %collective-permute-start.29 = (bf16[144,640]{1,0:T(8,128)(2,1)S(1)}, bf16[144,640]{1,0:T(8,128)(2,1)S(1)}, u32[]{:S(2)}, u32[]{:S(2)}) collective-permute-start(bf16[144,640]{1,0:T(8,128)(2,1)S(1)} %get-tuple-element.54), channel_id=1, source_target_pairs={{0,12},{4,0},{8,4},{12,8},{1,13},{5,1},{9,5},{13,9},{2,14},{6,2},{... | collective-permute-start | bytes 552968 | tf_op jit(solution)/shard_map/ppermute | solution.py:26
  108.2 15.6 %collective-permute-start.25 = (bf16[2,160,288]{2,1,0:T(8,128)(2,1)S(1)}, bf16[2,160,288]{2,1,0:T(8,128)(2,1)S(1)}, u32[]{:S(2)}, u32[]{:S(2)}) collective-permute-start(bf16[2,160,288]{2,1,0:T(8,128)(2,1)S(1)} %pad_maximum_fusion.11), channel_id=1, source_target_pairs={{0,1},{1,0},{2,3},{3,2},{4,5},{5,4},{6,7},{7,6},{8,9},{9,8},{10,11... | collective-permute-start | bytes 552968 | tf_op jit(solution)/shard_map/ppermute | solution.py:43
  111.4 6.8 %collective-permute-start.31 = (bf16[144,640]{1,0:T(8,128)(2,1)S(1)}, bf16[144,640]{1,0:T(8,128)(2,1)S(1)}, u32[]{:S(2)}, u32[]{:S(2)}) collective-permute-start(bf16[144,640]{1,0:T(8,128)(2,1)S(1)} %fusion.20), channel_id=1, source_target_pairs={{0,4},{4,8},{8,12},{12,0},{1,5},{5,9},{9,13},{13,1},{2,6},{6,10},{... | collective-permute-start | bytes 552968 | tf_op jit(solution)/shard_map/ppermute | solution.py:26
  111.8 12.0 %collective-permute-start.26 = (bf16[2,160,288]{2,1,0:T(8,128)(2,1)S(1)}, bf16[2,160,288]{2,1,0:T(8,128)(2,1)S(1)}, u32[]{:S(2)}, u32[]{:S(2)}) collective-permute-start(bf16[2,160,288]{2,1,0:T(8,128)(2,1)S(1)} %pad_maximum_fusion.12), channel_id=1, source_target_pairs={{0,2},{1,3},{2,0},{3,1},{4,6},{5,7},{6,4},{7,5},{8,10},{9,11},{10,... | collective-permute-start | bytes 552968 | tf_op jit(solution)/shard_map/ppermute | solution.py:43
  114.2 9.9 %collective-permute-start.27 = (bf16[2,160,288]{2,1,0:T(8,128)(2,1)S(1)}, bf16[2,160,288]{2,1,0:T(8,128)(2,1)S(1)}, u32[]{:S(2)}, u32[]{:S(2)}) collective-permute-start(bf16[2,160,288]{2,1,0:T(8,128)(2,1)S(1)} %pad_maximum_fusion.13), channel_id=1, source_target_pairs={{0,3},{1,2},{2,1},{3,0},{4,7},{5,6},{6,5},{7,4},{8,11},{9,10},{10,... | collective-permute-start | bytes 552968 | tf_op jit(solution)/shard_map/ppermute | solution.py:43
  119.1 15.0 %all-to-all-start.3 = ((bf16[8,18,640]{2,1,0:T(8,128)(2,1)}), bf16[8,18,640]{2,1,0:T(8,128)(2,1)S(1)}, u32[]{:S(2)}, u32[]{:S(2)}) async-start(bf16[8,18,640]{2,1,0:T(8,128)(2,1)} %reshape.153), calls=%async_computation.3 | async-start | bytes 491520 | tf_op jit(solution)/shard_map/all_to_all | solution.py:18
  (28 other events, 158.2 us)
